TPU v7x, 32 devices: a whole 2x2x4 slice. The times are simulated.
32 devices in a mesh: row: 8 (over y, x, core), col: 4 (over z).
Axes of the slice: x: 2, y: 2, z: 4, core: 2. Of those that a mesh axis runs over, the one named last changes fastest.
Arguments:
- homolog_activations: bfloat16 [128, 352, 256], P('row', 'col'), may hold values from -8 to 8
- coupling_activations: bfloat16 [352, 352, 128], P('row', 'col'), may hold values from -6 to 6
- homolog_existence_marks: int32 [128, 352], P('row', 'col'), may hold values from 0 to 1, as said below
- observed_peptide_marks: int32 [352], replicated, may hold values 0 or 1
- peptide_ordinals: int32 [352], replicated, may hold values from 1 to 1056, as said below
- strand_membership: int32 [352], replicated, may hold values from 0 to 7, never falling along the last dimension, each value on 1 to 88 neighbouring positions
- distance_ordinal_vectors: bfloat16 [66, 128], replicated, may hold values from -6 to 6
- coupling_score_mapping: bfloat16 [128, 8], replicated, may hold values from -0.5 to 0.5
- question_mapping_weights: bfloat16 [256, 256], replicated, may hold values from -4 to 4
- address_payload_mapping: bfloat16 [256, 512], replicated, may hold values from -4 to 4
- logistic_valve_mapping: bfloat16 [256, 256], replicated, may hold values from -0.375 to 0.375
- mixture_exit_mapping: bfloat16 [256, 256], replicated, may hold values from -0.375 to 0.375
- twofold_covariance_mapping: bfloat16 [256, 64], replicated, may hold values from -0.375 to 0.375
- covariance_exit_mapping: bfloat16 [1024, 128], replicated, may hold values from -0.1875 to 0.1875
- triad_opening_mappings: bfloat16 [128, 512], replicated, may hold values from -0.5 to 0.5
- triad_valve_mapping: bfloat16 [128, 128], replicated, may hold values from -0.5 to 0.5
- triad_exit_mapping: bfloat16 [128, 128], replicated, may hold values from -0.5 to 0.5
Outputs:
- homologs_after: bfloat16 [128, 352, 256], P('row', 'col')
- couplings_after: bfloat16 [352, 352, 128], P('row', 'col')
Inputs may be any that keep to these rules, and one draw needn't show every extreme that they name: Row 0 and column 0 of homolog_existence_marks are all ones. `peptide_ordinals`: strictly increasing along the residues.
All inputs are finite; a program needn't handle non-finite values.
Results may differ from a plain program's by a relative error of at most 0.008.
Values may be sent and summed in bfloat16 or wider, within the bound.
No kernel may reach another device: no remote copies, remote signals or barrier semaphores. Data moves between devices by JAX's collectives and lax.ppermute only.
A program may use at most 192 MiB of HBM per device.

v0:
```python
import functools
import math

import jax
import jax.numpy as jnp
from jax import lax
from jax.experimental import pallas as pl
from jax.experimental.pallas import tpu as pltpu
from jax.sharding import PartitionSpec as P

REL_MAX = 32


norm_eps = 1e-05
count_eps = 0.001
masked_score = -1000000000.0


def swap(pieces, axis):
    total = len(pieces)
    return [pieces[0]] + [
        lax.ppermute(pieces[k], axis, [(i, i ^ k) for i in range(total)]) for k in range(1, total)
    ]


def collect(block, axis):
    return swap([block] * lax.axis_size(axis), axis)


def exchange(pieces, axis):
    me = lax.axis_index(axis)
    total = lax.axis_size(axis)
    return swap(
        [lax.dynamic_index_in_dim(pieces, me ^ k, 0, keepdims=False) for k in range(total)], axis
    )


def in_order(slots, axis):
    me = lax.axis_index(axis)
    stacked = jnp.stack(slots)
    return jnp.stack(
        [
            lax.dynamic_index_in_dim(stacked, me ^ k, 0, keepdims=False)
            for k in range(len(slots))
        ]
    )


def zscore_transform(inputs):
    inputs = inputs.astype(jnp.float32)
    centred = inputs - jnp.mean(inputs, axis=-1, keepdims=True)
    spread = jnp.mean(centred * centred, axis=-1, keepdims=True)
    return centred * lax.rsqrt(spread + norm_eps)


def regrouped_covariance(operand, weights):
    batch_shape = operand.shape[:-1]
    result = jnp.dot(
        operand.reshape(-1, operand.shape[-1]), weights, preferred_element_type=jnp.float32
    )
    return result.reshape(batch_shape + (weights.shape[-1],))


def position_bins(index_rows, index_cols, chain_rows, chain_cols):
    offset = jnp.clip(index_rows[:, None] - index_cols[None, :] + REL_MAX, 0, 2 * REL_MAX)
    return jnp.where(chain_rows[:, None] == chain_cols[None, :], offset, 2 * REL_MAX + 1)


def operand_kernel(x_ref, marks_ref, spread_ref, wl_ref, wr_ref, left_ref, right_ref, ln, side, acc):
    seqs, places, width = x_ref.shape
    groups = left_ref.shape[0] - 1
    rights = right_ref.shape[0] - 1
    lanes = left_ref.shape[2]
    per = places // groups
    for s in range(seqs):
        own = zscore_transform(x_ref[s])
        for h in range(width // 128):
            ln[h, s * places : (s + 1) * places, :] = own[:, h * 128 : (h + 1) * 128]
    marks = marks_ref[...]
    for s in range(seqs):
        own = jnp.concatenate(
            [ln[h, s * places : (s + 1) * places, :] for h in range(width // 128)], axis=1
        )
        got = lax.dot_general(
            wr_ref[...], own.astype(jnp.bfloat16), (((1,), (1,)), ((), ())),
            preferred_element_type=jnp.float32,
        )
        got = got * marks[s : s + 1, :]
        side[pl.ds(s, rights, stride=seqs), :] = jnp.concatenate(
            [got, jnp.zeros((rights, lanes - places), jnp.float32)], axis=1
        )
    right_ref[:rights] = side[...].reshape(rights, seqs, lanes).astype(jnp.bfloat16)
    for q in range(per):
        for g in range(groups):
            for h in range(width // 128):
                acc[g * seqs : (g + 1) * seqs, h * 128 : (h + 1) * 128] = ln[
                    h, pl.ds(g * per + q, seqs, stride=places), :
                ]
        part = jnp.dot(
            acc[...].astype(jnp.bfloat16), wl_ref[q], preferred_element_type=jnp.float32
        )
        total = part if q == 0 else total + part
    spread = jnp.dot(
        marks.astype(jnp.bfloat16), spread_ref[...], preferred_element_type=jnp.float32
    )
    for g in range(groups):
        left_ref[g] = (
            total[g * seqs : (g + 1) * seqs] * spread[:, g * lanes : (g + 1) * lanes]
        ).astype(jnp.bfloat16)
    block = jnp.zeros((seqs, lanes), jnp.float32)
    side[:seqs, :] = block
    side[:seqs, :places] = marks
    left_ref[groups] = side[:seqs, :].astype(jnp.bfloat16)
    right_ref[rights] = side[:seqs, :].astype(jnp.bfloat16)


def opm_operands(x, marks, mapping):
    seqs, places, width = x.shape
    opm = mapping.shape[1] // 2
    lanes = 128
    per = lanes // opm
    groups = places // per
    wl = jnp.stack(
        [
            jnp.pad(mapping[:, :opm], ((0, 0), (q * opm, lanes - (q + 1) * opm)))
            for q in range(per)
        ]
    )
    wr = mapping[:, opm:].T
    spread = jnp.repeat(jnp.eye(places, dtype=jnp.bfloat16), opm, axis=1)
    return pl.pallas_call(
        operand_kernel,
        out_shape=(
            jax.ShapeDtypeStruct((groups + 1, seqs, lanes), jnp.bfloat16),
            jax.ShapeDtypeStruct((opm + 1, seqs, lanes), jnp.bfloat16),
        ),
        scratch_shapes=[
            pltpu.VMEM((width // 128, seqs * places, 128), jnp.float32),
            pltpu.VMEM((opm * seqs, lanes), jnp.float32),
            pltpu.VMEM((groups * seqs, width), jnp.float32),
        ],
        compiler_params=pltpu.CompilerParams(vmem_limit_bytes=40 << 20),
        name="outer_operands",
    )(x, marks, spread, wl, wr)


def pair_kernel(total_rows, total_cols, *refs):
    spots = refs[0]
    rows_in = refs[1 : 1 + total_rows]
    cols_in = refs[1 + total_rows : 1 + 2 * total_rows]
    (
        pair_ref, place_ref, exit_ref, near_ref, open_ref, score_ref, live_ref,
    ) = refs[1 + 2 * total_rows : 8 + 2 * total_rows]
    outs = refs[8 + 2 * total_rows :]
    z_ref, high_ref, bias_ref = outs[:3]
    side_refs = outs[3 : 3 + total_cols]
    left, right, prod, counts, low = outs[3 + total_cols :]
    step = pl.program_id(0)
    group, places, width = pair_ref.shape
    seqs = rows_in[0].shape[1]
    lanes = 128
    opm = cols_in[0].shape[0] - 1
    blocks = rows_in[0].shape[0] - 1
    bf16 = jnp.bfloat16

    @pl.when(step == 0)
    def _():
        mark_rows, mark_cols = [], []
        for k in range(total_rows):
            for g in range(blocks):
                left[g, k * seqs : (k + 1) * seqs, :] = rows_in[k][g]
            for e in range(opm):
                right[k * seqs : (k + 1) * seqs, e * lanes : (e + 1) * lanes] = cols_in[k][e]
            mark_rows.append(rows_in[k][blocks])
            mark_cols.append(cols_in[k][opm])
        mark_rows = jnp.concatenate(mark_rows, axis=0)
        mark_cols = jnp.concatenate(mark_cols, axis=0)
        counts[...] = lax.dot_general(
            mark_rows, mark_cols, (((0,), (0,)), ((), ())), preferred_element_type=jnp.float32
        )

    grid_left = left[step]
    half = opm // 2
    for part in range(2):
        got = lax.dot_general(
            grid_left, right[:, part * half * lanes : (part + 1) * half * lanes],
            (((0,), (0,)), ((), ())), preferred_element_type=jnp.float32,
        ).astype(bf16)
        for e in range(half):
            for i in range(group):
                prod[
                    (part * half + e) * opm : (part * half + e + 1) * opm,
                    i * lanes : (i + 1) * lanes,
                ] = got[i * opm : (i + 1) * opm, e * lanes : (e + 1) * lanes]
    mixed = jnp.dot(exit_ref[...], prod[...], preferred_element_type=jnp.float32)
    pos_cols = place_ref[0:1, :]
    chain_cols = place_ref[1:2, :]
    bins, amount = [], []
    for i in range(group):
        here = step * group + i
        offset = jnp.clip(spots[0, here] - pos_cols + REL_MAX, 0, 2 * REL_MAX)
        bins.append(jnp.where(chain_cols == spots[1, here], offset, 2 * REL_MAX + 1))
        amount.append(counts[pl.ds(spots[2, 0] + here, 1), :])
    bins = jnp.concatenate(bins, axis=1)
    amount = jnp.concatenate(amount, axis=1)
    one_hot = (
        lax.broadcasted_iota(jnp.int32, (near_ref.shape[1], group * lanes), 0) == bins
    )
    one_hot = jnp.where(one_hot, 1.0, 0.0).astype(bf16)
    near = jnp.dot(near_ref[...], one_hot, preferred_element_type=jnp.float32)
    update = jnp.transpose(mixed / (count_eps + amount) + near)
    z = jnp.concatenate(
        [
            pair_ref[i].astype(jnp.float32) + update[i * lanes : i * lanes + places]
            for i in range(group)
        ],
        axis=0,
    )
    z_ref[...] = z
    ln = zscore_transform(z)
    high = ln.astype(bf16)
    start = pl.multiple_of(step * (group * places), 16)
    high_ref[pl.ds(start, group * places), :] = high
    low[pl.ds(start, group * places), :] = (ln - high.astype(jnp.float32)).astype(bf16)

    @pl.when(step == pl.num_programs(0) - 1)
    def _():
        pairs = high_ref.shape[0]
        chunk = 512
        transposed = (((1,), (1,)), ((), ()))
        half_rows = open_ref.shape[0] // 2
        each = half_rows // total_cols
        for first in range(0, pairs, chunk):
            last = min(first + chunk, pairs)
            ours = high_ref[first:last, :]
            bias = lax.dot_general(
                score_ref[...], ours, transposed, preferred_element_type=jnp.float32
            ) + lax.dot_general(
                score_ref[...], low[first:last, :], transposed, preferred_element_type=jnp.float32
            )
            bias_ref[:, first:last] = bias[: bias_ref.shape[0]].astype(bf16)
            opened = lax.dot_general(
                open_ref[...], ours, transposed, preferred_element_type=jnp.float32
            )
            sides = (
                jax.nn.sigmoid(opened[half_rows:]) * opened[:half_rows] * live_ref[:, first:last]
            ).astype(bf16)
            for m in range(total_cols):
                side_refs[m][:, first:last] = sides[m * each : (m + 1) * each]


def pair_stage(rows_in, cols_in, pair, spots, place, exit_t, near_t, open_t, score_t, live, total_cols):
    total_rows = len(rows_in)
    tile_rows, places, width = pair.shape
    blocks, seqs, lanes = rows_in[0].shape
    blocks -= 1
    group = tile_rows // blocks
    opm = cols_in[0].shape[0] - 1
    pairs = tile_rows * places
    heads = 8
    each = open_t.shape[0] // 2 // total_cols
    every = total_rows * seqs

    def whole(a):
        return pl.BlockSpec(a.shape, lambda g, n=a.ndim: (0,) * n)

    def whole_out(shape):
        return pl.BlockSpec(shape, lambda g, n=len(shape): (0,) * n)

    ins = list(rows_in) + list(cols_in)
    rest = [place, exit_t, near_t, open_t, score_t, live]
    bf16 = jnp.bfloat16
    outs = [
        jax.ShapeDtypeStruct((pairs, width), jnp.float32),
        jax.ShapeDtypeStruct((pairs, width), bf16),
        jax.ShapeDtypeStruct((score_t.shape[0], pairs), bf16),
    ] + [jax.ShapeDtypeStruct((each, pairs), bf16)] * total_cols
    return pl.pallas_call(
        functools.partial(pair_kernel, total_rows, total_cols),
        grid=(blocks,),
        in_specs=[pl.BlockSpec(memory_space=pltpu.SMEM)]
        + [whole(a) for a in ins]
        + [pl.BlockSpec((group, places, width), lambda g: (g, 0, 0))]
        + [whole(a) for a in rest],
        out_specs=[pl.BlockSpec((group * places, width), lambda g: (g, 0))]
        + [whole_out(o.shape) for o in outs[1:]],
        out_shape=outs,
        scratch_shapes=[
            pltpu.VMEM((blocks, every, lanes), bf16),
            pltpu.VMEM((every, opm * lanes), bf16),
            pltpu.VMEM((opm * opm, group * lanes), bf16),
            pltpu.VMEM((lanes, lanes), jnp.float32),
            pltpu.VMEM((pairs, width), bf16),
        ],
        compiler_params=pltpu.CompilerParams(
            vmem_limit_bytes=56 << 20, dimension_semantics=("arbitrary",)
        ),
        cost_estimate=pl.CostEstimate(
            flops=20 * 10**9, bytes_accessed=16 * 10**6, transcendentals=10**6
        ),
        name="pair_update",
    )(spots, *ins, pair, *rest)


def shards(
    homolog_activations,
    coupling_activations,
    homolog_existence_marks,
    observed_peptide_marks,
    peptide_ordinals,
    strand_membership,
    distance_ordinal_vectors,
    coupling_score_mapping,
    question_mapping_weights,
    address_payload_mapping,
    logistic_valve_mapping,
    mixture_exit_mapping,
    twofold_covariance_mapping,
    covariance_exit_mapping,
    triad_opening_mappings,
    triad_valve_mapping,
    triad_exit_mapping,
):
    row_total = lax.axis_size("row")
    col_total = lax.axis_size("col")
    group_ratio = row_total // col_total
    devices = row_total * col_total
    row_place = lax.axis_index("row")
    col_place = lax.axis_index("col")
    tile_rows = coupling_activations.shape[0]
    block_columns = coupling_activations.shape[1]
    number_of_homologs = homolog_activations.shape[0]
    residues = row_total * tile_rows
    heads = coupling_score_mapping.shape[1]
    breadth = question_mapping_weights.shape[1]
    head_breadth = breadth // heads
    opm = twofold_covariance_mapping.shape[1] // 2
    tri_width = triad_exit_mapping.shape[0]
    pair_width = coupling_activations.shape[2]
    own_seqs = number_of_homologs // col_total
    share = tri_width // devices
    row_first = row_place * tile_rows
    col_first = col_place * block_columns
    bf16 = jnp.bfloat16

    marks = homolog_existence_marks.astype(jnp.float32)
    left, right = opm_operands(homolog_activations, marks, twofold_covariance_mapping)
    right_slots = collect(right, "row")
    left_slots = jnp.stack(collect(left, "col"))
    blocks = (left.shape[0] - 1) // group_ratio
    left_pieces = []
    for k in range(row_total):
        target = row_place ^ k
        slot = (target // group_ratio) ^ col_place
        mine = lax.dynamic_index_in_dim(left_slots, slot, 0, keepdims=False)
        part = lax.dynamic_slice_in_dim(mine, target % group_ratio * blocks, blocks, 0)
        left_pieces.append(jnp.concatenate([part, mine[-1:]], axis=0))
    left_slots = swap(left_pieces, "row")

    split = homolog_activations.reshape(col_total, own_seqs, block_columns, -1)
    own_raw = in_order(exchange(split, "col"), "col")
    own_raw = jnp.swapaxes(own_raw, 0, 1).reshape(own_seqs, residues, -1)
    split_marks = homolog_existence_marks.astype(bf16).reshape(col_total, own_seqs, block_columns)
    own_marks = in_order(exchange(split_marks, "col"), "col")
    own_marks = jnp.swapaxes(own_marks, 0, 1).reshape(own_seqs, residues)

    lanes = 128
    spots = jnp.stack(
        [
            lax.dynamic_slice_in_dim(peptide_ordinals, row_first, tile_rows),
            lax.dynamic_slice_in_dim(strand_membership, row_first, tile_rows),
            jnp.full((tile_rows,), row_place % group_ratio * tile_rows, jnp.int32),
        ]
    )
    place = jnp.pad(
        jnp.stack(
            [
                lax.dynamic_slice_in_dim(peptide_ordinals, col_first, block_columns),
                lax.dynamic_slice_in_dim(strand_membership, col_first, block_columns),
            ]
        ),
        ((0, 6), (0, lanes - block_columns)),
    )
    exit_t = covariance_exit_mapping.reshape(opm, opm, pair_width).transpose(2, 1, 0)
    exit_t = exit_t.reshape(pair_width, opm * opm)
    near_t = jnp.pad(
        distance_ordinal_vectors, ((0, lanes - distance_ordinal_vectors.shape[0]), (0, 0))
    ).T
    open_t = triad_opening_mappings.reshape(pair_width, 2, 2, row_total, col_total, share)
    open_t = open_t.transpose(2, 4, 3, 1, 5, 0)
    open_t = jnp.concatenate(
        [
            lax.dynamic_slice_in_dim(open_t, col_place ^ m, 1, 1)
            for m in range(col_total)
        ],
        axis=1,
    ).reshape(4 * tri_width, pair_width)
    score_t = coupling_score_mapping.T
    live_rows = lax.dynamic_slice_in_dim(observed_peptide_marks, row_first, tile_rows)
    live_cols = lax.dynamic_slice_in_dim(observed_peptide_marks, col_first, block_columns)
    live = (live_rows[:, None] * live_cols[None, :]).astype(jnp.float32).reshape(1, -1)
    z_one, ln_tri, bias_flat, *side_pieces = pair_stage(
        left_slots, right_slots, coupling_activations, spots, place, exit_t, near_t, open_t,
        score_t, live, col_total,
    )
    z_one = z_one.reshape(tile_rows, block_columns, pair_width)
    ln_tri = ln_tri.reshape(tile_rows, block_columns, pair_width)

    bias_slots = in_order(collect(bias_flat, "col"), "col")
    bias_slots = in_order(collect(bias_slots, "row"), "row")
    bias_all = bias_slots.reshape(row_total, col_total, heads, tile_rows, block_columns)
    bias_all = bias_all.transpose(2, 0, 3, 1, 4).reshape(heads, residues, residues)

    side_slots = in_order(swap(side_pieces, "col"), "col")
    side_slots = side_slots.reshape(col_total, row_total, 2, share, -1)
    side_slots = in_order(exchange(jnp.swapaxes(side_slots, 0, 1), "row"), "row")
    side_all = side_slots.reshape(row_total, col_total, 2, share, tile_rows, block_columns)
    side_all = side_all.transpose(2, 3, 0, 4, 1, 5).reshape(2, share, residues, residues)

    own = zscore_transform(own_raw).astype(bf16)
    queries = regrouped_covariance(own, question_mapping_weights).astype(bf16)
    queries = queries.reshape(own_seqs, residues, heads, head_breadth)
    key_vals = regrouped_covariance(own, address_payload_mapping).astype(bf16)
    gate = jax.nn.sigmoid(regrouped_covariance(own, logistic_valve_mapping))
    keys = key_vals[:, :, :breadth].reshape(own_seqs, residues, heads, head_breadth)
    values = key_vals[:, :, breadth:].reshape(own_seqs, residues, heads, head_breadth)
    scores = jnp.einsum("sihd,sjhd->shij", queries, keys, preferred_element_type=jnp.float32)
    scores = scores * (1.0 / math.sqrt(head_breadth)) + bias_all[None].astype(jnp.float32)
    scores = jnp.where(own_marks[:, None, None, :] > 0, scores, masked_score)
    exp_terms = jnp.exp(scores - jnp.max(scores, axis=-1, keepdims=True))
    weight_sum = jnp.sum(exp_terms, axis=-1)
    attended = jnp.einsum(
        "shij,sjhd->shid", exp_terms.astype(bf16), values, preferred_element_type=jnp.float32
    )
    attended = attended / weight_sum[..., None]
    attended = attended.transpose(0, 2, 1, 3).reshape(own_seqs, residues, breadth)
    gated = (gate * attended).astype(bf16)
    own_after = (
        own_raw.astype(jnp.float32) + regrouped_covariance(gated, mixture_exit_mapping)
    ).astype(bf16)
    own_after = own_after.reshape(own_seqs, col_total, block_columns, -1)
    homologs_after = in_order(exchange(jnp.swapaxes(own_after, 0, 1), "col"), "col")
    homologs_after = homologs_after.reshape(number_of_homologs, block_columns, -1)

    crossed = jnp.einsum(
        "cik,cjk->cij", side_all[0], side_all[1], preferred_element_type=jnp.float32
    ).astype(bf16)
    crossed = crossed.reshape(share, row_total, tile_rows, col_total, block_columns)
    crossed = crossed.transpose(3, 1, 0, 2, 4).reshape(
        col_total, row_total, share, tile_rows * block_columns
    )
    back = in_order(exchange(crossed, "col"), "col")
    back = in_order(exchange(jnp.swapaxes(back, 0, 1), "row"), "row")
    crossed = back.reshape(tri_width, tile_rows * block_columns).astype(jnp.float32)
    centred = crossed - jnp.mean(crossed, axis=0, keepdims=True)
    spread = jnp.mean(centred * centred, axis=0, keepdims=True)
    normed = (centred * lax.rsqrt(spread + norm_eps)).astype(bf16)
    tri_proj = lax.dot_general(
        normed, triad_exit_mapping, (((0,), (0,)), ((), ())), preferred_element_type=jnp.float32
    ).reshape(tile_rows, block_columns, pair_width)
    tri_gate = jax.nn.sigmoid(regrouped_covariance(ln_tri, triad_valve_mapping))
    couplings_after = (z_one + tri_gate * tri_proj).astype(bf16)
    return (homologs_after, couplings_after)


def solution(mesh):
    placed = (
        P("row", "col", None),
        P("row", "col", None),
        P("row", "col"),
        P(),
        P(),
        P(),
        P(),
        P(),
        P(),
        P(),
        P(),
        P(),
        P(),
        P(),
        P(),
        P(),
        P(),
    )
    return jax.shard_map(
        shards,
        mesh=mesh,
        in_specs=placed,
        out_specs=(P("row", "col", None), P("row", "col", None)),
        check_vma=False,
    )
```

profile of v0, /device:TPU:9, one launch (start us, length us, event | category | flops | bytes accessed | tf_op | source)
XLA Modules:
  0.0 334.7 jit_solution(14124074637121239272)
XLA Ops:
  4.2 2.5 collective-permute-start.7
  14.8 2.3 collective-permute-start.16
  20.2 3.1 collective-permute-start.20
  25.6 2.0 collective-permute-start.15
  28.8 6.7 %collective-permute-done.20.refs_14_ = bf16[33,16,128]{2,1,0:T(8,128)(2,1)S(1)} collective-permute-done((bf16[33,16,128]{2,1,0:T(8,128)(2,1)S(1)}, bf16[33,16,128]{2,1,0:T(8,128)(2,1)S(1)}, u32[]{:S(2)}, u32[]{:S(2)}) %collective-permute-start.20) | collective-permute-done | bytes 135200 | tf_op jit(solution)/shard_map/ppermute | solution.py:22
  40.1 3.0 collective-permute-start
  45.1 17.2 %pair_update.1 = (f32[3872,128]{1,0:T(8,128)}, bf16[3872,128]{1,0:T(8,128)(2,1)}, bf16[8,3872]{1,0:T(8,128)(2,1)}, bf16[64,3872]{1,0:T(8,128)(2,1)}, bf16[64,387...) custom-call(s32[3,44]{1,0:T(4,128)} %add_add_fusion.refs_0_, ...), custom_call_target="tpu_custom_call" | custom-call | flops 20000000000 | bytes 16000000 | tf_op jit(solution)/shard_map/pair_update/pallas_call | solution.py:278
  62.3 2.2 collective-permute-start.23
  79.5 2.0 collective-permute-start.31
  81.5 2.2 collective-permute-done.27
  83.6 3.1 collective-permute-start.32
  86.7 3.2 collective-permute-done.28
  90.0 11.8 %collective-permute-done.30 = bf16[4,8,3872]{2,1,0:T(8,128)(2,1)S(1)} collective-permute-done((bf16[4,8,3872]{2,1,0:T(8,128)(2,1)S(1)}, bf16[4,8,3872]{2,1,0:T(8,128)(2,1)S(1)}, u32[]{:S(2)}, u32[]{:S(2)}) %collective-permute-start.30) | collective-permute-done | bytes 247840 | tf_op jit(solution)/shard_map/ppermute | solution.py:22
  102.2 6.5 %reshape.301 = f32[8,4,8,44,88]{4,3,2,1,0:T(8,128)} reshape(bf16[8,4,8,3872]{3,2,1,0:T(8,128)(2,1)S(1)} %dynamic-slice_dynamic-update-slice_fusion.8) | data formatting | bytes 5947392 | tf_op jit(solution)/shard_map/convert_element_type | solution.py:428
  108.7 10.2 %copy.97 = f32[8,8,44,4,88]{2,1,4,3,0:T(8,128)} copy(f32[8,8,44,4,88]{4,2,0,3,1:T(8,128)} %bitcast.286) | data formatting | bytes 7929856 | tf_op jit(solution)/shard_map/convert_element_type | solution.py:428
  118.9 10.0 %reshape.307 = f32[8,352,352]{1,2,0:T(8,128)} reshape(f32[8,8,44,4,88]{2,1,4,3,0:T(8,128)} %copy.97) | data formatting | bytes 7929856 | tf_op jit(solution)/shard_map/convert_element_type | solution.py:428
  128.9 8.2 %fusion.2 = (f32[4,8,352]{2,1,0:T(8,128)S(1)}, f32[4,8,352,352]{2,3,1,0:T(8,128)S(1)}) fusion(f32[8,352,352]{1,2,0:T(8,128)} %reshape.307, pred[4,352]{1,0:T(4,128)(4,1)S(1)} %gt.20, bf16[4,352,8,32]{1,3,2,0:T(8,128)(2,1)} %bitcast.290, bf16[4,352,8,32]{1,3,2,0:T(8,128)(2,1)} %bitcast.289), kind=kOutput, calls=%fused_computation.4 | convolution fusion | flops 269603840 | bytes 21312896 | tf_op jit(solution)/shard_map/sihd,sjhd->shij/dot_general | solution.py:427
  137.2 5.6 %fusion = f32[4,8,352]{2,1,0:T(8,128)S(1)} fusion(f32[4,8,352,352]{2,3,1,0:T(8,128)S(1)} %get-tuple-element.108, f32[4,8,352]{2,1,0:T(8,128)S(1)} %get-tuple-element.107, f32[8,352,352]{1,2,0:T(8,128)S(1)} %bitcast.285, pred[4,352]{1,0:T(4,128)(4,1)S(1)} %gt.20), kind=kLoop, calls=%fused_computation.2 | loop fusion | flops 19813376 | bytes 19916160 | tf_op jit(solution)/shard_map/reduce_sum | solution.py:431
  142.8 8.5 %bitcast_divide_fusion = f32[4,352,8,32]{1,3,2,0:T(8,128)} fusion(bf16[4,352,8,32]{1,3,2,0:T(8,128)(2,1)} %bitcast.298, f32[4,8,352,352]{2,3,1,0:T(8,128)S(1)} %get-tuple-element.108, f32[4,8,352]{2,1,0:T(8,128)S(1)} %get-tuple-element.107, f32[8,352,352]{1,2,0:T(8,128)} %reshape.307, pred[4,352]{1,0:T(4,128)(4,1)S(1)} %gt.20, f32[4,352,8]{1,2,0:T(8,128)S(1)} %bitcast.331), kind=kOutput, calls=%fused_computation.17 | convolution fusion | flops 273940480 | bytes 22078848 | tf_op jit(solution)/shard_map/shij,sjhd->shid/dot_general | solution.py:432
  151.3 3.1 copy.89
  154.5 2.0 fusion.18
  156.6 2.7 collective-permute-start.33
  159.4 2.1 collective-permute-start.37
  163.6 9.4 %collective-permute-done.33 = bf16[4,88,256]{2,1,0:T(8,128)(2,1)S(1)} collective-permute-done((bf16[4,88,256]{2,1,0:T(8,128)(2,1)S(1)}, bf16[4,88,256]{2,1,0:T(8,128)(2,1)S(1)}, u32[]{:S(2)}, u32[]{:S(2)}) %collective-permute-start.33) | collective-permute-done | bytes 180256 | tf_op jit(solution)/shard_map/ppermute | solution.py:22
  174.0 3.2 fusion.8
  177.2 38.9 %collective-permute-done.34 = bf16[4,88,256]{2,1,0:T(8,128)(2,1)S(1)} collective-permute-done((bf16[4,88,256]{2,1,0:T(8,128)(2,1)S(1)}, bf16[4,88,256]{2,1,0:T(8,128)(2,1)S(1)}, u32[]{:S(2)}, u32[]{:S(2)}) %collective-permute-start.34) | collective-permute-done | bytes 180256 | tf_op jit(solution)/shard_map/ppermute | solution.py:22
  216.2 5.1 %collective-permute-done.35 = bf16[4,88,256]{2,1,0:T(8,128)(2,1)S(1)} collective-permute-done((bf16[4,88,256]{2,1,0:T(8,128)(2,1)S(1)}, bf16[4,88,256]{2,1,0:T(8,128)(2,1)S(1)}, u32[]{:S(2)}, u32[]{:S(2)}) %collective-permute-start.35) | collective-permute-done | bytes 180256 | tf_op jit(solution)/shard_map/ppermute | solution.py:22
  224.3 3.3 reshape.294
  235.1 2.5 collective-permute-done.40
  237.5 2.6 collective-permute-start.45
  240.3 3.6 %collective-permute-done.41 = bf16[4,2,4,3872]{3,2,1,0:T(4,128)(2,1)S(1)} collective-permute-done((bf16[4,2,4,3872]{3,2,1,0:T(4,128)(2,1)S(1)}, bf16[4,2,4,3872]{3,2,1,0:T(4,128)(2,1)S(1)}, u32[]{:S(2)}, u32[]{:S(2)}) %collective-permute-start.41) | collective-permute-done | bytes 247840 | tf_op jit(solution)/shard_map/ppermute | solution.py:22
  244.1 11.6 %collective-permute-done.43 = bf16[4,2,4,3872]{3,2,1,0:T(4,128)(2,1)S(1)} collective-permute-done((bf16[4,2,4,3872]{3,2,1,0:T(4,128)(2,1)S(1)}, bf16[4,2,4,3872]{3,2,1,0:T(4,128)(2,1)S(1)}, u32[]{:S(2)}, u32[]{:S(2)}) %collective-permute-start.43) | collective-permute-done | bytes 247840 | tf_op jit(solution)/shard_map/ppermute | solution.py:22
  257.1 1.9 copy.91
  258.9 7.1 %reshape.295 = bf16[8,4,2,4,44,88]{5,4,0,3,2,1:T(8,128)(2,1)S(1)} reshape(bf16[8,4,2,4,3872]{4,0,3,2,1:T(8,128)(2,1)} %copy.91) | data formatting | bytes 3964928 | tf_op jit(solution)/shard_map/reshape | solution.py:417
  266.1 1.7 fusion.44
  268.9 1.8 squeeze.171
  271.8 1.8 squeeze.172
  273.6 3.1 convolution_convert_fusion.1
  276.7 3.1 reshape.296
  280.2 2.0 reshape.297
  282.3 2.1 collective-permute-start.47
  286.0 6.8 %collective-permute-done.46 = bf16[8,4,3872]{2,0,1:T(8,128)(2,1)S(1)} collective-permute-done((bf16[8,4,3872]{2,0,1:T(8,128)(2,1)S(1)}, bf16[8,4,3872]{2,0,1:T(8,128)(2,1)S(1)}, u32[]{:S(2)}, u32[]{:S(2)}) %collective-permute-start.46) | collective-permute-done | bytes 247840 | tf_op jit(solution)/shard_map/ppermute | solution.py:22
  292.8 3.3 collective-permute-done.47
  296.1 11.1 %collective-permute-done.48 = bf16[8,4,3872]{2,0,1:T(8,128)(2,1)S(1)} collective-permute-done((bf16[8,4,3872]{2,0,1:T(8,128)(2,1)S(1)}, bf16[8,4,3872]{2,0,1:T(8,128)(2,1)S(1)}, u32[]{:S(2)}, u32[]{:S(2)}) %collective-permute-start.48) | collective-permute-done | bytes 247840 | tf_op jit(solution)/shard_map/ppermute | solution.py:22
  307.6 2.1 constant_dynamic-slice_fusion
  316.9 1.9 collective-permute-start.55
  320.0 6.5 %collective-permute-done.53 = bf16[4,4,3872]{2,1,0:T(4,128)(2,1)S(1)} collective-permute-done((bf16[4,4,3872]{2,1,0:T(4,128)(2,1)S(1)}, bf16[4,4,3872]{2,1,0:T(4,128)(2,1)S(1)}, u32[]{:S(2)}, u32[]{:S(2)}) %collective-permute-start.53) | collective-permute-done | bytes 123936 | tf_op jit(solution)/shard_map/ppermute | solution.py:22
  331.6 2.9 add_convert_fusion
  (308 shorter events, 73.1 us)
Async XLA Ops:
  4.1 14.4 %collective-permute-start.6 = (bf16[23,16,128]{2,1,0:T(8,128)(2,1)S(1)}, bf16[23,16,128]{2,1,0:T(8,128)(2,1)S(1)}, u32[]{:S(2)}, u32[]{:S(2)}) collective-permute-start(bf16[23,16,128]{2,1,0:T(8,128)(2,1)S(1)} %get-tuple-element.11), channel_id=1, source_target_pairs={{0,1},{1,0},{2,3},{3,2},{4,5},{5,4},{6,7},{7,6},{8,9},{9,8},{10,11... | collective-permute-start | bytes 282632 | tf_op jit(solution)/shard_map/ppermute | solution.py:22
  4.2 14.8 %collective-permute-start.7 = (bf16[23,16,128]{2,1,0:T(8,128)(2,1)S(1)}, bf16[23,16,128]{2,1,0:T(8,128)(2,1)S(1)}, u32[]{:S(2)}, u32[]{:S(2)}) collective-permute-start(bf16[23,16,128]{2,1,0:T(8,128)(2,1)S(1)} %get-tuple-element.11), channel_id=1, source_target_pairs={{0,2},{1,3},{2,0},{3,1},{4,6},{5,7},{6,4},{7,5},{8,10},{9,11},{10,... | collective-permute-start | bytes 282632 | tf_op jit(solution)/shard_map/ppermute | solution.py:22
  6.6 7.9 %collective-permute-start.3 = (bf16[4,88]{1,0:T(4,128)(2,1)S(1)}, bf16[4,88]{1,0:T(4,128)(2,1)S(1)}, u32[]{:S(2)}, u32[]{:S(2)}) collective-permute-start(bf16[4,88]{1,0:T(4,128)(2,1)S(1)} %get-tuple-element.106), channel_id=1, source_target_pairs={{0,1},{1,0},{2,3},{3,2},{4,5},{5,4},{6,7},{7,6},{8,9},{9,8},{10,11... | collective-permute-start | bytes 2120 | tf_op jit(solution)/shard_map/ppermute | solution.py:22
  7.9 6.8 %collective-permute-start.4 = (bf16[4,88]{1,0:T(4,128)(2,1)S(1)}, bf16[4,88]{1,0:T(4,128)(2,1)S(1)}, u32[]{:S(2)}, u32[]{:S(2)}) collective-permute-start(bf16[4,88]{1,0:T(4,128)(2,1)S(1)} %get-tuple-element.105), channel_id=1, source_target_pairs={{0,2},{1,3},{2,0},{3,1},{4,6},{5,7},{6,4},{7,5},{8,10},{9,11},{10,... | collective-permute-start | bytes 2120 | tf_op jit(solution)/shard_map/ppermute | solution.py:22
  8.0 9.0 %collective-permute-start.5 = (bf16[4,88]{1,0:T(4,128)(2,1)S(1)}, bf16[4,88]{1,0:T(4,128)(2,1)S(1)}, u32[]{:S(2)}, u32[]{:S(2)}) collective-permute-start(bf16[4,88]{1,0:T(4,128)(2,1)S(1)} %get-tuple-element.104), channel_id=1, source_target_pairs={{0,3},{1,2},{2,1},{3,0},{4,7},{5,6},{6,5},{7,4},{8,11},{9,10},{10,... | collective-permute-start | bytes 2120 | tf_op jit(solution)/shard_map/ppermute | solution.py:22
  14.8 8.8 %collective-permute-start.16 = (bf16[33,16,128]{2,1,0:T(8,128)(2,1)S(1)}, bf16[33,16,128]{2,1,0:T(8,128)(2,1)S(1)}, u32[]{:S(2)}, u32[]{:S(2)}) collective-permute-start(bf16[33,16,128]{2,1,0:T(8,128)(2,1)S(1)} %get-tuple-element.12.refs_9_), channel_id=1, source_target_pairs={{0,4},{4,0},{8,12},{12,8},{16,20},{20,16},{24,28},{28,24},{1,5},{5... | collective-permute-start | bytes 405512 | tf_op jit(solution)/shard_map/ppermute | solution.py:22
  17.1 7.7 %collective-permute-start.17 = (bf16[33,16,128]{2,1,0:T(8,128)(2,1)S(1)}, bf16[33,16,128]{2,1,0:T(8,128)(2,1)S(1)}, u32[]{:S(2)}, u32[]{:S(2)}) collective-permute-start(bf16[33,16,128]{2,1,0:T(8,128)(2,1)S(1)} %get-tuple-element.12.refs_9_), channel_id=1, source_target_pairs={{0,8},{4,12},{8,0},{12,4},{16,24},{20,28},{24,16},{28,20},{1,9},{5... | collective-permute-start | bytes 405512 | tf_op jit(solution)/shard_map/ppermute | solution.py:22
  18.4 7.1 %collective-permute-start.18 = (bf16[33,16,128]{2,1,0:T(8,128)(2,1)S(1)}, bf16[33,16,128]{2,1,0:T(8,128)(2,1)S(1)}, u32[]{:S(2)}, u32[]{:S(2)}) collective-permute-start(bf16[33,16,128]{2,1,0:T(8,128)(2,1)S(1)} %get-tuple-element.12.refs_9_), channel_id=1, source_target_pairs={{0,12},{4,8},{8,4},{12,0},{16,28},{20,24},{24,20},{28,16},{1,13},{... | collective-permute-start | bytes 405512 | tf_op jit(solution)/shard_map/ppermute | solution.py:22
  19.0 8.6 %collective-permute-start.19 = (bf16[33,16,128]{2,1,0:T(8,128)(2,1)S(1)}, bf16[33,16,128]{2,1,0:T(8,128)(2,1)S(1)}, u32[]{:S(2)}, u32[]{:S(2)}) collective-permute-start(bf16[33,16,128]{2,1,0:T(8,128)(2,1)S(1)} %get-tuple-element.12.refs_9_), channel_id=1, source_target_pairs={{0,16},{4,20},{8,24},{12,28},{16,0},{20,4},{24,8},{28,12},{1,17},{... | collective-permute-start | bytes 405512 | tf_op jit(solution)/shard_map/ppermute | solution.py:22
  20.2 15.3 %collective-permute-start.20 = (bf16[33,16,128]{2,1,0:T(8,128)(2,1)S(1)}, bf16[33,16,128]{2,1,0:T(8,128)(2,1)S(1)}, u32[]{:S(2)}, u32[]{:S(2)}) collective-permute-start(bf16[33,16,128]{2,1,0:T(8,128)(2,1)S(1)} %get-tuple-element.12.refs_9_), channel_id=1, source_target_pairs={{0,20},{4,16},{8,28},{12,24},{16,4},{20,0},{24,12},{28,8},{1,21},{... | collective-permute-start | bytes 405512 | tf_op jit(solution)/shard_map/ppermute | solution.py:22
  23.6 13.4 %collective-permute-start.21 = (bf16[33,16,128]{2,1,0:T(8,128)(2,1)S(1)}, bf16[33,16,128]{2,1,0:T(8,128)(2,1)S(1)}, u32[]{:S(2)}, u32[]{:S(2)}) collective-permute-start(bf16[33,16,128]{2,1,0:T(8,128)(2,1)S(1)} %get-tuple-element.12.refs_9_), channel_id=1, source_target_pairs={{0,24},{4,28},{8,16},{12,20},{16,8},{20,12},{24,0},{28,4},{1,25},{... | collective-permute-start | bytes 405512 | tf_op jit(solution)/shard_map/ppermute | solution.py:22
  24.8 12.5 %collective-permute-start.22 = (bf16[33,16,128]{2,1,0:T(8,128)(2,1)S(1)}, bf16[33,16,128]{2,1,0:T(8,128)(2,1)S(1)}, u32[]{:S(2)}, u32[]{:S(2)}) collective-permute-start(bf16[33,16,128]{2,1,0:T(8,128)(2,1)S(1)} %get-tuple-element.12.refs_9_), channel_id=1, source_target_pairs={{0,28},{4,24},{8,20},{12,16},{16,12},{20,8},{24,4},{28,0},{1,29},{... | collective-permute-start | bytes 405512 | tf_op jit(solution)/shard_map/ppermute | solution.py:22
  25.6 13.2 %collective-permute-start.15 = (bf16[12,16,128]{2,1,0:T(8,128)(2,1)S(1)}, bf16[12,16,128]{2,1,0:T(8,128)(2,1)S(1)}, u32[]{:S(2)}, u32[]{:S(2)}) collective-permute-start(bf16[12,16,128]{2,1,0:T(8,128)(2,1)S(1)} %pad_maximum_fusion.20), channel_id=1, source_target_pairs={{0,28},{4,24},{8,20},{12,16},{16,12},{20,8},{24,4},{28,0},{1,29},{... | collective-permute-start | bytes 147464 | tf_op jit(solution)/shard_map/ppermute | solution.py:22
  27.6 11.4 %collective-permute-start.14 = (bf16[12,16,128]{2,1,0:T(8,128)(2,1)S(1)}, bf16[12,16,128]{2,1,0:T(8,128)(2,1)S(1)}, u32[]{:S(2)}, u32[]{:S(2)}) collective-permute-start(bf16[12,16,128]{2,1,0:T(8,128)(2,1)S(1)} %pad_maximum_fusion.19), channel_id=1, source_target_pairs={{0,24},{4,28},{8,16},{12,20},{16,8},{20,12},{24,0},{28,4},{1,25},{... | collective-permute-start | bytes 147464 | tf_op jit(solution)/shard_map/ppermute | solution.py:22
  36.9 6.1 %collective-permute-start.12 = (bf16[12,16,128]{2,1,0:T(8,128)(2,1)S(1)}, bf16[12,16,128]{2,1,0:T(8,128)(2,1)S(1)}, u32[]{:S(2)}, u32[]{:S(2)}) collective-permute-start(bf16[12,16,128]{2,1,0:T(8,128)(2,1)S(1)} %pad_maximum_fusion.17), channel_id=1, source_target_pairs={{0,16},{4,20},{8,24},{12,28},{16,0},{20,4},{24,8},{28,12},{1,17},{... | collective-permute-start | bytes 147464 | tf_op jit(solution)/shard_map/ppermute | solution.py:22
  37.3 6.4 %collective-permute-start.11 = (bf16[12,16,128]{2,1,0:T(8,128)(2,1)S(1)}, bf16[12,16,128]{2,1,0:T(8,128)(2,1)S(1)}, u32[]{:S(2)}, u32[]{:S(2)}) collective-permute-start(bf16[12,16,128]{2,1,0:T(8,128)(2,1)S(1)} %pad_maximum_fusion.16), channel_id=1, source_target_pairs={{0,12},{4,8},{8,4},{12,0},{16,28},{20,24},{24,20},{28,16},{1,13},{... | collective-permute-start | bytes 147464 | tf_op jit(solution)/shard_map/ppermute | solution.py:22
  40.1 25.0 %collective-permute-start = (bf16[4,88,256]{2,1,0:T(8,128)(2,1)S(1)}, bf16[4,88,256]{2,1,0:T(8,128)(2,1)S(1)}, u32[]{:S(2)}, u32[]{:S(2)}) collective-permute-start(bf16[4,88,256]{2,1,0:T(8,128)(2,1)S(1)} %get-tuple-element.66), channel_id=1, source_target_pairs={{0,1},{1,0},{2,3},{3,2},{4,5},{5,4},{6,7},{7,6},{8,9},{9,8},{10,11... | collective-permute-start | bytes 540680 | tf_op jit(solution)/shard_map/ppermute | solution.py:22
  43.1 22.8 %collective-permute-start.1 = (bf16[4,88,256]{2,1,0:T(8,128)(2,1)S(1)}, bf16[4,88,256]{2,1,0:T(8,128)(2,1)S(1)}, u32[]{:S(2)}, u32[]{:S(2)}) collective-permute-start(bf16[4,88,256]{2,1,0:T(8,128)(2,1)S(1)} %get-tuple-element.65), channel_id=1, source_target_pairs={{0,2},{1,3},{2,0},{3,1},{4,6},{5,7},{6,4},{7,5},{8,10},{9,11},{10,... | collective-permute-start | bytes 540680 | tf_op jit(solution)/shard_map/ppermute | solution.py:22
  43.7 22.2 %collective-permute-start.2 = (bf16[4,88,256]{2,1,0:T(8,128)(2,1)S(1)}, bf16[4,88,256]{2,1,0:T(8,128)(2,1)S(1)}, u32[]{:S(2)}, u32[]{:S(2)}) collective-permute-start(bf16[4,88,256]{2,1,0:T(8,128)(2,1)S(1)} %get-tuple-element.64), channel_id=1, source_target_pairs={{0,3},{1,2},{2,1},{3,0},{4,7},{5,6},{6,5},{7,4},{8,11},{9,10},{10,... | collective-permute-start | bytes 540680 | tf_op jit(solution)/shard_map/ppermute | solution.py:22
  62.3 11.9 %collective-permute-start.23 = (bf16[8,3872]{1,0:T(8,128)(2,1)}, bf16[8,3872]{1,0:T(8,128)(2,1)S(1)}, u32[]{:S(2)}, u32[]{:S(2)}) collective-permute-start(bf16[8,3872]{1,0:T(8,128)(2,1)} %get-tuple-element.13), channel_id=1, source_target_pairs={{0,1},{1,0},{2,3},{3,2},{4,5},{5,4},{6,7},{7,6},{8,9},{9,8},{10,11... | collective-permute-start | bytes 185864 | tf_op jit(solution)/shard_map/ppermute | solution.py:22
  64.6 9.7 %collective-permute-start.24 = (bf16[8,3872]{1,0:T(8,128)(2,1)}, bf16[8,3872]{1,0:T(8,128)(2,1)S(1)}, u32[]{:S(2)}, u32[]{:S(2)}) collective-permute-start(bf16[8,3872]{1,0:T(8,128)(2,1)} %get-tuple-element.13), channel_id=1, source_target_pairs={{0,2},{1,3},{2,0},{3,1},{4,6},{5,7},{6,4},{7,5},{8,10},{9,11},{10,... | collective-permute-start | bytes 185864 | tf_op jit(solution)/shard_map/ppermute | solution.py:22
  65.1 9.1 %collective-permute-start.25 = (bf16[8,3872]{1,0:T(8,128)(2,1)}, bf16[8,3872]{1,0:T(8,128)(2,1)S(1)}, u32[]{:S(2)}, u32[]{:S(2)}) collective-permute-start(bf16[8,3872]{1,0:T(8,128)(2,1)} %get-tuple-element.13), channel_id=1, source_target_pairs={{0,3},{1,2},{2,1},{3,0},{4,7},{5,6},{6,5},{7,4},{8,11},{9,10},{10,... | collective-permute-start | bytes 185864 | tf_op jit(solution)/shard_map/ppermute | solution.py:22
  75.9 7.7 %collective-permute-start.27 = (bf16[4,8,3872]{2,1,0:T(8,128)(2,1)S(1)}, bf16[4,8,3872]{2,1,0:T(8,128)(2,1)S(1)}, u32[]{:S(2)}, u32[]{:S(2)}) collective-permute-start(bf16[4,8,3872]{2,1,0:T(8,128)(2,1)S(1)} %pad_maximum_fusion.11), channel_id=1, source_target_pairs={{0,8},{4,12},{8,0},{12,4},{16,24},{20,28},{24,16},{28,20},{1,9},{5... | collective-permute-start | bytes 743432 | tf_op jit(solution)/shard_map/ppermute | solution.py:22
  77.1 12.8 %collective-permute-start.28 = (bf16[4,8,3872]{2,1,0:T(8,128)(2,1)S(1)}, bf16[4,8,3872]{2,1,0:T(8,128)(2,1)S(1)}, u32[]{:S(2)}, u32[]{:S(2)}) collective-permute-start(bf16[4,8,3872]{2,1,0:T(8,128)(2,1)S(1)} %pad_maximum_fusion.11), channel_id=1, source_target_pairs={{0,12},{4,8},{8,4},{12,0},{16,28},{20,24},{24,20},{28,16},{1,13},{... | collective-permute-start | bytes 743432 | tf_op jit(solution)/shard_map/ppermute | solution.py:22
  77.6 12.4 %collective-permute-start.29 = (bf16[4,8,3872]{2,1,0:T(8,128)(2,1)S(1)}, bf16[4,8,3872]{2,1,0:T(8,128)(2,1)S(1)}, u32[]{:S(2)}, u32[]{:S(2)}) collective-permute-start(bf16[4,8,3872]{2,1,0:T(8,128)(2,1)S(1)} %pad_maximum_fusion.11), channel_id=1, source_target_pairs={{0,16},{4,20},{8,24},{12,28},{16,0},{20,4},{24,8},{28,12},{1,17},{... | collective-permute-start | bytes 743432 | tf_op jit(solution)/shard_map/ppermute | solution.py:22
  78.6 23.2 %collective-permute-start.30 = (bf16[4,8,3872]{2,1,0:T(8,128)(2,1)S(1)}, bf16[4,8,3872]{2,1,0:T(8,128)(2,1)S(1)}, u32[]{:S(2)}, u32[]{:S(2)}) collective-permute-start(bf16[4,8,3872]{2,1,0:T(8,128)(2,1)S(1)} %pad_maximum_fusion.11), channel_id=1, source_target_pairs={{0,20},{4,16},{8,28},{12,24},{16,4},{20,0},{24,12},{28,8},{1,21},{... | collective-permute-start | bytes 743432 | tf_op jit(solution)/shard_map/ppermute | solution.py:22
  79.5 22.4 %collective-permute-start.31 = (bf16[4,8,3872]{2,1,0:T(8,128)(2,1)S(1)}, bf16[4,8,3872]{2,1,0:T(8,128)(2,1)S(1)}, u32[]{:S(2)}, u32[]{:S(2)}) collective-permute-start(bf16[4,8,3872]{2,1,0:T(8,128)(2,1)S(1)} %pad_maximum_fusion.11), channel_id=1, source_target_pairs={{0,24},{4,28},{8,16},{12,20},{16,8},{20,12},{24,0},{28,4},{1,25},{... | collective-permute-start | bytes 743432 | tf_op jit(solution)/shard_map/ppermute | solution.py:22
  83.6 18.2 %collective-permute-start.32 = (bf16[4,8,3872]{2,1,0:T(8,128)(2,1)S(1)}, bf16[4,8,3872]{2,1,0:T(8,128)(2,1)S(1)}, u32[]{:S(2)}, u32[]{:S(2)}) collective-permute-start(bf16[4,8,3872]{2,1,0:T(8,128)(2,1)S(1)} %pad_maximum_fusion.11), channel_id=1, source_target_pairs={{0,28},{4,24},{8,20},{12,16},{16,12},{20,8},{24,4},{28,0},{1,29},{... | collective-permute-start | bytes 743432 | tf_op jit(solution)/shard_map/ppermute | solution.py:22
  156.6 16.4 %collective-permute-start.33 = (bf16[4,88,256]{2,1,0:T(8,128)(2,1)S(1)}, bf16[4,88,256]{2,1,0:T(8,128)(2,1)S(1)}, u32[]{:S(2)}, u32[]{:S(2)}) collective-permute-start(bf16[4,88,256]{2,1,0:T(8,128)(2,1)S(1)} %get-tuple-element.58), channel_id=1, source_target_pairs={{0,1},{1,0},{2,3},{3,2},{4,5},{5,4},{6,7},{7,6},{8,9},{9,8},{10,11... | collective-permute-start | bytes 540680 | tf_op jit(solution)/shard_map/ppermute | solution.py:22
  159.3 62.9 %collective-permute-start.36 = (bf16[64,3872]{1,0:T(8,128)(2,1)}, bf16[64,3872]{1,0:T(8,128)(2,1)S(1)}, u32[]{:S(2)}, u32[]{:S(2)}) collective-permute-start(bf16[64,3872]{1,0:T(8,128)(2,1)} %get-tuple-element.17), channel_id=1, source_target_pairs={{0,1},{1,0},{2,3},{3,2},{4,5},{5,4},{6,7},{7,6},{8,9},{9,8},{10,11... | collective-permute-start | bytes 1486856 | tf_op jit(solution)/shard_map/ppermute | solution.py:22
  159.4 62.9 %collective-permute-start.37 = (bf16[64,3872]{1,0:T(8,128)(2,1)}, bf16[64,3872]{1,0:T(8,128)(2,1)S(1)}, u32[]{:S(2)}, u32[]{:S(2)}) collective-permute-start(bf16[64,3872]{1,0:T(8,128)(2,1)} %get-tuple-element.18), channel_id=1, source_target_pairs={{0,2},{1,3},{2,0},{3,1},{4,6},{5,7},{6,4},{7,5},{8,10},{9,11},{10,... | collective-permute-start | bytes 1486856 | tf_op jit(solution)/shard_map/ppermute | solution.py:22
  161.4 60.8 %collective-permute-start.38 = (bf16[64,3872]{1,0:T(8,128)(2,1)}, bf16[64,3872]{1,0:T(8,128)(2,1)S(1)}, u32[]{:S(2)}, u32[]{:S(2)}) collective-permute-start(bf16[64,3872]{1,0:T(8,128)(2,1)} %get-tuple-element.19), channel_id=1, source_target_pairs={{0,3},{1,2},{2,1},{3,0},{4,7},{5,6},{6,5},{7,4},{8,11},{9,10},{10,... | collective-permute-start | bytes 1486856 | tf_op jit(solution)/shard_map/ppermute | solution.py:22
  161.9 54.2 %collective-permute-start.34 = (bf16[4,88,256]{2,1,0:T(8,128)(2,1)S(1)}, bf16[4,88,256]{2,1,0:T(8,128)(2,1)S(1)}, u32[]{:S(2)}, u32[]{:S(2)}) collective-permute-start(bf16[4,88,256]{2,1,0:T(8,128)(2,1)S(1)} %get-tuple-element.57), channel_id=1, source_target_pairs={{0,2},{1,3},{2,0},{3,1},{4,6},{5,7},{6,4},{7,5},{8,10},{9,11},{10,... | collective-permute-start | bytes 540680 | tf_op jit(solution)/shard_map/ppermute | solution.py:22
  173.0 48.2 %collective-permute-start.35 = (bf16[4,88,256]{2,1,0:T(8,128)(2,1)S(1)}, bf16[4,88,256]{2,1,0:T(8,128)(2,1)S(1)}, u32[]{:S(2)}, u32[]{:S(2)}) collective-permute-start(bf16[4,88,256]{2,1,0:T(8,128)(2,1)S(1)} %get-tuple-element.56), channel_id=1, source_target_pairs={{0,3},{1,2},{2,1},{3,0},{4,7},{5,6},{6,5},{7,4},{8,11},{9,10},{10,... | collective-permute-start | bytes 540680 | tf_op jit(solution)/shard_map/ppermute | solution.py:22
  229.8 7.7 %collective-permute-start.40 = (bf16[4,2,4,3872]{3,2,1,0:T(4,128)(2,1)S(1)}, bf16[4,2,4,3872]{3,2,1,0:T(4,128)(2,1)S(1)}, u32[]{:S(2)}, u32[]{:S(2)}) collective-permute-start(bf16[4,2,4,3872]{3,2,1,0:T(4,128)(2,1)S(1)} %get-tuple-element.27), channel_id=1, source_target_pairs={{0,8},{4,12},{8,0},{12,4},{16,24},{20,28},{24,16},{28,20},{1,9},{5... | collective-permute-start | bytes 743432 | tf_op jit(solution)/shard_map/ppermute | solution.py:22
  231.0 12.8 %collective-permute-start.41 = (bf16[4,2,4,3872]{3,2,1,0:T(4,128)(2,1)S(1)}, bf16[4,2,4,3872]{3,2,1,0:T(4,128)(2,1)S(1)}, u32[]{:S(2)}, u32[]{:S(2)}) collective-permute-start(bf16[4,2,4,3872]{3,2,1,0:T(4,128)(2,1)S(1)} %get-tuple-element.26), channel_id=1, source_target_pairs={{0,12},{4,8},{8,4},{12,0},{16,28},{20,24},{24,20},{28,16},{1,13},{... | collective-permute-start | bytes 743432 | tf_op jit(solution)/shard_map/ppermute | solution.py:22
  231.5 12.5 %collective-permute-start.42 = (bf16[4,2,4,3872]{3,2,1,0:T(4,128)(2,1)S(1)}, bf16[4,2,4,3872]{3,2,1,0:T(4,128)(2,1)S(1)}, u32[]{:S(2)}, u32[]{:S(2)}) collective-permute-start(bf16[4,2,4,3872]{3,2,1,0:T(4,128)(2,1)S(1)} %get-tuple-element.25), channel_id=1, source_target_pairs={{0,16},{4,20},{8,24},{12,28},{16,0},{20,4},{24,8},{28,12},{1,17},{... | collective-permute-start | bytes 743432 | tf_op jit(solution)/shard_map/ppermute | solution.py:22
  232.1 23.6 %collective-permute-start.43 = (bf16[4,2,4,3872]{3,2,1,0:T(4,128)(2,1)S(1)}, bf16[4,2,4,3872]{3,2,1,0:T(4,128)(2,1)S(1)}, u32[]{:S(2)}, u32[]{:S(2)}) collective-permute-start(bf16[4,2,4,3872]{3,2,1,0:T(4,128)(2,1)S(1)} %get-tuple-element.24), channel_id=1, source_target_pairs={{0,20},{4,16},{8,28},{12,24},{16,4},{20,0},{24,12},{28,8},{1,21},{... | collective-permute-start | bytes 743432 | tf_op jit(solution)/shard_map/ppermute | solution.py:22
  233.4 22.4 %collective-permute-start.44 = (bf16[4,2,4,3872]{3,2,1,0:T(4,128)(2,1)S(1)}, bf16[4,2,4,3872]{3,2,1,0:T(4,128)(2,1)S(1)}, u32[]{:S(2)}, u32[]{:S(2)}) collective-permute-start(bf16[4,2,4,3872]{3,2,1,0:T(4,128)(2,1)S(1)} %get-tuple-element.23), channel_id=1, source_target_pairs={{0,24},{4,28},{8,16},{12,20},{16,8},{20,12},{24,0},{28,4},{1,25},{... | collective-permute-start | bytes 743432 | tf_op jit(solution)/shard_map/ppermute | solution.py:22
  237.5 18.4 %collective-permute-start.45 = (bf16[4,2,4,3872]{3,2,1,0:T(4,128)(2,1)S(1)}, bf16[4,2,4,3872]{3,2,1,0:T(4,128)(2,1)S(1)}, u32[]{:S(2)}, u32[]{:S(2)}) collective-permute-start(bf16[4,2,4,3872]{3,2,1,0:T(4,128)(2,1)S(1)} %get-tuple-element.22), channel_id=1, source_target_pairs={{0,28},{4,24},{8,20},{12,16},{16,12},{20,8},{24,4},{28,0},{1,29},{... | collective-permute-start | bytes 743432 | tf_op jit(solution)/shard_map/ppermute | solution.py:22
  282.2 10.5 %collective-permute-start.46 = (bf16[8,4,3872]{2,0,1:T(8,128)(2,1)S(1)}, bf16[8,4,3872]{2,0,1:T(8,128)(2,1)S(1)}, u32[]{:S(2)}, u32[]{:S(2)}) collective-permute-start(bf16[8,4,3872]{2,0,1:T(8,128)(2,1)S(1)} %get-tuple-element.50), channel_id=1, source_target_pairs={{0,1},{1,0},{2,3},{3,2},{4,5},{5,4},{6,7},{7,6},{8,9},{9,8},{10,11... | collective-permute-start | bytes 743432 | tf_op jit(solution)/shard_map/ppermute | solution.py:22
  282.3 13.8 %collective-permute-start.47 = (bf16[8,4,3872]{2,0,1:T(8,128)(2,1)S(1)}, bf16[8,4,3872]{2,0,1:T(8,128)(2,1)S(1)}, u32[]{:S(2)}, u32[]{:S(2)}) collective-permute-start(bf16[8,4,3872]{2,0,1:T(8,128)(2,1)S(1)} %get-tuple-element.49), channel_id=1, source_target_pairs={{0,2},{1,3},{2,0},{3,1},{4,6},{5,7},{6,4},{7,5},{8,10},{9,11},{10,... | collective-permute-start | bytes 743432 | tf_op jit(solution)/shard_map/ppermute | solution.py:22
  284.5 22.7 %collective-permute-start.48 = (bf16[8,4,3872]{2,0,1:T(8,128)(2,1)S(1)}, bf16[8,4,3872]{2,0,1:T(8,128)(2,1)S(1)}, u32[]{:S(2)}, u32[]{:S(2)}) collective-permute-start(bf16[8,4,3872]{2,0,1:T(8,128)(2,1)S(1)} %get-tuple-element.48), channel_id=1, source_target_pairs={{0,3},{1,2},{2,1},{3,0},{4,7},{5,6},{6,5},{7,4},{8,11},{9,10},{10,... | collective-permute-start | bytes 743432 | tf_op jit(solution)/shard_map/ppermute | solution.py:22
  312.6 7.3 %collective-permute-start.51 = (bf16[4,4,3872]{2,1,0:T(4,128)(2,1)S(1)}, bf16[4,4,3872]{2,1,0:T(4,128)(2,1)S(1)}, u32[]{:S(2)}, u32[]{:S(2)}) collective-permute-start(bf16[4,4,3872]{2,1,0:T(4,128)(2,1)S(1)} %bitcast.321), channel_id=1, source_target_pairs={{0,12},{4,8},{8,4},{12,0},{16,28},{20,24},{24,20},{28,16},{1,13},{... | collective-permute-start | bytes 371720 | tf_op jit(solution)/shard_map/ppermute | solution.py:22
  313.2 6.8 %collective-permute-start.52 = (bf16[4,4,3872]{2,1,0:T(4,128)(2,1)S(1)}, bf16[4,4,3872]{2,1,0:T(4,128)(2,1)S(1)}, u32[]{:S(2)}, u32[]{:S(2)}) collective-permute-start(bf16[4,4,3872]{2,1,0:T(4,128)(2,1)S(1)} %bitcast.320), channel_id=1, source_target_pairs={{0,16},{4,20},{8,24},{12,28},{16,0},{20,4},{24,8},{28,12},{1,17},{... | collective-permute-start | bytes 371720 | tf_op jit(solution)/shard_map/ppermute | solution.py:22
  313.9 12.7 %collective-permute-start.53 = (bf16[4,4,3872]{2,1,0:T(4,128)(2,1)S(1)}, bf16[4,4,3872]{2,1,0:T(4,128)(2,1)S(1)}, u32[]{:S(2)}, u32[]{:S(2)}) collective-permute-start(bf16[4,4,3872]{2,1,0:T(4,128)(2,1)S(1)} %bitcast.319), channel_id=1, source_target_pairs={{0,20},{4,16},{8,28},{12,24},{16,4},{20,0},{24,12},{28,8},{1,21},{... | collective-permute-start | bytes 371720 | tf_op jit(solution)/shard_map/ppermute | solution.py:22
  315.4 11.2 %collective-permute-start.54 = (bf16[4,4,3872]{2,1,0:T(4,128)(2,1)S(1)}, bf16[4,4,3872]{2,1,0:T(4,128)(2,1)S(1)}, u32[]{:S(2)}, u32[]{:S(2)}) collective-permute-start(bf16[4,4,3872]{2,1,0:T(4,128)(2,1)S(1)} %bitcast.318), channel_id=1, source_target_pairs={{0,24},{4,28},{8,16},{12,20},{16,8},{20,12},{24,0},{28,4},{1,25},{... | collective-permute-start | bytes 371720 | tf_op jit(solution)/shard_map/ppermute | solution.py:22
  316.9 9.7 %collective-permute-start.55 = (bf16[4,4,3872]{2,1,0:T(4,128)(2,1)S(1)}, bf16[4,4,3872]{2,1,0:T(4,128)(2,1)S(1)}, u32[]{:S(2)}, u32[]{:S(2)}) collective-permute-start(bf16[4,4,3872]{2,1,0:T(4,128)(2,1)S(1)} %bitcast.317), channel_id=1, source_target_pairs={{0,28},{4,24},{8,20},{12,16},{16,12},{20,8},{24,4},{28,0},{1,29},{... | collective-permute-start | bytes 371720 | tf_op jit(solution)/shard_map/ppermute | solution.py:22
  (48 other events, 415.5 us)
where the time goes:
time: 340 us; the launch traced here: 335 us
  waiting for transfers between devices  124 us (36%)
  local copies, waits for them, and re-layouts  75.5 us (22%)
  starting transfers between devices  69.4 us (20%)
  matrix products  26.6 us (8%)
  other arithmetic  19.3 us (6%)
  Pallas kernels  18.2 us (5%)
    ppermute x56, waiting for transfers between devices, swap(): lax.ppermute(pieces[k], axis, [(i, i ^ k) for i in range(total)])  124 us
    ppermute x56, starting transfers between devices, swap(): lax.ppermute(pieces[k], axis, [(i, i ^ k) for i in range(total)])  69.4 us
    convert_element_type x3, local copies, waits for them, and re-layouts, shards(): bias_all[None].astype(jnp.float32)  26.7 us
    pallas_call x1, Pallas kernels, pair_stage(): pl.pallas_call(functools.partial(pair_kernel, total_rows, total_cols), gr...  17.2 us
    dot_general x1, matrix products, shards(): jnp.einsum('shij,sjhd->shid', exp_terms.astype(bf16), values, preferred_e...  8.46 us
    dot_general x1, matrix products, shards(): jnp.einsum('sihd,sjhd->shij', queries, keys, preferred_element_type=jnp.f...  8.25 us
    reshape x1, local copies, waits for them, and re-layouts, shards(): side_slots.reshape(row_total, col_total, 2, share, tile_rows, block_columns)  7.13 us
  transfers between devices with their start and end apart: 56, of which 15 were waited for; matrix products, arithmetic and copies ran while one was open for 6% of the time, Pallas kernels for 5%

commit v1 on v0

--- a/solution.py
+++ b/solution.py
@@ -230,6 +230,7 @@
         transposed = (((1,), (1,)), ((), ()))
         half_rows = open_ref.shape[0] // 2
         each = half_rows // total_cols
+        count = each // total_rows
         for first in range(0, pairs, chunk):
             last = min(first + chunk, pairs)
             ours = high_ref[first:last, :]
@@ -244,9 +245,11 @@
             )
             sides = (
                 jax.nn.sigmoid(opened[half_rows:]) * opened[:half_rows] * live_ref[:, first:last]
-            ).astype(bf16)
+            )
             for m in range(total_cols):
-                side_refs[m][:, first:last] = sides[m * each : (m + 1) * each]
+                for r in range(total_rows):
+                    at = m * each + r * count
+                    side_refs[m][r, :, first:last] = sides[at : at + count].astype(bf16)
 
 
 def pair_stage(rows_in, cols_in, pair, spots, place, exit_t, near_t, open_t, score_t, live, total_cols):
@@ -274,7 +277,7 @@
         jax.ShapeDtypeStruct((pairs, width), jnp.float32),
         jax.ShapeDtypeStruct((pairs, width), bf16),
         jax.ShapeDtypeStruct((score_t.shape[0], pairs), bf16),
-    ] + [jax.ShapeDtypeStruct((each, pairs), bf16)] * total_cols
+    ] + [jax.ShapeDtypeStruct((total_rows, each // total_rows, pairs), bf16)] * total_cols
     return pl.pallas_call(
         functools.partial(pair_kernel, total_rows, total_cols),
         grid=(blocks,),
@@ -300,6 +303,299 @@
         ),
         name="pair_update",
     )(spots, *ins, pair, *rest)
+
+
+def spread_slots(slots, stack, base_ref, tiles, total_cols, places):
+    total = len(slots)
+    pairs = slots[0].shape[1]
+    count = slots[0].shape[0] // total_cols
+    rows = pairs // places
+    residues = rows * total
+    lane = lax.broadcasted_iota(jnp.int32, (count, 128), 1)
+    for k in range(total):
+        stack[k, :, :pairs] = slots[k][...]
+
+    def one(k, carry):
+        base = base_ref[k]
+        for i in range(rows):
+            first = i * places // 128 * 128
+            off = i * places - first
+            window = stack[k, :, first : first + 256].astype(jnp.float32)
+            made = [None] * tiles.shape[0]
+            for c in range(total_cols):
+                to, at = divmod(c * places, 128)
+                piece = window[c * count : (c + 1) * count]
+                if at != off:
+                    piece = pltpu.roll(piece, (at - off) % 256, 1)
+                begin = piece[:, :128]
+                made[to] = begin if made[to] is None else jnp.where(lane >= at, begin, made[to])
+                if at + places > 128:
+                    made[to + 1] = piece[:, 128:]
+            kept = residues - 128 * (len(made) - 1)
+            made[-1] = jnp.where(lane < kept, made[-1], 0.0)
+            for t, tile in enumerate(made):
+                tiles[t, pl.ds(base + i, count, stride=residues), :] = tile
+        return carry
+
+    lax.fori_loop(0, total, one, 0)
+
+
+def attention_kernel(total_rows, total_cols, *refs):
+    base_ref = refs[0]
+    bias_in = refs[1 : 1 + total_rows]
+    x_in = refs[1 + total_rows : 1 + total_rows + total_cols]
+    mark_ref, project_ref, mix_ref = refs[1 + total_rows + total_cols : 4 + total_rows + total_cols]
+    outs = refs[4 + total_rows + total_cols : 4 + total_rows + 2 * total_cols]
+    stack, tiles, mixed = refs[4 + total_rows + 2 * total_cols :]
+    places, width = x_in[0].shape[1:]
+    residues = places * total_cols
+    heads = bias_in[0].shape[0] // total_cols
+    each = width // heads
+    group = 128 // each
+    padded = tiles.shape[0] * 128
+    bf16 = jnp.bfloat16
+    transposed = (((1,), (1,)), ((), ()))
+    chunk = 176
+
+    @pl.when(pl.program_id(0) == 0)
+    def _():
+        spread_slots(bias_in, stack, base_ref, tiles, total_cols, places)
+
+    x = jnp.concatenate([r[0].astype(jnp.float32) for r in x_in], axis=0)
+    made = jnp.dot(
+        zscore_transform(x).astype(bf16), project_ref[...], preferred_element_type=jnp.float32
+    )
+    present = mark_ref[0] > 0.0
+    lane = lax.broadcasted_iota(jnp.int32, (1, 128), 1)
+    scale = 1.0 / math.sqrt(each)
+    filler = jnp.zeros((padded - residues, 128), bf16)
+    for h0 in range(0, heads, group):
+        at = h0 * each
+        queries = made[:, at : at + 128].astype(bf16)
+        keys = made[:, width + at : width + at + 128].astype(bf16)
+        values = made[:, 2 * width + at : 2 * width + at + 128].astype(bf16)
+        keys = jnp.concatenate([keys, filler], axis=0)
+        values = jnp.concatenate([values, filler], axis=0)
+        for first in range(0, residues, chunk):
+            total = jnp.zeros((chunk, 128), jnp.float32)
+            for h in range(group):
+                ours = (lane >= h * each) & (lane < (h + 1) * each)
+                own_keys = jnp.where(ours, keys, jnp.zeros_like(keys))
+                own_values = jnp.where(ours, values, jnp.zeros_like(values))
+                scores = lax.dot_general(
+                    queries[first : first + chunk], own_keys, transposed,
+                    preferred_element_type=jnp.float32,
+                )
+                start = (h0 + h) * residues + first
+                bias = jnp.concatenate(
+                    [tiles[t, start : start + chunk, :] for t in range(tiles.shape[0])], axis=1
+                )
+                scores = jnp.where(present, scores * scale + bias, masked_score)
+                terms = jnp.exp(scores - jnp.max(scores, axis=1, keepdims=True))
+                weight = jnp.sum(terms, axis=1, keepdims=True)
+                got = jnp.dot(terms.astype(bf16), own_values, preferred_element_type=jnp.float32)
+                total = total + got / weight
+            gate = jax.nn.sigmoid(made[first : first + chunk, 3 * width + at : 3 * width + at + 128])
+            mixed[first : first + chunk, at : at + 128] = (gate * total).astype(bf16)
+    after = x + jnp.dot(mixed[...], mix_ref[...], preferred_element_type=jnp.float32)
+    for m in range(total_cols):
+        outs[m][0] = after[m * places : (m + 1) * places].astype(bf16)
+
+
+def attend(base, bias_slots, x_slots, marks, project, mix):
+    total_rows, total_cols = len(bias_slots), len(x_slots)
+    seqs, places, width = x_slots[0].shape
+    residues = places * total_cols
+    padded = -(-residues // 128) * 128
+    rows, pairs = bias_slots[0].shape
+    heads = rows // total_cols
+    wide = -(-pairs // 128) * 128 + 128
+
+    def whole(a):
+        return pl.BlockSpec(a.shape, lambda s, n=a.ndim: (0,) * n)
+
+    per_seq = pl.BlockSpec((1, places, width), lambda s: (s, 0, 0))
+    bf16 = jnp.bfloat16
+    return pl.pallas_call(
+        functools.partial(attention_kernel, total_rows, total_cols),
+        grid=(seqs,),
+        in_specs=[pl.BlockSpec(memory_space=pltpu.SMEM)]
+        + [whole(a) for a in bias_slots]
+        + [per_seq] * total_cols
+        + [pl.BlockSpec((1, 1, padded), lambda s: (s, 0, 0)), whole(project), whole(mix)],
+        out_specs=[per_seq] * total_cols,
+        out_shape=[jax.ShapeDtypeStruct((seqs, places, width), bf16)] * total_cols,
+        scratch_shapes=[
+            pltpu.VMEM((total_rows, rows, wide), bf16),
+            pltpu.VMEM((padded // 128, heads * residues, 128), jnp.float32),
+            pltpu.VMEM((residues, width), bf16),
+        ],
+        compiler_params=pltpu.CompilerParams(
+            vmem_limit_bytes=56 << 20, dimension_semantics=("arbitrary",)
+        ),
+        cost_estimate=pl.CostEstimate(
+            flops=40 * 10**9, bytes_accessed=30 * 10**6, transcendentals=4 * 10**6
+        ),
+        name="row_attention",
+    )(base, *bias_slots, *x_slots, marks, project, mix)
+
+
+def regroup_kernel(ahead, lead_ref, *refs):
+    total_in = len(refs) - ahead
+    for k in range(ahead):
+        lead = lead_ref[k]
+        parts = [refs[m][lead].astype(jnp.float32) for m in range(total_in)]
+        refs[total_in + k][...] = jnp.concatenate(parts, axis=0).astype(jnp.bfloat16)
+
+
+def regroup(lead, slots):
+    total_out, count, pairs = slots[0].shape
+    return pl.pallas_call(
+        functools.partial(regroup_kernel, total_out),
+        in_specs=[pl.BlockSpec(memory_space=pltpu.SMEM)]
+        + [pl.BlockSpec(memory_space=pltpu.VMEM)] * len(slots),
+        out_specs=[pl.BlockSpec(memory_space=pltpu.VMEM)] * total_out,
+        out_shape=[jax.ShapeDtypeStruct((len(slots) * count, pairs), jnp.bfloat16)] * total_out,
+        compiler_params=pltpu.CompilerParams(vmem_limit_bytes=40 << 20),
+        name="regroup",
+    )(lead, *slots)
+
+
+def triangle_kernel(total_rows, total_cols, *refs):
+    base_ref = refs[0]
+    slots = refs[1 : 1 + total_rows]
+    outs = refs[1 + total_rows : 1 + total_rows + total_cols]
+    stack, tiles, crossed = refs[1 + total_rows + total_cols :]
+    pairs = outs[0].shape[2]
+    share = outs[0].shape[1]
+    residues = tiles.shape[1] // (2 * share)
+    rows = residues // total_rows
+    places = residues // total_cols
+    bf16 = jnp.bfloat16
+    spread_slots(slots, stack, base_ref, tiles, total_cols, places)
+    for c in range(share):
+        sides = []
+        for side in range(2):
+            start = (side * share + c) * residues
+            sides.append(
+                jnp.concatenate(
+                    [tiles[t, start : start + residues, :] for t in range(tiles.shape[0])], axis=1
+                ).astype(bf16)
+            )
+        got = lax.dot_general(
+            sides[0], sides[1], (((1,), (1,)), ((), ())), preferred_element_type=jnp.float32
+        )
+        for t in range(tiles.shape[0]):
+            last = min(128, residues - t * 128)
+            crossed[t, c * residues : (c + 1) * residues, :last] = got[:, t * 128 : t * 128 + last]
+    lane = lax.broadcasted_iota(jnp.int32, (share, 128), 1)
+
+    def one(k, carry):
+        base = base_ref[k]
+        made = [dict() for _ in range(total_cols)]
+        for i in range(rows):
+            row = [
+                crossed[t, pl.ds(base + i, share, stride=residues), :]
+                for t in range(tiles.shape[0])
+            ]
+            for m in range(total_cols):
+                come, off = divmod(m * places, 128)
+                after = row[come + 1] if come + 1 < len(row) else row[come]
+                piece = jnp.concatenate([row[come], after], axis=1)
+                to, at = divmod(i * places, 128)
+                if at != off:
+                    piece = pltpu.roll(piece, (at - off) % 256, 1)
+                begin = piece[:, :128]
+                if to in made[m]:
+                    begin = jnp.where(lane >= at, begin, made[m][to])
+                made[m][to] = begin
+                if at + places > 128:
+                    made[m][to + 1] = piece[:, 128:]
+                if at + places >= 128 or i == rows - 1:
+                    size = min(128, pairs - to * 128)
+                    outs[m][k, :, to * 128 : to * 128 + size] = made[m].pop(to)[:, :size].astype(bf16)
+                    if i == rows - 1 and to + 1 in made[m]:
+                        size = pairs - (to + 1) * 128
+                        outs[m][k, :, (to + 1) * 128 : pairs] = made[m].pop(to + 1)[:, :size].astype(bf16)
+        return carry
+
+    lax.fori_loop(0, total_rows, one, 0)
+
+
+def triangle(base, slots, share, total_cols, residues):
+    total_rows = len(slots)
+    rows, pairs = slots[0].shape
+    padded = -(-residues // 128)
+    wide = -(-pairs // 128) * 128 + 128
+    bf16 = jnp.bfloat16
+    return pl.pallas_call(
+        functools.partial(triangle_kernel, total_rows, total_cols),
+        in_specs=[pl.BlockSpec(memory_space=pltpu.SMEM)]
+        + [pl.BlockSpec(memory_space=pltpu.VMEM)] * total_rows,
+        out_specs=[pl.BlockSpec(memory_space=pltpu.VMEM)] * total_cols,
+        out_shape=[jax.ShapeDtypeStruct((total_rows, share, pairs), bf16)] * total_cols,
+        scratch_shapes=[
+            pltpu.VMEM((total_rows, rows, wide), bf16),
+            pltpu.VMEM((padded, 2 * share * residues, 128), jnp.float32),
+            pltpu.VMEM((padded, share * residues, 128), jnp.float32),
+        ],
+        compiler_params=pltpu.CompilerParams(vmem_limit_bytes=56 << 20),
+        cost_estimate=pl.CostEstimate(
+            flops=10 * 10**9, bytes_accessed=8 * 10**6, transcendentals=0
+        ),
+        name="triangle",
+    )(base, *slots)
+
+
+def finish_kernel(total_rows, *refs):
+    slots = refs[:total_rows]
+    high_ref, z_ref, valve_ref, exit_ref, out_ref = refs[total_rows:]
+    pairs = out_ref.shape[0]
+    chunk = 512
+    for first in range(0, pairs, chunk):
+        last = min(first + chunk, pairs)
+        crossed = jnp.concatenate(
+            [s[:, first:last].astype(jnp.float32) for s in slots], axis=0
+        )
+        centred = crossed - jnp.mean(crossed, axis=0, keepdims=True)
+        spread = jnp.mean(centred * centred, axis=0, keepdims=True)
+        normed = (centred * lax.rsqrt(spread + norm_eps)).astype(jnp.bfloat16)
+        projected = lax.dot_general(
+            normed, exit_ref[...], (((0,), (0,)), ((), ())), preferred_element_type=jnp.float32
+        )
+        gate = jax.nn.sigmoid(
+            jnp.dot(high_ref[first:last, :], valve_ref[...], preferred_element_type=jnp.float32)
+        )
+        out_ref[first:last, :] = (z_ref[first:last, :] + gate * projected).astype(jnp.bfloat16)
+
+
+def finish(slots, high, z_one, valve, exit_w):
+    return pl.pallas_call(
+        functools.partial(finish_kernel, len(slots)),
+        out_shape=jax.ShapeDtypeStruct(high.shape, jnp.bfloat16),
+        compiler_params=pltpu.CompilerParams(vmem_limit_bytes=40 << 20),
+        name="pair_finish",
+    )(*slots, high, z_one, valve, exit_w)
+
+
+def place_kernel(start_ref, *refs):
+    out = refs[-1]
+    for m, slot in enumerate(refs[:-1]):
+        out[pl.ds(start_ref[m], slot.shape[0])] = slot[...]
+
+
+def place_slots(starts, slots):
+    total = len(slots)
+    shape = (total * slots[0].shape[0],) + slots[0].shape[1:]
+    return pl.pallas_call(
+        place_kernel,
+        in_specs=[pl.BlockSpec(memory_space=pltpu.SMEM)]
+        + [pl.BlockSpec(memory_space=pltpu.VMEM)] * total,
+        out_specs=pl.BlockSpec(memory_space=pltpu.VMEM),
+        out_shape=jax.ShapeDtypeStruct(shape, slots[0].dtype),
+        compiler_params=pltpu.CompilerParams(vmem_limit_bytes=40 << 20),
+        name="place_sequences",
+    )(starts, *slots)
 
 
 def shards(
@@ -346,23 +642,24 @@
     marks = homolog_existence_marks.astype(jnp.float32)
     left, right = opm_operands(homolog_activations, marks, twofold_covariance_mapping)
     right_slots = collect(right, "row")
-    left_slots = jnp.stack(collect(left, "col"))
+    left_slots_z = jnp.stack(collect(left, "col"))
     blocks = (left.shape[0] - 1) // group_ratio
     left_pieces = []
     for k in range(row_total):
         target = row_place ^ k
         slot = (target // group_ratio) ^ col_place
-        mine = lax.dynamic_index_in_dim(left_slots, slot, 0, keepdims=False)
+        mine = lax.dynamic_index_in_dim(left_slots_z, slot, 0, keepdims=False)
         part = lax.dynamic_slice_in_dim(mine, target % group_ratio * blocks, blocks, 0)
         left_pieces.append(jnp.concatenate([part, mine[-1:]], axis=0))
     left_slots = swap(left_pieces, "row")
 
-    split = homolog_activations.reshape(col_total, own_seqs, block_columns, -1)
-    own_raw = in_order(exchange(split, "col"), "col")
-    own_raw = jnp.swapaxes(own_raw, 0, 1).reshape(own_seqs, residues, -1)
-    split_marks = homolog_existence_marks.astype(bf16).reshape(col_total, own_seqs, block_columns)
-    own_marks = in_order(exchange(split_marks, "col"), "col")
-    own_marks = jnp.swapaxes(own_marks, 0, 1).reshape(own_seqs, residues)
+    x_slots = exchange(
+        homolog_activations.reshape(col_total, own_seqs, block_columns, -1), "col"
+    )
+    own_marks = lax.dynamic_slice_in_dim(left_slots_z[:, -1], col_place * own_seqs, own_seqs, 1)
+    own_marks = jnp.swapaxes(own_marks[:, :, :block_columns], 0, 1).reshape(own_seqs, 1, residues)
+    padded = -(-residues // 128) * 128
+    own_marks = jnp.pad(own_marks.astype(jnp.float32), ((0, 0), (0, 0), (0, padded - residues)))
 
     lanes = 128
     spots = jnp.stack(
@@ -403,64 +700,29 @@
         left_slots, right_slots, coupling_activations, spots, place, exit_t, near_t, open_t,
         score_t, live, col_total,
     )
-    z_one = z_one.reshape(tile_rows, block_columns, pair_width)
-    ln_tri = ln_tri.reshape(tile_rows, block_columns, pair_width)
-
-    bias_slots = in_order(collect(bias_flat, "col"), "col")
-    bias_slots = in_order(collect(bias_slots, "row"), "row")
-    bias_all = bias_slots.reshape(row_total, col_total, heads, tile_rows, block_columns)
-    bias_all = bias_all.transpose(2, 0, 3, 1, 4).reshape(heads, residues, residues)
-
-    side_slots = in_order(swap(side_pieces, "col"), "col")
-    side_slots = side_slots.reshape(col_total, row_total, 2, share, -1)
-    side_slots = in_order(exchange(jnp.swapaxes(side_slots, 0, 1), "row"), "row")
-    side_all = side_slots.reshape(row_total, col_total, 2, share, tile_rows, block_columns)
-    side_all = side_all.transpose(2, 3, 0, 4, 1, 5).reshape(2, share, residues, residues)
-
-    own = zscore_transform(own_raw).astype(bf16)
-    queries = regrouped_covariance(own, question_mapping_weights).astype(bf16)
-    queries = queries.reshape(own_seqs, residues, heads, head_breadth)
-    key_vals = regrouped_covariance(own, address_payload_mapping).astype(bf16)
-    gate = jax.nn.sigmoid(regrouped_covariance(own, logistic_valve_mapping))
-    keys = key_vals[:, :, :breadth].reshape(own_seqs, residues, heads, head_breadth)
-    values = key_vals[:, :, breadth:].reshape(own_seqs, residues, heads, head_breadth)
-    scores = jnp.einsum("sihd,sjhd->shij", queries, keys, preferred_element_type=jnp.float32)
-    scores = scores * (1.0 / math.sqrt(head_breadth)) + bias_all[None].astype(jnp.float32)
-    scores = jnp.where(own_marks[:, None, None, :] > 0, scores, masked_score)
-    exp_terms = jnp.exp(scores - jnp.max(scores, axis=-1, keepdims=True))
-    weight_sum = jnp.sum(exp_terms, axis=-1)
-    attended = jnp.einsum(
-        "shij,sjhd->shid", exp_terms.astype(bf16), values, preferred_element_type=jnp.float32
-    )
-    attended = attended / weight_sum[..., None]
-    attended = attended.transpose(0, 2, 1, 3).reshape(own_seqs, residues, breadth)
-    gated = (gate * attended).astype(bf16)
-    own_after = (
-        own_raw.astype(jnp.float32) + regrouped_covariance(gated, mixture_exit_mapping)
-    ).astype(bf16)
-    own_after = own_after.reshape(own_seqs, col_total, block_columns, -1)
-    homologs_after = in_order(exchange(jnp.swapaxes(own_after, 0, 1), "col"), "col")
-    homologs_after = homologs_after.reshape(number_of_homologs, block_columns, -1)
-
-    crossed = jnp.einsum(
-        "cik,cjk->cij", side_all[0], side_all[1], preferred_element_type=jnp.float32
-    ).astype(bf16)
-    crossed = crossed.reshape(share, row_total, tile_rows, col_total, block_columns)
-    crossed = crossed.transpose(3, 1, 0, 2, 4).reshape(
-        col_total, row_total, share, tile_rows * block_columns
-    )
-    back = in_order(exchange(crossed, "col"), "col")
-    back = in_order(exchange(jnp.swapaxes(back, 0, 1), "row"), "row")
-    crossed = back.reshape(tri_width, tile_rows * block_columns).astype(jnp.float32)
-    centred = crossed - jnp.mean(crossed, axis=0, keepdims=True)
-    spread = jnp.mean(centred * centred, axis=0, keepdims=True)
-    normed = (centred * lax.rsqrt(spread + norm_eps)).astype(bf16)
-    tri_proj = lax.dot_general(
-        normed, triad_exit_mapping, (((0,), (0,)), ((), ())), preferred_element_type=jnp.float32
-    ).reshape(tile_rows, block_columns, pair_width)
-    tri_gate = jax.nn.sigmoid(regrouped_covariance(ln_tri, triad_valve_mapping))
-    couplings_after = (z_one + tri_gate * tri_proj).astype(bf16)
-    return (homologs_after, couplings_after)
+
+    row_ids = row_place ^ jnp.arange(row_total, dtype=jnp.int32)
+    col_ids = col_place ^ jnp.arange(col_total, dtype=jnp.int32)
+    base = (row_ids // group_ratio ^ col_place) * block_columns + row_ids % group_ratio * tile_rows
+    bias_part = jnp.concatenate(collect(bias_flat, "col"), axis=0)
+    side_slots = swap(side_pieces, "col")
+    bias_slots = collect(bias_part, "row")
+    side_slots = swap(regroup(row_ids, side_slots), "row")
+
+    project = jnp.concatenate(
+        [question_mapping_weights, address_payload_mapping, logistic_valve_mapping], axis=1
+    )
+    own_after = attend(base, bias_slots, x_slots, own_marks, project, mixture_exit_mapping)
+    after_slots = swap(own_after, "col")
+    homologs_after = place_slots(col_ids * own_seqs, after_slots)
+
+    crossed = triangle(base, side_slots, share, col_total, residues)
+    crossed = swap(crossed, "col")
+    crossed = swap(regroup(jnp.arange(row_total, dtype=jnp.int32), crossed), "row")
+    exit_w = triad_exit_mapping.reshape(row_total, col_total, share, pair_width)
+    exit_w = exit_w[row_ids][:, col_ids].reshape(tri_width, pair_width)
+    couplings_after = finish(crossed, ln_tri, z_one, triad_valve_mapping, exit_w)
+    return (homologs_after, couplings_after.reshape(coupling_activations.shape))
 
 
 def solution(mesh):

time: 340 us -> 247 us (0.73); the launches traced: 335 us -> 245 us
  local copies, waits for them, and re-layouts: 75.5 us -> 22.4 us
  Pallas kernels: 18.2 us -> 63.3 us
  matrix products: 26.6 us -> 0 us
  waiting for transfers between devices: 124 us -> 97.9 us
  other arithmetic: 19.3 us -> 3.64 us
  starting transfers between devices: 69.4 us -> 56.9 us
    pallas_call x0 -> x6, Pallas kernels: none -> 45 us  [the longest x1 28.2 us: attend(): pl.pallas_call(functools.partial(attention_kernel, total_rows, total_cols...]
    convert_element_type x5 -> x3, local copies, waits for them, and re-layouts: 28.2 us -> 0.1 us  [shards(): own_marks.astype(jnp.float32)]
    dot_general x8 -> x0, matrix products: 26.6 us -> none  [the longest x1 8.46 us: shards(): jnp.einsum('shij,sjhd->shid', exp_terms.astype(bf16), values, preferred_e...]
    ppermute x56 -> x53, waiting for transfers between devices: 124 us -> 97.9 us  [swap(): lax.ppermute(pieces[k], axis, [(i, i ^ k) for i in range(total)])]
    reshape x6 -> x0, local copies, waits for them, and re-layouts: 18.9 us -> none  [the longest x1 7.13 us: shards(): side_slots.reshape(row_total, col_total, 2, share, tile_rows, block_columns)]
    ppermute x56 -> x53, starting transfers between devices: 69.4 us -> 56.9 us  [swap(): lax.ppermute(pieces[k], axis, [(i, i ^ k) for i in range(total)])]
    reduce_sum x5 -> x0, other arithmetic: 7.71 us -> none  [the longest x1 5.65 us: shards(): weight_sum = jnp.sum(exp_terms, axis=-1)]
    slice x6 -> x1, local copies, waits for them, and re-layouts: 6.42 us -> 0.01 us  [shards(): left_slots_z[:, -1]]
  transfers between devices with their start and end apart: 56 -> 53, of which waited for: 15 -> 17; matrix products, arithmetic and copies ran while one was open for 6% -> 6% of each run, Pallas kernels for 5% -> 24%
where the time goes in v1:
time: 247 us; the launch traced here: 245 us
  waiting for transfers between devices  97.9 us (40%)
  Pallas kernels  63.3 us (26%)
  starting transfers between devices  56.9 us (23%)
  local copies, waits for them, and re-layouts  22.4 us (9%)
  other arithmetic  3.64 us (1%)
    ppermute x53, waiting for transfers between devices, swap(): lax.ppermute(pieces[k], axis, [(i, i ^ k) for i in range(total)])  97.9 us
    ppermute x53, starting transfers between devices, swap(): lax.ppermute(pieces[k], axis, [(i, i ^ k) for i in range(total)])  56.9 us
    pallas_call x1, Pallas kernels, attend(): pl.pallas_call(functools.partial(attention_kernel, total_rows, total_cols...  28.2 us
    pallas_call x1, Pallas kernels, pair_stage(): pl.pallas_call(functools.partial(pair_kernel, total_rows, total_cols), gr...  17.2 us
    unnamed x112, local copies, waits for them, and re-layouts  10.9 us
    pallas_call x1, Pallas kernels, triangle(): pl.pallas_call(functools.partial(triangle_kernel, total_rows, total_cols)...  10 us
    gather x4, local copies, waits for them, and re-layouts, shards(): exit_w = exit_w[row_ids][:, col_ids].reshape(tri_width, pair_width)  5.25 us
  transfers between devices with their start and end apart: 53, of which 17 were waited for; matrix products, arithmetic and copies ran while one was open for 6% of the time, Pallas kernels for 24%

profile of v1, /device:TPU:9, one launch (start us, length us, event | category | flops | bytes accessed | tf_op | source)
XLA Modules:
  0.0 245.4 jit_solution(678305228138865304)
XLA Ops:
  3.3 2.4 collective-permute-start.1
  5.7 1.3 collective-permute-start
  7.0 1.5 collective-permute-start.10
  8.5 1.2 collective-permute-start.11
  16.0 1.2 collective-permute-start.13
  18.1 2.2 collective-permute-start.15
  21.4 1.8 collective-permute-start.9
  23.7 7.9 %collective-permute-done.14.refs_14_ = bf16[33,16,128]{2,1,0:T(8,128)(2,1)S(1)} collective-permute-done((bf16[33,16,128]{2,1,0:T(8,128)(2,1)S(1)}, bf16[33,16,128]{2,1,0:T(8,128)(2,1)S(1)}, u32[]{:S(2)}, u32[]{:S(2)}) %collective-permute-start.14) | collective-permute-done | bytes 135200 | tf_op jit(solution)/shard_map/ppermute | solution.py:22
  31.6 1.2 collective-permute-start.7
  32.8 1.2 collective-permute-start.6
  39.2 17.2 %pair_update.1 = (f32[3872,128]{1,0:T(8,128)}, bf16[3872,128]{1,0:T(8,128)(2,1)}, bf16[8,3872]{1,0:T(8,128)(2,1)}, bf16[8,8,3872]{2,1,0:T(8,128)(2,1)}, bf16[8,8...) custom-call(s32[3,44]{1,0:T(4,128)} %add_add_fusion.refs_0_, ...), custom_call_target="tpu_custom_call" | custom-call | flops 20000000000 | bytes 16000000 | tf_op jit(solution)/shard_map/pair_update/pallas_call | solution.py:281
  57.4 2.4 collective-permute-start.18
  61.0 1.5 collective-permute-start.34
  62.5 1.2 collective-permute-done.18
  63.6 2.2 collective-permute-done.19
  65.8 1.4 collective-permute-start.28
  67.2 16.0 %collective-permute-done.33.refs_1_ = bf16[8,8,3872]{2,1,0:T(8,128)(2,1)S(1)} collective-permute-done((bf16[8,8,3872]{2,1,0:T(8,128)(2,1)}, bf16[8,8,3872]{2,1,0:T(8,128)(2,1)S(1)}, u32[]{:S(2)}, u32[]{:S(2)}) %collective-permute-start.33) | collective-permute-done | bytes 495648 | tf_op jit(solution)/shard_map/ppermute | solution.py:22
  83.2 1.4 collective-permute-start.20
  84.5 17.9 %collective-permute-done.34.refs_2_ = bf16[8,8,3872]{2,1,0:T(8,128)(2,1)S(1)} collective-permute-done((bf16[8,8,3872]{2,1,0:T(8,128)(2,1)}, bf16[8,8,3872]{2,1,0:T(8,128)(2,1)S(1)}, u32[]{:S(2)}, u32[]{:S(2)}) %collective-permute-start.34) | collective-permute-done | bytes 495648 | tf_op jit(solution)/shard_map/ppermute | solution.py:22
  103.0 10.4 %collective-permute-done.35.refs_3_ = bf16[8,8,3872]{2,1,0:T(8,128)(2,1)S(1)} collective-permute-done((bf16[8,8,3872]{2,1,0:T(8,128)(2,1)}, bf16[8,8,3872]{2,1,0:T(8,128)(2,1)S(1)}, u32[]{:S(2)}, u32[]{:S(2)}) %collective-permute-start.35) | collective-permute-done | bytes 495648 | tf_op jit(solution)/shard_map/ppermute | solution.py:22
  115.8 1.8 collective-permute-start.36
  120.8 8.8 %collective-permute-done.29.refs_12_ = bf16[4,88,256]{2,1,0:T(8,128)(2,1)S(1)} collective-permute-done((bf16[4,88,256]{2,1,0:T(8,128)(2,1)S(1)}, bf16[4,88,256]{2,1,0:T(8,128)(2,1)S(1)}, u32[]{:S(2)}, u32[]{:S(2)}) %collective-permute-start.29) | collective-permute-done | bytes 180256 | tf_op jit(solution)/shard_map/ppermute | solution.py:22
  129.5 1.1 collective-permute-start.38
  130.6 1.2 collective-permute-start.39
  132.3 1.6 collective-permute-start.41
  133.9 1.1 collective-permute-start.42
  135.7 2.6 %collective-permute-done.38.refs_4_ = bf16[32,3872]{1,0:T(8,128)(2,1)S(1)} collective-permute-done((bf16[32,3872]{1,0:T(8,128)(2,1)S(1)}, bf16[32,3872]{1,0:T(8,128)(2,1)S(1)}, u32[]{:S(2)}, u32[]{:S(2)}) %collective-permute-start.38) | collective-permute-done | bytes 247840 | tf_op jit(solution)/shard_map/ppermute | solution.py:22
  138.8 9.8 %collective-permute-done.39.refs_5_ = bf16[32,3872]{1,0:T(8,128)(2,1)S(1)} collective-permute-done((bf16[32,3872]{1,0:T(8,128)(2,1)S(1)}, bf16[32,3872]{1,0:T(8,128)(2,1)S(1)}, u32[]{:S(2)}, u32[]{:S(2)}) %collective-permute-start.39) | collective-permute-done | bytes 247840 | tf_op jit(solution)/shard_map/ppermute | solution.py:22
  148.6 2.2 collective-permute-start.23
  150.8 4.5 %collective-permute-done.40.refs_6_ = bf16[32,3872]{1,0:T(8,128)(2,1)} collective-permute-done((bf16[32,3872]{1,0:T(8,128)(2,1)S(1)}, bf16[32,3872]{1,0:T(8,128)(2,1)}, u32[]{:S(2)}, u32[]{:S(2)}) %collective-permute-start.40) | collective-permute-done | bytes 247840 | tf_op jit(solution)/shard_map/ppermute | solution.py:22
  155.3 1.3 collective-permute-start.24
  157.0 2.2 collective-permute-start.26
  159.2 10.0 %triangle.1 = (bf16[8,4,3872]{2,1,0:T(4,128)(2,1)}, bf16[8,4,3872]{2,1,0:T(4,128)(2,1)}, bf16[8,4,3872]{2,1,0:T(4,128)(2,1)}, bf16[8,4,3872]{2,1,0:T(4,128)(2,1)}) custom-call(s32[8]{0:T(128)} %fusion.11.refs_0_, bf16[32,3872]{1,0:T(8,128)(2,1)} %copy-done.14, bf16[32,3872]{1,0:T(8,128)(2,1)} %collective-permute-done.36.refs_2_, ...), custom_call_target="tpu_custom_call" | custom-call | flops 10000000000 | bytes 8000000 | tf_op jit(solution)/shard_map/triangle/pallas_call | solution.py:531
  170.4 1.4 collective-permute-start.44
  171.7 5.1 %collective-permute-done.24.refs_6_ = bf16[32,3872]{1,0:T(8,128)(2,1)S(1)} collective-permute-done((bf16[32,3872]{1,0:T(8,128)(2,1)S(1)}, bf16[32,3872]{1,0:T(8,128)(2,1)S(1)}, u32[]{:S(2)}, u32[]{:S(2)}) %collective-permute-start.24) | collective-permute-done | bytes 247840 | tf_op jit(solution)/shard_map/ppermute | solution.py:22
  178.5 28.2 %row_attention.1 = (bf16[4,88,256]{2,1,0:T(8,128)(2,1)}, bf16[4,88,256]{2,1,0:T(8,128)(2,1)}, bf16[4,88,256]{2,1,0:T(8,128)(2,1)}, bf16[4,88,256]{2,1,0:T(8,128)(2,1)}) custom-call(s32[8]{0:T(128)} %fusion.11.refs_0_, bf16[32,3872]{1,0:T(8,128)(2,1)} %copy-done.22, bf16[32,3872]{1,0:T(8,128)(2,1)} %copy-done.26, bf16[32,3872]{1,0:T(8,128)(2,1)} %copy-done.27, ...), custom_call_target="tpu_custom_call" | custom-call | flops 40000000000 | bytes 30000000 | tf_op jit(solution)/shard_map/row_attention/pallas_call | solution.py:419
  206.9 1.8 collective-permute-start.31
  209.5 1.4 regroup.3
  211.6 1.7 collective-permute-start.46
  214.1 2.0 collective-permute-start.48
  216.1 1.2 collective-permute-done.31.refs_2_
  217.7 7.1 %collective-permute-done.32.refs_3_ = bf16[4,88,256]{2,1,0:T(8,128)(2,1)S(1)} collective-permute-done((bf16[4,88,256]{2,1,0:T(8,128)(2,1)}, bf16[4,88,256]{2,1,0:T(8,128)(2,1)S(1)}, u32[]{:S(2)}, u32[]{:S(2)}) %collective-permute-start.32) | collective-permute-done | bytes 180256 | tf_op jit(solution)/shard_map/ppermute | solution.py:22
  224.8 3.3 %collective-permute-start.50 = (bf16[16,3872]{1,0:T(8,128)(2,1)}, bf16[16,3872]{1,0:T(8,128)(2,1)}, u32[]{:S(2)}, u32[]{:S(2)}) collective-permute-start(bf16[16,3872]{1,0:T(8,128)(2,1)} %get-tuple-element.63), channel_id=1, source_target_pairs={{0,20},{4,16},{8,28},{12,24},{16,4},{20,0},{24,12},{28,8},{1,21},{... | collective-permute-start | bytes 371720 | tf_op jit(solution)/shard_map/ppermute | solution.py:22
  231.1 1.2 gather_fusion
  232.3 1.4 copy.44
  233.7 1.9 gather_fusion.1
  237.3 1.4 place_sequences.1
  242.3 3.2 %pair_finish.1 = bf16[3872,128]{1,0:T(8,128)(2,1)} custom-call(bf16[16,3872]{1,0:T(8,128)(2,1)S(1)} %copy-done.8, bf16[16,3872]{1,0:T(8,128)(2,1)S(1)} %copy-done.10, bf16[16,3872]{1,0:T(8,128)(2,1)S(1)} %copy-done.12, bf16[16,3872]{1,0:T(8,128)(2,1)} %collective-permute-done.48.refs_3_, bf16[16,3872]{1,0:T(8,128)(2,1)} %collective-permute-done.49.refs_4_, ...), custom_call_target="tpu_custom_call" | custom-call | tf_op jit(solution)/shard_map/pair_finish/pallas_call | solution.py:573
  (232 shorter events, 40.4 us)
Async XLA Ops:
  3.3 12.3 %collective-permute-start.1 = (bf16[23,16,128]{2,1,0:T(8,128)(2,1)S(1)}, bf16[23,16,128]{2,1,0:T(8,128)(2,1)S(1)}, u32[]{:S(2)}, u32[]{:S(2)}) collective-permute-start(bf16[23,16,128]{2,1,0:T(8,128)(2,1)S(1)} %get-tuple-element.35), channel_id=1, source_target_pairs={{0,2},{1,3},{2,0},{3,1},{4,6},{5,7},{6,4},{7,5},{8,10},{9,11},{10,... | collective-permute-start | bytes 282632 | tf_op jit(solution)/shard_map/ppermute | solution.py:22
  5.7 10.3 %collective-permute-start.2 = (bf16[23,16,128]{2,1,0:T(8,128)(2,1)S(1)}, bf16[23,16,128]{2,1,0:T(8,128)(2,1)S(1)}, u32[]{:S(2)}, u32[]{:S(2)}) collective-permute-start(bf16[23,16,128]{2,1,0:T(8,128)(2,1)S(1)} %get-tuple-element.35), channel_id=1, source_target_pairs={{0,3},{1,2},{2,1},{3,0},{4,7},{5,6},{6,5},{7,4},{8,11},{9,10},{10,... | collective-permute-start | bytes 282632 | tf_op jit(solution)/shard_map/ppermute | solution.py:22
  5.7 11.6 %collective-permute-start = (bf16[23,16,128]{2,1,0:T(8,128)(2,1)S(1)}, bf16[23,16,128]{2,1,0:T(8,128)(2,1)S(1)}, u32[]{:S(2)}, u32[]{:S(2)}) collective-permute-start(bf16[23,16,128]{2,1,0:T(8,128)(2,1)S(1)} %get-tuple-element.35), channel_id=1, source_target_pairs={{0,1},{1,0},{2,3},{3,2},{4,5},{5,4},{6,7},{7,6},{8,9},{9,8},{10,11... | collective-permute-start | bytes 282632 | tf_op jit(solution)/shard_map/ppermute | solution.py:22
  7.0 11.2 %collective-permute-start.10 = (bf16[33,16,128]{2,1,0:T(8,128)(2,1)S(1)}, bf16[33,16,128]{2,1,0:T(8,128)(2,1)S(1)}, u32[]{:S(2)}, u32[]{:S(2)}) collective-permute-start(bf16[33,16,128]{2,1,0:T(8,128)(2,1)S(1)} %get-tuple-element.36.refs_9_), channel_id=1, source_target_pairs={{0,4},{4,0},{8,12},{12,8},{16,20},{20,16},{24,28},{28,24},{1,5},{5... | collective-permute-start | bytes 405512 | tf_op jit(solution)/shard_map/ppermute | solution.py:22
  8.5 11.9 %collective-permute-start.11 = (bf16[33,16,128]{2,1,0:T(8,128)(2,1)S(1)}, bf16[33,16,128]{2,1,0:T(8,128)(2,1)S(1)}, u32[]{:S(2)}, u32[]{:S(2)}) collective-permute-start(bf16[33,16,128]{2,1,0:T(8,128)(2,1)S(1)} %get-tuple-element.36.refs_9_), channel_id=1, source_target_pairs={{0,8},{4,12},{8,0},{12,4},{16,24},{20,28},{24,16},{28,20},{1,9},{5... | collective-permute-start | bytes 405512 | tf_op jit(solution)/shard_map/ppermute | solution.py:22
  15.6 5.8 %collective-permute-start.12 = (bf16[33,16,128]{2,1,0:T(8,128)(2,1)S(1)}, bf16[33,16,128]{2,1,0:T(8,128)(2,1)S(1)}, u32[]{:S(2)}, u32[]{:S(2)}) collective-permute-start(bf16[33,16,128]{2,1,0:T(8,128)(2,1)S(1)} %get-tuple-element.36.refs_9_), channel_id=1, source_target_pairs={{0,12},{4,8},{8,4},{12,0},{16,28},{20,24},{24,20},{28,16},{1,13},{... | collective-permute-start | bytes 405512 | tf_op jit(solution)/shard_map/ppermute | solution.py:22
  16.0 7.2 %collective-permute-start.13 = (bf16[33,16,128]{2,1,0:T(8,128)(2,1)S(1)}, bf16[33,16,128]{2,1,0:T(8,128)(2,1)S(1)}, u32[]{:S(2)}, u32[]{:S(2)}) collective-permute-start(bf16[33,16,128]{2,1,0:T(8,128)(2,1)S(1)} %get-tuple-element.36.refs_9_), channel_id=1, source_target_pairs={{0,16},{4,20},{8,24},{12,28},{16,0},{20,4},{24,8},{28,12},{1,17},{... | collective-permute-start | bytes 405512 | tf_op jit(solution)/shard_map/ppermute | solution.py:22
  17.3 14.3 %collective-permute-start.14 = (bf16[33,16,128]{2,1,0:T(8,128)(2,1)S(1)}, bf16[33,16,128]{2,1,0:T(8,128)(2,1)S(1)}, u32[]{:S(2)}, u32[]{:S(2)}) collective-permute-start(bf16[33,16,128]{2,1,0:T(8,128)(2,1)S(1)} %get-tuple-element.36.refs_9_), channel_id=1, source_target_pairs={{0,20},{4,16},{8,28},{12,24},{16,4},{20,0},{24,12},{28,8},{1,21},{... | collective-permute-start | bytes 405512 | tf_op jit(solution)/shard_map/ppermute | solution.py:22
  18.1 14.6 %collective-permute-start.15 = (bf16[33,16,128]{2,1,0:T(8,128)(2,1)S(1)}, bf16[33,16,128]{2,1,0:T(8,128)(2,1)S(1)}, u32[]{:S(2)}, u32[]{:S(2)}) collective-permute-start(bf16[33,16,128]{2,1,0:T(8,128)(2,1)S(1)} %get-tuple-element.36.refs_9_), channel_id=1, source_target_pairs={{0,24},{4,28},{8,16},{12,20},{16,8},{20,12},{24,0},{28,4},{1,25},{... | collective-permute-start | bytes 405512 | tf_op jit(solution)/shard_map/ppermute | solution.py:22
  20.4 13.5 %collective-permute-start.16 = (bf16[33,16,128]{2,1,0:T(8,128)(2,1)S(1)}, bf16[33,16,128]{2,1,0:T(8,128)(2,1)S(1)}, u32[]{:S(2)}, u32[]{:S(2)}) collective-permute-start(bf16[33,16,128]{2,1,0:T(8,128)(2,1)S(1)} %get-tuple-element.36.refs_9_), channel_id=1, source_target_pairs={{0,28},{4,24},{8,20},{12,16},{16,12},{20,8},{24,4},{28,0},{1,29},{... | collective-permute-start | bytes 405512 | tf_op jit(solution)/shard_map/ppermute | solution.py:22
  21.4 13.5 %collective-permute-start.9 = (bf16[12,16,128]{2,1,0:T(8,128)(2,1)S(1)}, bf16[12,16,128]{2,1,0:T(8,128)(2,1)S(1)}, u32[]{:S(2)}, u32[]{:S(2)}) collective-permute-start(bf16[12,16,128]{2,1,0:T(8,128)(2,1)S(1)} %pad_maximum_fusion.11), channel_id=1, source_target_pairs={{0,28},{4,24},{8,20},{12,16},{16,12},{20,8},{24,4},{28,0},{1,29},{... | collective-permute-start | bytes 147464 | tf_op jit(solution)/shard_map/ppermute | solution.py:22
  23.2 11.9 %collective-permute-start.8 = (bf16[12,16,128]{2,1,0:T(8,128)(2,1)S(1)}, bf16[12,16,128]{2,1,0:T(8,128)(2,1)S(1)}, u32[]{:S(2)}, u32[]{:S(2)}) collective-permute-start(bf16[12,16,128]{2,1,0:T(8,128)(2,1)S(1)} %pad_maximum_fusion.10), channel_id=1, source_target_pairs={{0,24},{4,28},{8,16},{12,20},{16,8},{20,12},{24,0},{28,4},{1,25},{... | collective-permute-start | bytes 147464 | tf_op jit(solution)/shard_map/ppermute | solution.py:22
  31.6 5.1 %collective-permute-start.7 = (bf16[12,16,128]{2,1,0:T(8,128)(2,1)S(1)}, bf16[12,16,128]{2,1,0:T(8,128)(2,1)S(1)}, u32[]{:S(2)}, u32[]{:S(2)}) collective-permute-start(bf16[12,16,128]{2,1,0:T(8,128)(2,1)S(1)} %pad_maximum_fusion.9), channel_id=1, source_target_pairs={{0,20},{4,16},{8,28},{12,24},{16,4},{20,0},{24,12},{28,8},{1,21},{... | collective-permute-start | bytes 147464 | tf_op jit(solution)/shard_map/ppermute | solution.py:22
  36.7 80.9 %collective-permute-start.27 = (bf16[4,88,256]{2,1,0:T(8,128)(2,1)S(1)}, bf16[4,88,256]{2,1,0:T(8,128)(2,1)S(1)}, u32[]{:S(2)}, u32[]{:S(2)}) collective-permute-start(bf16[4,88,256]{2,1,0:T(8,128)(2,1)S(1)} %get-tuple-element.70), channel_id=1, source_target_pairs={{0,1},{1,0},{2,3},{3,2},{4,5},{5,4},{6,7},{7,6},{8,9},{9,8},{10,11... | collective-permute-start | bytes 540680 | tf_op jit(solution)/shard_map/ppermute | solution.py:22
  57.4 6.2 %collective-permute-start.18 = (bf16[8,3872]{1,0:T(8,128)(2,1)}, bf16[8,3872]{1,0:T(8,128)(2,1)S(1)}, u32[]{:S(2)}, u32[]{:S(2)}) collective-permute-start(bf16[8,3872]{1,0:T(8,128)(2,1)} %get-tuple-element.37), channel_id=1, source_target_pairs={{0,2},{1,3},{2,0},{3,1},{4,6},{5,7},{6,4},{7,5},{8,10},{9,11},{10,... | collective-permute-start | bytes 185864 | tf_op jit(solution)/shard_map/ppermute | solution.py:22
  59.8 6.0 %collective-permute-start.19 = (bf16[8,3872]{1,0:T(8,128)(2,1)}, bf16[8,3872]{1,0:T(8,128)(2,1)S(1)}, u32[]{:S(2)}, u32[]{:S(2)}) collective-permute-start(bf16[8,3872]{1,0:T(8,128)(2,1)} %get-tuple-element.37), channel_id=1, source_target_pairs={{0,3},{1,2},{2,1},{3,0},{4,7},{5,6},{6,5},{7,4},{8,11},{9,10},{10,... | collective-permute-start | bytes 185864 | tf_op jit(solution)/shard_map/ppermute | solution.py:22
  60.0 23.2 %collective-permute-start.33 = (bf16[8,8,3872]{2,1,0:T(8,128)(2,1)}, bf16[8,8,3872]{2,1,0:T(8,128)(2,1)S(1)}, u32[]{:S(2)}, u32[]{:S(2)}) collective-permute-start(bf16[8,8,3872]{2,1,0:T(8,128)(2,1)} %get-tuple-element.43), channel_id=1, source_target_pairs={{0,1},{1,0},{2,3},{3,2},{4,5},{5,4},{6,7},{7,6},{8,9},{9,8},{10,11... | collective-permute-start | bytes 1486856 | tf_op jit(solution)/shard_map/ppermute | solution.py:22
  61.0 41.4 %collective-permute-start.34 = (bf16[8,8,3872]{2,1,0:T(8,128)(2,1)}, bf16[8,8,3872]{2,1,0:T(8,128)(2,1)S(1)}, u32[]{:S(2)}, u32[]{:S(2)}) collective-permute-start(bf16[8,8,3872]{2,1,0:T(8,128)(2,1)} %get-tuple-element.44), channel_id=1, source_target_pairs={{0,2},{1,3},{2,0},{3,1},{4,6},{5,7},{6,4},{7,5},{8,10},{9,11},{10,... | collective-permute-start | bytes 1486856 | tf_op jit(solution)/shard_map/ppermute | solution.py:22
  63.6 49.8 %collective-permute-start.35 = (bf16[8,8,3872]{2,1,0:T(8,128)(2,1)}, bf16[8,8,3872]{2,1,0:T(8,128)(2,1)S(1)}, u32[]{:S(2)}, u32[]{:S(2)}) collective-permute-start(bf16[8,8,3872]{2,1,0:T(8,128)(2,1)} %get-tuple-element.45), channel_id=1, source_target_pairs={{0,3},{1,2},{2,1},{3,0},{4,7},{5,6},{6,5},{7,4},{8,11},{9,10},{10,... | collective-permute-start | bytes 1486856 | tf_op jit(solution)/shard_map/ppermute | solution.py:22
  65.8 53.4 %collective-permute-start.28 = (bf16[4,88,256]{2,1,0:T(8,128)(2,1)S(1)}, bf16[4,88,256]{2,1,0:T(8,128)(2,1)}, u32[]{:S(2)}, u32[]{:S(2)}) collective-permute-start(bf16[4,88,256]{2,1,0:T(8,128)(2,1)S(1)} %get-tuple-element.69), channel_id=1, source_target_pairs={{0,2},{1,3},{2,0},{3,1},{4,6},{5,7},{6,4},{7,5},{8,10},{9,11},{10,... | collective-permute-start | bytes 540680 | tf_op jit(solution)/shard_map/ppermute | solution.py:22
  83.2 47.4 %collective-permute-start.20 = (bf16[32,3872]{1,0:T(8,128)(2,1)S(1)}, bf16[32,3872]{1,0:T(8,128)(2,1)S(1)}, u32[]{:S(2)}, u32[]{:S(2)}) collective-permute-start(bf16[32,3872]{1,0:T(8,128)(2,1)S(1)} %constant_dynamic-update-slice_fusion.refs_1_), channel_id=1, source_target_pairs={{0,4},{4,0},{8,12},{12,8},{16,20},{20,16},{24,28},{28,24},{1,5},{5... | collective-permute-start | bytes 743432 | tf_op jit(solution)/shard_map/ppermute | solution.py:22
  102.4 29.4 %collective-permute-start.21 = (bf16[32,3872]{1,0:T(8,128)(2,1)S(1)}, bf16[32,3872]{1,0:T(8,128)(2,1)S(1)}, u32[]{:S(2)}, u32[]{:S(2)}) collective-permute-start(bf16[32,3872]{1,0:T(8,128)(2,1)S(1)} %constant_dynamic-update-slice_fusion.refs_1_), channel_id=1, source_target_pairs={{0,8},{4,12},{8,0},{12,4},{16,24},{20,28},{24,16},{28,20},{1,9},{5... | collective-permute-start | bytes 743432 | tf_op jit(solution)/shard_map/ppermute | solution.py:22
  115.8 16.4 %collective-permute-start.36 = (bf16[32,3872]{1,0:T(8,128)(2,1)S(1)}, bf16[32,3872]{1,0:T(8,128)(2,1)}, u32[]{:S(2)}, u32[]{:S(2)}) collective-permute-start(bf16[32,3872]{1,0:T(8,128)(2,1)S(1)} %get-tuple-element.47), channel_id=1, source_target_pairs={{0,4},{4,0},{8,12},{12,8},{16,20},{20,16},{24,28},{28,24},{1,5},{5... | collective-permute-start | bytes 743432 | tf_op jit(solution)/shard_map/ppermute | solution.py:22
  117.6 16.3 %collective-permute-start.37 = (bf16[32,3872]{1,0:T(8,128)(2,1)S(1)}, bf16[32,3872]{1,0:T(8,128)(2,1)}, u32[]{:S(2)}, u32[]{:S(2)}) collective-permute-start(bf16[32,3872]{1,0:T(8,128)(2,1)S(1)} %get-tuple-element.48), channel_id=1, source_target_pairs={{0,8},{4,12},{8,0},{12,4},{16,24},{20,28},{24,16},{28,20},{1,9},{5... | collective-permute-start | bytes 743432 | tf_op jit(solution)/shard_map/ppermute | solution.py:22
  119.2 10.3 %collective-permute-start.29 = (bf16[4,88,256]{2,1,0:T(8,128)(2,1)S(1)}, bf16[4,88,256]{2,1,0:T(8,128)(2,1)S(1)}, u32[]{:S(2)}, u32[]{:S(2)}) collective-permute-start(bf16[4,88,256]{2,1,0:T(8,128)(2,1)S(1)} %get-tuple-element.68), channel_id=1, source_target_pairs={{0,3},{1,2},{2,1},{3,0},{4,7},{5,6},{6,5},{7,4},{8,11},{9,10},{10,... | collective-permute-start | bytes 540680 | tf_op jit(solution)/shard_map/ppermute | solution.py:22
  129.5 8.7 %collective-permute-start.38 = (bf16[32,3872]{1,0:T(8,128)(2,1)S(1)}, bf16[32,3872]{1,0:T(8,128)(2,1)S(1)}, u32[]{:S(2)}, u32[]{:S(2)}) collective-permute-start(bf16[32,3872]{1,0:T(8,128)(2,1)S(1)} %get-tuple-element.49), channel_id=1, source_target_pairs={{0,12},{4,8},{8,4},{12,0},{16,28},{20,24},{24,20},{28,16},{1,13},{... | collective-permute-start | bytes 743432 | tf_op jit(solution)/shard_map/ppermute | solution.py:22
  130.6 18.0 %collective-permute-start.39 = (bf16[32,3872]{1,0:T(8,128)(2,1)S(1)}, bf16[32,3872]{1,0:T(8,128)(2,1)S(1)}, u32[]{:S(2)}, u32[]{:S(2)}) collective-permute-start(bf16[32,3872]{1,0:T(8,128)(2,1)S(1)} %get-tuple-element.50), channel_id=1, source_target_pairs={{0,16},{4,20},{8,24},{12,28},{16,0},{20,4},{24,8},{28,12},{1,17},{... | collective-permute-start | bytes 743432 | tf_op jit(solution)/shard_map/ppermute | solution.py:22
  131.8 23.5 %collective-permute-start.40 = (bf16[32,3872]{1,0:T(8,128)(2,1)S(1)}, bf16[32,3872]{1,0:T(8,128)(2,1)}, u32[]{:S(2)}, u32[]{:S(2)}) collective-permute-start(bf16[32,3872]{1,0:T(8,128)(2,1)S(1)} %get-tuple-element.51), channel_id=1, source_target_pairs={{0,20},{4,16},{8,28},{12,24},{16,4},{20,0},{24,12},{28,8},{1,21},{... | collective-permute-start | bytes 743432 | tf_op jit(solution)/shard_map/ppermute | solution.py:22
  132.3 24.4 %collective-permute-start.41 = (bf16[32,3872]{1,0:T(8,128)(2,1)S(1)}, bf16[32,3872]{1,0:T(8,128)(2,1)S(1)}, u32[]{:S(2)}, u32[]{:S(2)}) collective-permute-start(bf16[32,3872]{1,0:T(8,128)(2,1)S(1)} %get-tuple-element.52), channel_id=1, source_target_pairs={{0,24},{4,28},{8,16},{12,20},{16,8},{20,12},{24,0},{28,4},{1,25},{... | collective-permute-start | bytes 743432 | tf_op jit(solution)/shard_map/ppermute | solution.py:22
  133.9 23.1 %collective-permute-start.42 = (bf16[32,3872]{1,0:T(8,128)(2,1)S(1)}, bf16[32,3872]{1,0:T(8,128)(2,1)}, u32[]{:S(2)}, u32[]{:S(2)}) collective-permute-start(bf16[32,3872]{1,0:T(8,128)(2,1)S(1)} %get-tuple-element.53), channel_id=1, source_target_pairs={{0,28},{4,24},{8,20},{12,16},{16,12},{20,8},{24,4},{28,0},{1,29},{... | collective-permute-start | bytes 743432 | tf_op jit(solution)/shard_map/ppermute | solution.py:22
  138.3 31.0 %collective-permute-start.22 = (bf16[32,3872]{1,0:T(8,128)(2,1)S(1)}, bf16[32,3872]{1,0:T(8,128)(2,1)S(1)}, u32[]{:S(2)}, u32[]{:S(2)}) collective-permute-start(bf16[32,3872]{1,0:T(8,128)(2,1)S(1)} %constant_dynamic-update-slice_fusion.refs_1_), channel_id=1, source_target_pairs={{0,12},{4,8},{8,4},{12,0},{16,28},{20,24},{24,20},{28,16},{1,13},{... | collective-permute-start | bytes 743432 | tf_op jit(solution)/shard_map/ppermute | solution.py:22
  148.6 21.8 %collective-permute-start.23 = (bf16[32,3872]{1,0:T(8,128)(2,1)S(1)}, bf16[32,3872]{1,0:T(8,128)(2,1)S(1)}, u32[]{:S(2)}, u32[]{:S(2)}) collective-permute-start(bf16[32,3872]{1,0:T(8,128)(2,1)S(1)} %constant_dynamic-update-slice_fusion.refs_1_), channel_id=1, source_target_pairs={{0,16},{4,20},{8,24},{12,28},{16,0},{20,4},{24,8},{28,12},{1,17},{... | collective-permute-start | bytes 743432 | tf_op jit(solution)/shard_map/ppermute | solution.py:22
  155.3 21.5 %collective-permute-start.24 = (bf16[32,3872]{1,0:T(8,128)(2,1)S(1)}, bf16[32,3872]{1,0:T(8,128)(2,1)S(1)}, u32[]{:S(2)}, u32[]{:S(2)}) collective-permute-start(bf16[32,3872]{1,0:T(8,128)(2,1)S(1)} %constant_dynamic-update-slice_fusion.refs_1_), channel_id=1, source_target_pairs={{0,20},{4,16},{8,28},{12,24},{16,4},{20,0},{24,12},{28,8},{1,21},{... | collective-permute-start | bytes 743432 | tf_op jit(solution)/shard_map/ppermute | solution.py:22
  156.7 21.0 %collective-permute-start.25 = (bf16[32,3872]{1,0:T(8,128)(2,1)S(1)}, bf16[32,3872]{1,0:T(8,128)(2,1)S(1)}, u32[]{:S(2)}, u32[]{:S(2)}) collective-permute-start(bf16[32,3872]{1,0:T(8,128)(2,1)S(1)} %constant_dynamic-update-slice_fusion.refs_1_), channel_id=1, source_target_pairs={{0,24},{4,28},{8,16},{12,20},{16,8},{20,12},{24,0},{28,4},{1,25},{... | collective-permute-start | bytes 743432 | tf_op jit(solution)/shard_map/ppermute | solution.py:22
  157.0 20.7 %collective-permute-start.26 = (bf16[32,3872]{1,0:T(8,128)(2,1)S(1)}, bf16[32,3872]{1,0:T(8,128)(2,1)S(1)}, u32[]{:S(2)}, u32[]{:S(2)}) collective-permute-start(bf16[32,3872]{1,0:T(8,128)(2,1)S(1)} %constant_dynamic-update-slice_fusion.refs_1_), channel_id=1, source_target_pairs={{0,28},{4,24},{8,20},{12,16},{16,12},{20,8},{24,4},{28,0},{1,29},{... | collective-permute-start | bytes 743432 | tf_op jit(solution)/shard_map/ppermute | solution.py:22
  169.3 39.4 %collective-permute-start.43 = (bf16[8,4,3872]{2,1,0:T(4,128)(2,1)}, bf16[8,4,3872]{2,1,0:T(4,128)(2,1)S(1)}, u32[]{:S(2)}, u32[]{:S(2)}) collective-permute-start(bf16[8,4,3872]{2,1,0:T(4,128)(2,1)} %get-tuple-element.55), channel_id=1, source_target_pairs={{0,1},{1,0},{2,3},{3,2},{4,5},{5,4},{6,7},{7,6},{8,9},{9,8},{10,11... | collective-permute-start | bytes 743432 | tf_op jit(solution)/shard_map/ppermute | solution.py:22
  170.4 39.1 %collective-permute-start.44 = (bf16[8,4,3872]{2,1,0:T(4,128)(2,1)}, bf16[8,4,3872]{2,1,0:T(4,128)(2,1)S(1)}, u32[]{:S(2)}, u32[]{:S(2)}) collective-permute-start(bf16[8,4,3872]{2,1,0:T(4,128)(2,1)} %get-tuple-element.56), channel_id=1, source_target_pairs={{0,2},{1,3},{2,0},{3,1},{4,6},{5,7},{6,4},{7,5},{8,10},{9,11},{10,... | collective-permute-start | bytes 743432 | tf_op jit(solution)/shard_map/ppermute | solution.py:22
  176.8 32.7 %collective-permute-start.45 = (bf16[8,4,3872]{2,1,0:T(4,128)(2,1)}, bf16[8,4,3872]{2,1,0:T(4,128)(2,1)S(1)}, u32[]{:S(2)}, u32[]{:S(2)}) collective-permute-start(bf16[8,4,3872]{2,1,0:T(4,128)(2,1)} %get-tuple-element.57), channel_id=1, source_target_pairs={{0,3},{1,2},{2,1},{3,0},{4,7},{5,6},{6,5},{7,4},{8,11},{9,10},{10,... | collective-permute-start | bytes 743432 | tf_op jit(solution)/shard_map/ppermute | solution.py:22
  206.8 7.3 %collective-permute-start.30 = (bf16[4,88,256]{2,1,0:T(8,128)(2,1)}, bf16[4,88,256]{2,1,0:T(8,128)(2,1)S(1)}, u32[]{:S(2)}, u32[]{:S(2)}) collective-permute-start(bf16[4,88,256]{2,1,0:T(8,128)(2,1)} %get-tuple-element.39), channel_id=1, source_target_pairs={{0,1},{1,0},{2,3},{3,2},{4,5},{5,4},{6,7},{7,6},{8,9},{9,8},{10,11... | collective-permute-start | bytes 540680 | tf_op jit(solution)/shard_map/ppermute | solution.py:22
  206.9 10.4 %collective-permute-start.31 = (bf16[4,88,256]{2,1,0:T(8,128)(2,1)}, bf16[4,88,256]{2,1,0:T(8,128)(2,1)S(1)}, u32[]{:S(2)}, u32[]{:S(2)}) collective-permute-start(bf16[4,88,256]{2,1,0:T(8,128)(2,1)} %get-tuple-element.40), channel_id=1, source_target_pairs={{0,2},{1,3},{2,0},{3,1},{4,6},{5,7},{6,4},{7,5},{8,10},{9,11},{10,... | collective-permute-start | bytes 540680 | tf_op jit(solution)/shard_map/ppermute | solution.py:22
  208.7 16.2 %collective-permute-start.32 = (bf16[4,88,256]{2,1,0:T(8,128)(2,1)}, bf16[4,88,256]{2,1,0:T(8,128)(2,1)S(1)}, u32[]{:S(2)}, u32[]{:S(2)}) collective-permute-start(bf16[4,88,256]{2,1,0:T(8,128)(2,1)} %get-tuple-element.41), channel_id=1, source_target_pairs={{0,3},{1,2},{2,1},{3,0},{4,7},{5,6},{6,5},{7,4},{8,11},{9,10},{10,... | collective-permute-start | bytes 540680 | tf_op jit(solution)/shard_map/ppermute | solution.py:22
  211.6 16.6 %collective-permute-start.46 = (bf16[16,3872]{1,0:T(8,128)(2,1)S(1)}, bf16[16,3872]{1,0:T(8,128)(2,1)S(1)}, u32[]{:S(2)}, u32[]{:S(2)}) collective-permute-start(bf16[16,3872]{1,0:T(8,128)(2,1)S(1)} %get-tuple-element.59), channel_id=1, source_target_pairs={{0,4},{4,0},{8,12},{12,8},{16,20},{20,16},{24,28},{28,24},{1,5},{5... | collective-permute-start | bytes 371720 | tf_op jit(solution)/shard_map/ppermute | solution.py:22
  213.3 16.1 %collective-permute-start.47 = (bf16[16,3872]{1,0:T(8,128)(2,1)S(1)}, bf16[16,3872]{1,0:T(8,128)(2,1)S(1)}, u32[]{:S(2)}, u32[]{:S(2)}) collective-permute-start(bf16[16,3872]{1,0:T(8,128)(2,1)S(1)} %get-tuple-element.60), channel_id=1, source_target_pairs={{0,8},{4,12},{8,0},{12,4},{16,24},{20,28},{24,16},{28,20},{1,9},{5... | collective-permute-start | bytes 371720 | tf_op jit(solution)/shard_map/ppermute | solution.py:22
  214.1 24.6 %collective-permute-start.48 = (bf16[16,3872]{1,0:T(8,128)(2,1)}, bf16[16,3872]{1,0:T(8,128)(2,1)}, u32[]{:S(2)}, u32[]{:S(2)}) collective-permute-start(bf16[16,3872]{1,0:T(8,128)(2,1)} %get-tuple-element.61), channel_id=1, source_target_pairs={{0,12},{4,8},{8,4},{12,0},{16,28},{20,24},{24,20},{28,16},{1,13},{... | collective-permute-start | bytes 371720 | tf_op jit(solution)/shard_map/ppermute | solution.py:22
  217.2 21.5 %collective-permute-start.49 = (bf16[16,3872]{1,0:T(8,128)(2,1)}, bf16[16,3872]{1,0:T(8,128)(2,1)}, u32[]{:S(2)}, u32[]{:S(2)}) collective-permute-start(bf16[16,3872]{1,0:T(8,128)(2,1)} %get-tuple-element.62), channel_id=1, source_target_pairs={{0,16},{4,20},{8,24},{12,28},{16,0},{20,4},{24,8},{28,12},{1,17},{... | collective-permute-start | bytes 371720 | tf_op jit(solution)/shard_map/ppermute | solution.py:22
  224.8 13.9 %collective-permute-start.50 = (bf16[16,3872]{1,0:T(8,128)(2,1)}, bf16[16,3872]{1,0:T(8,128)(2,1)}, u32[]{:S(2)}, u32[]{:S(2)}) collective-permute-start(bf16[16,3872]{1,0:T(8,128)(2,1)} %get-tuple-element.63), channel_id=1, source_target_pairs={{0,20},{4,16},{8,28},{12,24},{16,4},{20,0},{24,12},{28,8},{1,21},{... | collective-permute-start | bytes 371720 | tf_op jit(solution)/shard_map/ppermute | solution.py:22
  228.8 9.9 %collective-permute-start.51 = (bf16[16,3872]{1,0:T(8,128)(2,1)}, bf16[16,3872]{1,0:T(8,128)(2,1)}, u32[]{:S(2)}, u32[]{:S(2)}) collective-permute-start(bf16[16,3872]{1,0:T(8,128)(2,1)} %get-tuple-element.64), channel_id=1, source_target_pairs={{0,24},{4,28},{8,16},{12,20},{16,8},{20,12},{24,0},{28,4},{1,25},{... | collective-permute-start | bytes 371720 | tf_op jit(solution)/shard_map/ppermute | solution.py:22
  230.1 8.7 %collective-permute-start.52 = (bf16[16,3872]{1,0:T(8,128)(2,1)}, bf16[16,3872]{1,0:T(8,128)(2,1)}, u32[]{:S(2)}, u32[]{:S(2)}) collective-permute-start(bf16[16,3872]{1,0:T(8,128)(2,1)} %get-tuple-element.65), channel_id=1, source_target_pairs={{0,28},{4,24},{8,20},{12,16},{16,12},{20,8},{24,4},{28,0},{1,29},{... | collective-permute-start | bytes 371720 | tf_op jit(solution)/shard_map/ppermute | solution.py:22
  (58 other events, 1081.4 us)

commit v2 on v1

--- a/solution.py
+++ b/solution.py
@@ -146,33 +146,39 @@
 
 def pair_kernel(total_rows, total_cols, *refs):
     spots = refs[0]
-    rows_in = refs[1 : 1 + total_rows]
-    cols_in = refs[1 + total_rows : 1 + 2 * total_rows]
-    (
-        pair_ref, place_ref, exit_ref, near_ref, open_ref, score_ref, live_ref,
-    ) = refs[1 + 2 * total_rows : 8 + 2 * total_rows]
-    outs = refs[8 + 2 * total_rows :]
+    rows_in = refs[1:3]
+    cols_in = refs[3:5]
+    pair_ref, place_ref, exit_ref, near_ref, open_ref, score_ref, live_ref = refs[5:12]
+    outs = refs[12:]
     z_ref, high_ref, bias_ref = outs[:3]
     side_refs = outs[3 : 3 + total_cols]
-    left, right, prod, counts, low = outs[3 + total_cols :]
+    given_ref = outs[3 + total_cols]
+    left, right, prod, counts, low = outs[4 + total_cols :]
     step = pl.program_id(0)
     group, places, width = pair_ref.shape
     seqs = rows_in[0].shape[1]
     lanes = 128
-    opm = cols_in[0].shape[0] - 1
-    blocks = rows_in[0].shape[0] - 1
+    chips = total_rows // 2
+    opm = cols_in[0].shape[0] // chips - 1
+    sent = rows_in[0].shape[0] // chips
+    blocks = left.shape[0]
     bf16 = jnp.bfloat16
 
     @pl.when(step == 0)
     def _():
         mark_rows, mark_cols = [], []
         for k in range(total_rows):
+            half, chip = k % 2, k // 2
             for g in range(blocks):
-                left[g, k * seqs : (k + 1) * seqs, :] = rows_in[k][g]
+                left[g, k * seqs : (k + 1) * seqs, :] = rows_in[half][
+                    chip * sent + spots[3, 0] * blocks + g
+                ]
             for e in range(opm):
-                right[k * seqs : (k + 1) * seqs, e * lanes : (e + 1) * lanes] = cols_in[k][e]
-            mark_rows.append(rows_in[k][blocks])
-            mark_cols.append(cols_in[k][opm])
+                right[k * seqs : (k + 1) * seqs, e * lanes : (e + 1) * lanes] = cols_in[half][
+                    chip * (opm + 1) + e
+                ]
+            mark_rows.append(rows_in[half][chip * sent + sent - 1])
+            mark_cols.append(cols_in[half][chip * (opm + 1) + opm])
         mark_rows = jnp.concatenate(mark_rows, axis=0)
         mark_cols = jnp.concatenate(mark_cols, axis=0)
         counts[...] = lax.dot_general(
@@ -229,8 +235,8 @@
         chunk = 512
         transposed = (((1,), (1,)), ((), ()))
         half_rows = open_ref.shape[0] // 2
-        each = half_rows // total_cols
-        count = each // total_rows
+        each = half_rows // total_cols // 2
+        count = each // chips
         for first in range(0, pairs, chunk):
             last = min(first + chunk, pairs)
             ours = high_ref[first:last, :]
@@ -247,21 +253,22 @@
                 jax.nn.sigmoid(opened[half_rows:]) * opened[:half_rows] * live_ref[:, first:last]
             )
             for m in range(total_cols):
-                for r in range(total_rows):
+                for r in range(chips):
                     at = m * each + r * count
                     side_refs[m][r, :, first:last] = sides[at : at + count].astype(bf16)
-
-
-def pair_stage(rows_in, cols_in, pair, spots, place, exit_t, near_t, open_t, score_t, live, total_cols):
-    total_rows = len(rows_in)
+                    at = (total_cols + m) * each + r * count
+                    given_ref[m, r, :, first:last] = sides[at : at + count].astype(bf16)
+
+
+def pair_stage(rows_in, cols_in, pair, spots, place, exit_t, near_t, open_t, score_t, live, total_rows, total_cols):
     tile_rows, places, width = pair.shape
-    blocks, seqs, lanes = rows_in[0].shape
-    blocks -= 1
+    sent, seqs, lanes = rows_in[0].shape
+    chips = total_rows // 2
+    blocks = (sent // chips - 1) // 2
     group = tile_rows // blocks
-    opm = cols_in[0].shape[0] - 1
+    opm = cols_in[0].shape[0] // chips - 1
     pairs = tile_rows * places
-    heads = 8
-    each = open_t.shape[0] // 2 // total_cols
+    count = open_t.shape[0] // 2 // total_cols // total_rows
     every = total_rows * seqs
 
     def whole(a):
@@ -277,7 +284,8 @@
         jax.ShapeDtypeStruct((pairs, width), jnp.float32),
         jax.ShapeDtypeStruct((pairs, width), bf16),
         jax.ShapeDtypeStruct((score_t.shape[0], pairs), bf16),
-    ] + [jax.ShapeDtypeStruct((total_rows, each // total_rows, pairs), bf16)] * total_cols
+    ] + [jax.ShapeDtypeStruct((chips, count, pairs), bf16)] * total_cols
+    outs.append(jax.ShapeDtypeStruct((total_cols, chips, count, pairs), bf16))
     return pl.pallas_call(
         functools.partial(pair_kernel, total_rows, total_cols),
         grid=(blocks,),
@@ -306,14 +314,15 @@
 
 
 def spread_slots(slots, stack, base_ref, tiles, total_cols, places):
-    total = len(slots)
+    total, high, wide = stack.shape
     pairs = slots[0].shape[1]
-    count = slots[0].shape[0] // total_cols
+    count = high // total_cols
     rows = pairs // places
     residues = rows * total
     lane = lax.broadcasted_iota(jnp.int32, (count, 128), 1)
     for k in range(total):
-        stack[k, :, :pairs] = slots[k][...]
+        slot, at = k % len(slots), k // len(slots) * high
+        stack[k, :, :pairs] = slots[slot][at : at + high]
 
     def one(k, carry):
         base = base_ref[k]
@@ -340,16 +349,16 @@
     lax.fori_loop(0, total, one, 0)
 
 
-def attention_kernel(total_rows, total_cols, *refs):
+def attention_kernel(halves, total_cols, *refs):
     base_ref = refs[0]
-    bias_in = refs[1 : 1 + total_rows]
-    x_in = refs[1 + total_rows : 1 + total_rows + total_cols]
-    mark_ref, project_ref, mix_ref = refs[1 + total_rows + total_cols : 4 + total_rows + total_cols]
-    outs = refs[4 + total_rows + total_cols : 4 + total_rows + 2 * total_cols]
-    stack, tiles, mixed = refs[4 + total_rows + 2 * total_cols :]
+    bias_in = refs[1 : 1 + halves]
+    x_in = refs[1 + halves : 1 + halves + total_cols]
+    mark_ref, project_ref, mix_ref = refs[1 + halves + total_cols : 4 + halves + total_cols]
+    outs = refs[4 + halves + total_cols : 4 + halves + 2 * total_cols]
+    stack, tiles, mixed = refs[4 + halves + 2 * total_cols :]
     places, width = x_in[0].shape[1:]
     residues = places * total_cols
-    heads = bias_in[0].shape[0] // total_cols
+    heads = stack.shape[1] // total_cols
     each = width // heads
     group = 128 // each
     padded = tiles.shape[0] * 128
@@ -403,11 +412,12 @@
 
 
 def attend(base, bias_slots, x_slots, marks, project, mix):
-    total_rows, total_cols = len(bias_slots), len(x_slots)
+    total_rows, total_cols = base.shape[0], len(x_slots)
     seqs, places, width = x_slots[0].shape
     residues = places * total_cols
     padded = -(-residues // 128) * 128
     rows, pairs = bias_slots[0].shape
+    rows = rows * len(bias_slots) // total_rows
     heads = rows // total_cols
     wide = -(-pairs // 128) * 128 + 128
 
@@ -417,7 +427,7 @@
     per_seq = pl.BlockSpec((1, places, width), lambda s: (s, 0, 0))
     bf16 = jnp.bfloat16
     return pl.pallas_call(
-        functools.partial(attention_kernel, total_rows, total_cols),
+        functools.partial(attention_kernel, len(bias_slots), total_cols),
         grid=(seqs,),
         in_specs=[pl.BlockSpec(memory_space=pltpu.SMEM)]
         + [whole(a) for a in bias_slots]
@@ -459,6 +469,22 @@
         compiler_params=pltpu.CompilerParams(vmem_limit_bytes=40 << 20),
         name="regroup",
     )(lead, *slots)
+
+
+def stack_kernel(*refs):
+    count = refs[0].shape[0]
+    for n, ref in enumerate(refs[:-1]):
+        refs[-1][n * count : (n + 1) * count] = ref[...]
+
+
+def stack_blocks(blocks):
+    shape = (len(blocks) * blocks[0].shape[0],) + blocks[0].shape[1:]
+    return pl.pallas_call(
+        stack_kernel,
+        out_shape=jax.ShapeDtypeStruct(shape, blocks[0].dtype),
+        compiler_params=pltpu.CompilerParams(vmem_limit_bytes=40 << 20),
+        name="stack_blocks",
+    )(*blocks)
 
 
 def triangle_kernel(total_rows, total_cols, *refs):
@@ -548,10 +574,14 @@
 
 
 def finish_kernel(total_rows, *refs):
-    slots = refs[:total_rows]
-    high_ref, z_ref, valve_ref, exit_ref, out_ref = refs[total_rows:]
+    lead_ref = refs[0]
+    slots = refs[1 : 1 + total_rows]
+    high_ref, z_ref, valve_ref, exit_ref, out_ref = refs[1 + total_rows :]
     pairs = out_ref.shape[0]
     chunk = 512
+    exits = jnp.concatenate(
+        [exit_ref[lead_ref[n]].astype(jnp.float32) for n in range(exit_ref.shape[0])], axis=0
+    ).astype(jnp.bfloat16)
     for first in range(0, pairs, chunk):
         last = min(first + chunk, pairs)
         crossed = jnp.concatenate(
@@ -561,7 +591,7 @@
         spread = jnp.mean(centred * centred, axis=0, keepdims=True)
         normed = (centred * lax.rsqrt(spread + norm_eps)).astype(jnp.bfloat16)
         projected = lax.dot_general(
-            normed, exit_ref[...], (((0,), (0,)), ((), ())), preferred_element_type=jnp.float32
+            normed, exits, (((0,), (0,)), ((), ())), preferred_element_type=jnp.float32
         )
         gate = jax.nn.sigmoid(
             jnp.dot(high_ref[first:last, :], valve_ref[...], preferred_element_type=jnp.float32)
@@ -569,13 +599,16 @@
         out_ref[first:last, :] = (z_ref[first:last, :] + gate * projected).astype(jnp.bfloat16)
 
 
-def finish(slots, high, z_one, valve, exit_w):
+def finish(lead, slots, high, z_one, valve, exit_w):
     return pl.pallas_call(
         functools.partial(finish_kernel, len(slots)),
+        in_specs=[pl.BlockSpec(memory_space=pltpu.SMEM)]
+        + [pl.BlockSpec(memory_space=pltpu.VMEM)] * (len(slots) + 4),
+        out_specs=pl.BlockSpec(memory_space=pltpu.VMEM),
         out_shape=jax.ShapeDtypeStruct(high.shape, jnp.bfloat16),
         compiler_params=pltpu.CompilerParams(vmem_limit_bytes=40 << 20),
         name="pair_finish",
-    )(*slots, high, z_one, valve, exit_w)
+    )(lead, *slots, high, z_one, valve, exit_w)
 
 
 def place_kernel(start_ref, *refs):
@@ -641,22 +674,38 @@
 
     marks = homolog_existence_marks.astype(jnp.float32)
     left, right = opm_operands(homolog_activations, marks, twofold_covariance_mapping)
-    right_slots = collect(right, "row")
-    left_slots_z = jnp.stack(collect(left, "col"))
-    blocks = (left.shape[0] - 1) // group_ratio
-    left_pieces = []
-    for k in range(row_total):
-        target = row_place ^ k
-        slot = (target // group_ratio) ^ col_place
-        mine = lax.dynamic_index_in_dim(left_slots_z, slot, 0, keepdims=False)
-        part = lax.dynamic_slice_in_dim(mine, target % group_ratio * blocks, blocks, 0)
-        left_pieces.append(jnp.concatenate([part, mine[-1:]], axis=0))
-    left_slots = swap(left_pieces, "row")
-
-    x_slots = exchange(
-        homolog_activations.reshape(col_total, own_seqs, block_columns, -1), "col"
-    )
-    own_marks = lax.dynamic_slice_in_dim(left_slots_z[:, -1], col_place * own_seqs, own_seqs, 1)
+    chips = range(0, row_total, 2)
+
+    def over_chips(pieces):
+        return [pieces[0]] + [
+            lax.ppermute(piece, "row", [(i, i ^ k) for i in range(row_total)])
+            for k, piece in zip(chips[1:], pieces[1:])
+        ]
+
+    def other_core(block):
+        return lax.ppermute(block, "row", [(i, i ^ 1) for i in range(row_total)])
+
+    left_z = collect(left, "col")
+    left_stack = jnp.stack(left_z)
+    right_even = jnp.concatenate(over_chips([right] * len(chips)), axis=0)
+    right_odd = other_core(right_even)
+    left_even = jnp.concatenate(
+        over_chips(
+            [
+                lax.dynamic_index_in_dim(
+                    left_stack, (row_place ^ k) // group_ratio ^ col_place, 0, keepdims=False
+                )
+                for k in chips
+            ]
+        ),
+        axis=0,
+    )
+    left_odd = other_core(left_even)
+    operands = [left_even, left_odd, right_even, right_odd]
+
+    operands, x_own = lax.optimization_barrier((operands, homolog_activations))
+    x_slots = exchange(x_own.reshape(col_total, own_seqs, block_columns, -1), "col")
+    own_marks = lax.dynamic_slice_in_dim(left_stack[:, -1], col_place * own_seqs, own_seqs, 1)
     own_marks = jnp.swapaxes(own_marks[:, :, :block_columns], 0, 1).reshape(own_seqs, 1, residues)
     padded = -(-residues // 128) * 128
     own_marks = jnp.pad(own_marks.astype(jnp.float32), ((0, 0), (0, 0), (0, padded - residues)))
@@ -667,6 +716,7 @@
             lax.dynamic_slice_in_dim(peptide_ordinals, row_first, tile_rows),
             lax.dynamic_slice_in_dim(strand_membership, row_first, tile_rows),
             jnp.full((tile_rows,), row_place % group_ratio * tile_rows, jnp.int32),
+            jnp.full((tile_rows,), row_place % group_ratio, jnp.int32),
         ]
     )
     place = jnp.pad(
@@ -683,45 +733,58 @@
     near_t = jnp.pad(
         distance_ordinal_vectors, ((0, lanes - distance_ordinal_vectors.shape[0]), (0, 0))
     ).T
-    open_t = triad_opening_mappings.reshape(pair_width, 2, 2, row_total, col_total, share)
-    open_t = open_t.transpose(2, 4, 3, 1, 5, 0)
+    open_t = triad_opening_mappings.reshape(
+        pair_width, 2, 2, row_total // 2, 2, col_total, share
+    )
+    open_t = open_t.transpose(2, 4, 5, 3, 1, 6, 0)
     open_t = jnp.concatenate(
-        [
-            lax.dynamic_slice_in_dim(open_t, col_place ^ m, 1, 1)
-            for m in range(col_total)
-        ],
-        axis=1,
+        [lax.dynamic_slice_in_dim(open_t, row_place % 2 ^ h, 1, 1) for h in range(2)], axis=1
+    )
+    open_t = jnp.concatenate(
+        [lax.dynamic_slice_in_dim(open_t, col_place ^ m, 1, 2) for m in range(col_total)], axis=2
     ).reshape(4 * tri_width, pair_width)
     score_t = coupling_score_mapping.T
     live_rows = lax.dynamic_slice_in_dim(observed_peptide_marks, row_first, tile_rows)
     live_cols = lax.dynamic_slice_in_dim(observed_peptide_marks, col_first, block_columns)
     live = (live_rows[:, None] * live_cols[None, :]).astype(jnp.float32).reshape(1, -1)
-    z_one, ln_tri, bias_flat, *side_pieces = pair_stage(
-        left_slots, right_slots, coupling_activations, spots, place, exit_t, near_t, open_t,
-        score_t, live, col_total,
-    )
+    z_one, ln_tri, bias_flat, *kept, given = pair_stage(
+        operands[:2], operands[2:], coupling_activations, spots, place, exit_t, near_t, open_t,
+        score_t, live, row_total, col_total,
+    )
+    bias_flat, x_slots = lax.optimization_barrier((bias_flat, x_slots))
 
     row_ids = row_place ^ jnp.arange(row_total, dtype=jnp.int32)
     col_ids = col_place ^ jnp.arange(col_total, dtype=jnp.int32)
     base = (row_ids // group_ratio ^ col_place) * block_columns + row_ids % group_ratio * tile_rows
-    bias_part = jnp.concatenate(collect(bias_flat, "col"), axis=0)
-    side_slots = swap(side_pieces, "col")
-    bias_slots = collect(bias_part, "row")
-    side_slots = swap(regroup(row_ids, side_slots), "row")
+    chip_ids = row_ids[::2] // 2
+    received = other_core(given)
+    bias_part, kept = lax.optimization_barrier((collect(bias_flat, "col"), kept))
+    bias_part = stack_blocks(bias_part)
+    kept = swap(kept, "col")
+    bias_even = stack_blocks(over_chips([bias_part] * len(chips)))
+    bias_slots = [bias_even, other_core(bias_even)]
+    kept, received = lax.optimization_barrier((kept, received))
+    received = swap([received[m] for m in range(col_total)], "col")
+    kept = over_chips(regroup(chip_ids, kept))
 
     project = jnp.concatenate(
         [question_mapping_weights, address_payload_mapping, logistic_valve_mapping], axis=1
     )
     own_after = attend(base, bias_slots, x_slots, own_marks, project, mixture_exit_mapping)
+
     after_slots = swap(own_after, "col")
     homologs_after = place_slots(col_ids * own_seqs, after_slots)
 
+    received, own_after = lax.optimization_barrier((received, own_after))
+    received = over_chips(regroup(chip_ids, received))
+    side_slots = [slot for both in zip(kept, received) for slot in both]
     crossed = triangle(base, side_slots, share, col_total, residues)
+    crossed, after_slots = lax.optimization_barrier((crossed, after_slots))
     crossed = swap(crossed, "col")
     crossed = swap(regroup(jnp.arange(row_total, dtype=jnp.int32), crossed), "row")
-    exit_w = triad_exit_mapping.reshape(row_total, col_total, share, pair_width)
-    exit_w = exit_w[row_ids][:, col_ids].reshape(tri_width, pair_width)
-    couplings_after = finish(crossed, ln_tri, z_one, triad_valve_mapping, exit_w)
+    exit_w = triad_exit_mapping.reshape(devices, share, pair_width)
+    lead = (row_ids[:, None] * col_total + col_ids[None, :]).reshape(-1)
+    couplings_after = finish(lead, crossed, ln_tri, z_one, triad_valve_mapping, exit_w)
     return (homologs_after, couplings_after.reshape(coupling_activations.shape))
 
 

time: 247 us -> 206 us (0.83)
  waiting for transfers between devices: 97.9 us -> 61.8 us
  starting transfers between devices: 56.9 us -> 52.1 us
    ppermute x53 -> x28, waiting for transfers between devices: 97.9 us -> 44.4 us  [swap(): lax.ppermute(pieces[k], axis, [(i, i ^ k) for i in range(total)])]
    ppermute x53 -> x28, starting transfers between devices: 56.9 us -> 28.4 us  [swap(): lax.ppermute(pieces[k], axis, [(i, i ^ k) for i in range(total)])]
    ppermute x0 -> x19, starting transfers between devices: none -> 23.7 us  [the longest x15 15.5 us: over_chips(): lax.ppermute(piece, 'row', [(i, i ^ k) for i in range(row_total)])]
    ppermute x0 -> x19, waiting for transfers between devices: none -> 17.4 us  [the longest x15 17.4 us: over_chips(): lax.ppermute(piece, 'row', [(i, i ^ k) for i in range(row_total)])]
    gather x4 -> x0, local copies, waits for them, and re-layouts: 5.25 us -> none  [shards(): exit_w = exit_w[row_ids][:, col_ids].reshape(tri_width, pair_width)]
    unnamed x112 -> x88, local copies, waits for them, and re-layouts: 10.9 us -> 10.7 us
    pallas_call x2 -> x4, Pallas kernels: 31.4 us -> 31.3 us  [the longest x1 28.1 us: attend(): pl.pallas_call(functools.partial(attention_kernel, len(bias_slots), total...]
  transfers between devices with their start and end apart: 53 -> 47, of which waited for: 17 -> 19; matrix products, arithmetic and copies ran while one was open for 6% -> 7% of each run, Pallas kernels for 24% -> 28%
where the time goes in v2:
time: 206 us; the launch traced here: 205 us
  Pallas kernels  63.7 us (31%)
  waiting for transfers between devices  61.8 us (30%)
  starting transfers between devices  52.1 us (25%)
  local copies, waits for them, and re-layouts  23.1 us (11%)
  other arithmetic  3.21 us (2%)
    ppermute x28, waiting for transfers between devices, swap(): lax.ppermute(pieces[k], axis, [(i, i ^ k) for i in range(total)])  44.4 us
    ppermute x28, starting transfers between devices, swap(): lax.ppermute(pieces[k], axis, [(i, i ^ k) for i in range(total)])  28.4 us
    pallas_call x1, Pallas kernels, attend(): pl.pallas_call(functools.partial(attention_kernel, len(bias_slots), total...  28.1 us
    ppermute x15, waiting for transfers between devices, over_chips(): lax.ppermute(piece, 'row', [(i, i ^ k) for i in range(row_total)])  17.4 us
    pallas_call x1, Pallas kernels, pair_stage(): pl.pallas_call(functools.partial(pair_kernel, total_rows, total_cols), gr...  17 us
    ppermute x15, starting transfers between devices, over_chips(): lax.ppermute(piece, 'row', [(i, i ^ k) for i in range(row_total)])  15.5 us
    unnamed x88, local copies, waits for them, and re-layouts  10.7 us
    pallas_call x1, Pallas kernels, triangle(): pl.pallas_call(functools.partial(triangle_kernel, total_rows, total_cols)...  10.2 us
  transfers between devices with their start and end apart: 47, of which 19 were waited for; matrix products, arithmetic and copies ran while one was open for 7% of the time, Pallas kernels for 28%

profile of v2, /device:TPU:9, one launch (start us, length us, event | category | flops | bytes accessed | tf_op | source)
XLA Modules:
  0.0 205.1 jit_solution(4923932212682349328)
XLA Ops:
  2.2 1.0 outer_operands.1
  3.3 2.4 %collective-permute-start.1 = (bf16[23,16,128]{2,1,0:T(8,128)(2,1)S(1)}, bf16[23,16,128]{2,1,0:T(8,128)(2,1)S(1)}, u32[]{:S(2)}, u32[]{:S(2)}) collective-permute-start(bf16[23,16,128]{2,1,0:T(8,128)(2,1)S(1)} %get-tuple-element.67), channel_id=1, source_target_pairs={{0,2},{1,3},{2,0},{3,1},{4,6},{5,7},{6,4},{7,5},{8,10},{9,11},{10,... | collective-permute-start | bytes 282632 | tf_op jit(solution)/shard_map/ppermute | solution.py:22
  5.7 1.3 collective-permute-start
  6.9 1.2 collective-permute-start.7
  8.1 1.2 collective-permute-start.8
  10.2 1.8 collective-permute-done.1
  12.1 2.2 %collective-permute-start.9 = (bf16[33,16,128]{2,1,0:T(8,128)(2,1)S(1)}, bf16[33,16,128]{2,1,0:T(8,128)(2,1)S(1)}, u32[]{:S(2)}, u32[]{:S(2)}) collective-permute-start(bf16[33,16,128]{2,1,0:T(8,128)(2,1)S(1)} %get-tuple-element.68), channel_id=1, source_target_pairs={{0,24},{4,28},{8,16},{12,20},{16,8},{20,12},{24,0},{28,4},{1,25},{... | collective-permute-start | bytes 405512 | tf_op jit(solution)/shard_map/ppermute | solution.py:681
  14.3 1.1 collective-permute-start.3
  15.5 1.2 collective-permute-start.4
  17.5 2.1 %collective-permute-start.10 = (bf16[132,16,128]{2,1,0:T(8,128)(2,1)S(1)}, bf16[132,16,128]{2,1,0:T(8,128)(2,1)}, u32[]{:S(2)}, u32[]{:S(2)}) collective-permute-start(bf16[132,16,128]{2,1,0:T(8,128)(2,1)S(1)} %constant_dynamic-update-slice_fusion.refs_3_), channel_id=1, source_target_pairs={{0,4},{4,0},{8,12},{12,8},{16,20},{20,16},{24,28},{28,24},{1,5},{5... | collective-permute-start | bytes 1622024 | tf_op jit(solution)/shard_map/ppermute | solution.py:686
  19.9 1.5 collective-permute-done.5
  21.5 1.9 collective-permute-start.6
  29.8 3.0 %collective-permute-start.12 = (bf16[4,88,256]{2,1,0:T(8,128)(2,1)S(1)}, bf16[4,88,256]{2,1,0:T(8,128)(2,1)S(1)}, u32[]{:S(2)}, u32[]{:S(2)}) collective-permute-start(bf16[4,88,256]{2,1,0:T(8,128)(2,1)S(1)} %get-tuple-element.137), channel_id=1, source_target_pairs={{0,2},{1,3},{2,0},{3,1},{4,6},{5,7},{6,4},{7,5},{8,10},{9,11},{10,... | collective-permute-start | bytes 540680 | tf_op jit(solution)/shard_map/ppermute | solution.py:22
  32.8 17.0 %pair_update.1 = (f32[3872,128]{1,0:T(8,128)}, bf16[3872,128]{1,0:T(8,128)(2,1)}, bf16[8,3872]{1,0:T(8,128)(2,1)}, bf16[4,8,3872]{2,1,0:T(8,128)(2,1)}, bf16[4,8...) custom-call(s32[4,44]{1,0:T(4,128)} %add_add_fusion.refs_0_, ...), custom_call_target="tpu_custom_call" | custom-call | flops 20000000000 | bytes 16000000 | tf_op jit(solution)/shard_map/pair_update/pallas_call | solution.py:289
  50.6 1.2 collective-permute-start.14
  51.8 2.2 %collective-permute-start.15 = (bf16[8,3872]{1,0:T(8,128)(2,1)}, bf16[8,3872]{1,0:T(8,128)(2,1)S(1)}, u32[]{:S(2)}, u32[]{:S(2)}) collective-permute-start(bf16[8,3872]{1,0:T(8,128)(2,1)} %get-tuple-element.80.refs_0_), channel_id=1, source_target_pairs={{0,2},{1,3},{2,0},{3,1},{4,6},{5,7},{6,4},{7,5},{8,10},{9,11},{10,... | collective-permute-start | bytes 185864 | tf_op jit(solution)/shard_map/ppermute | solution.py:22
  54.6 3.4 %collective-permute-done.15.refs_2_ = bf16[8,3872]{1,0:T(8,128)(2,1)S(1)} collective-permute-done((bf16[8,3872]{1,0:T(8,128)(2,1)}, bf16[8,3872]{1,0:T(8,128)(2,1)S(1)}, u32[]{:S(2)}, u32[]{:S(2)}) %collective-permute-start.15) | collective-permute-done | bytes 61984 | tf_op jit(solution)/shard_map/ppermute | solution.py:22
  57.9 2.9 %collective-permute-done.16.refs_3_ = bf16[8,3872]{1,0:T(8,128)(2,1)S(1)} collective-permute-done((bf16[8,3872]{1,0:T(8,128)(2,1)}, bf16[8,3872]{1,0:T(8,128)(2,1)S(1)}, u32[]{:S(2)}, u32[]{:S(2)}) %collective-permute-start.16) | collective-permute-done | bytes 61984 | tf_op jit(solution)/shard_map/ppermute | solution.py:22
  61.7 1.3 collective-permute-start.17
  63.0 1.2 collective-permute-start.18
  65.8 2.8 %collective-permute-done.17.refs_1_ = bf16[32,3872]{1,0:T(8,128)(2,1)S(1)} collective-permute-done((bf16[32,3872]{1,0:T(8,128)(2,1)S(1)}, bf16[32,3872]{1,0:T(8,128)(2,1)S(1)}, u32[]{:S(2)}, u32[]{:S(2)}) %collective-permute-start.17) | collective-permute-done | bytes 247840 | tf_op jit(solution)/shard_map/ppermute | solution.py:681
  69.5 1.2 collective-permute-start.26
  70.8 4.3 %collective-permute-done.19.refs_3_ = bf16[32,3872]{1,0:T(8,128)(2,1)S(1)} collective-permute-done((bf16[32,3872]{1,0:T(8,128)(2,1)S(1)}, bf16[32,3872]{1,0:T(8,128)(2,1)S(1)}, u32[]{:S(2)}, u32[]{:S(2)}) %collective-permute-start.19) | collective-permute-done | bytes 247840 | tf_op jit(solution)/shard_map/ppermute | solution.py:681
  75.2 1.4 copy.48
  76.6 3.5 %collective-permute-start.20 = (bf16[128,3872]{0,1:T(8,128)(2,1)}, bf16[128,3872]{0,1:T(8,128)(2,1)}, u32[]{:S(2)}, u32[]{:S(2)}) collective-permute-start(bf16[128,3872]{0,1:T(8,128)(2,1)} %copy.48), channel_id=1, source_target_pairs={{0,4},{4,0},{8,12},{12,8},{16,20},{20,16},{24,28},{28,24},{1,5},{5... | collective-permute-start | bytes 2973704 | tf_op jit(solution)/shard_map/ppermute | solution.py:686
  80.7 9.8 %collective-permute-done.26.refs_3_ = bf16[4,8,3872]{2,1,0:T(8,128)(2,1)S(1)} collective-permute-done((bf16[4,8,3872]{2,1,0:T(8,128)(2,1)}, bf16[4,8,3872]{2,1,0:T(8,128)(2,1)S(1)}, u32[]{:S(2)}, u32[]{:S(2)}) %collective-permute-start.26) | collective-permute-done | bytes 247840 | tf_op jit(solution)/shard_map/ppermute | solution.py:22
  90.5 2.2 %slice_bitcast_fusion = (bf16[4,8,3872]{2,1,0:T(8,128)(2,1)S(1)}, bf16[4,8,3872]{2,1,0:T(8,128)(2,1)}, bf16[4,8,3872]{2,1,0:T(8,128)(2,1)}, bf16[4,8,3872]{2,1,0:T(8,128)(2,1)S(1)}) fusion(bf16[4,4,8,3872]{3,2,1,0:T(8,128)(2,1)} %collective-permute-done.27), kind=kLoop, calls=%fused_computation.4 | loop fusion | bytes 1982464 | tf_op jit(solution)/shard_map/squeeze | solution.py:767
  93.6 1.8 collective-permute-start.30
  96.7 1.2 collective-permute-start.33
  97.9 2.3 %copy.51.refs_2_ = bf16[128,3872]{1,0:T(8,128)(2,1)} copy(bf16[128,3872]{0,1:T(8,128)(2,1)} %collective-permute-done.20) | data formatting | bytes 1982464 | tf_op jit(solution)/shard_map/ppermute | solution.py:686
  100.1 28.1 %row_attention.1 = (bf16[4,88,256]{2,1,0:T(8,128)(2,1)}, bf16[4,88,256]{2,1,0:T(8,128)(2,1)}, bf16[4,88,256]{2,1,0:T(8,128)(2,1)}, bf16[4,88,256]{2,1,0:T(8,128)(2,1)}) custom-call(s32[8]{0:T(128)} %fusion.7.refs_0_, bf16[128,3872]{1,0:T(8,128)(2,1)} %copy-done, bf16[128,3872]{1,0:T(8,128)(2,1)} %copy.51.refs_2_, ...), custom_call_target="tpu_custom_call" | custom-call | flops 40000000000 | bytes 30000000 | tf_op jit(solution)/shard_map/row_attention/pallas_call | solution.py:429
  131.1 1.2 collective-permute-start.34
  137.0 5.7 %collective-permute-done.36.refs_8_ = bf16[32,3872]{1,0:T(8,128)(2,1)S(1)} collective-permute-done((bf16[32,3872]{1,0:T(8,128)(2,1)S(1)}, bf16[32,3872]{1,0:T(8,128)(2,1)S(1)}, u32[]{:S(2)}, u32[]{:S(2)}) %collective-permute-start.36) | collective-permute-done | bytes 247840 | tf_op jit(solution)/shard_map/ppermute | solution.py:681
  143.4 10.2 %triangle.1 = (bf16[8,4,3872]{2,1,0:T(4,128)(2,1)}, bf16[8,4,3872]{2,1,0:T(4,128)(2,1)}, bf16[8,4,3872]{2,1,0:T(4,128)(2,1)}, bf16[8,4,3872]{2,1,0:T(4,128)(2,1)}) custom-call(s32[8]{0:T(128)} %fusion.7.refs_0_, bf16[32,3872]{1,0:T(8,128)(2,1)} %copy-done.18, bf16[32,3872]{1,0:T(8,128)(2,1)} %copy-done.19, bf16[32,3872]{1,0:T(8,128)(2,1)} %copy-done.32, ...), custom_call_target="tpu_custom_call" | custom-call | flops 10000000000 | bytes 8000000 | tf_op jit(solution)/shard_map/triangle/pallas_call | solution.py:557
  153.7 1.0 collective-permute-start.37
  154.8 1.7 collective-permute-start.39
  156.4 2.9 %collective-permute-done.37.refs_1_ = bf16[8,4,3872]{2,1,0:T(4,128)(2,1)S(1)} collective-permute-done((bf16[8,4,3872]{2,1,0:T(4,128)(2,1)}, bf16[8,4,3872]{2,1,0:T(4,128)(2,1)S(1)}, u32[]{:S(2)}, u32[]{:S(2)}) %collective-permute-start.37) | collective-permute-done | bytes 247840 | tf_op jit(solution)/shard_map/ppermute | solution.py:22
  159.3 2.1 %collective-permute-done.38.refs_2_ = bf16[8,4,3872]{2,1,0:T(4,128)(2,1)S(1)} collective-permute-done((bf16[8,4,3872]{2,1,0:T(4,128)(2,1)}, bf16[8,4,3872]{2,1,0:T(4,128)(2,1)S(1)}, u32[]{:S(2)}, u32[]{:S(2)}) %collective-permute-start.38) | collective-permute-done | bytes 247840 | tf_op jit(solution)/shard_map/ppermute | solution.py:22
  161.4 16.4 %collective-permute-done.39.refs_3_ = bf16[8,4,3872]{2,1,0:T(4,128)(2,1)S(1)} collective-permute-done((bf16[8,4,3872]{2,1,0:T(4,128)(2,1)}, bf16[8,4,3872]{2,1,0:T(4,128)(2,1)S(1)}, u32[]{:S(2)}, u32[]{:S(2)}) %collective-permute-start.39) | collective-permute-done | bytes 247840 | tf_op jit(solution)/shard_map/ppermute | solution.py:22
  178.8 1.4 regroup.5
  180.8 2.3 %collective-permute-start.40 = (bf16[16,3872]{1,0:T(8,128)(2,1)S(1)}, bf16[16,3872]{1,0:T(8,128)(2,1)S(1)}, u32[]{:S(2)}, u32[]{:S(2)}) collective-permute-start(bf16[16,3872]{1,0:T(8,128)(2,1)S(1)} %get-tuple-element.123), channel_id=1, source_target_pairs={{0,4},{4,0},{8,12},{12,8},{16,20},{20,16},{24,28},{28,24},{1,5},{5... | collective-permute-start | bytes 371720 | tf_op jit(solution)/shard_map/ppermute | solution.py:22
  183.1 1.2 collective-permute-start.41
  185.0 1.6 collective-permute-start.44
  187.3 1.2 collective-permute-start.45
  189.1 2.0 collective-permute-start.46
  192.2 1.4 place_sequences.1
  193.6 4.8 %collective-permute-done.44.refs_6_ = bf16[16,3872]{1,0:T(8,128)(2,1)} collective-permute-done((bf16[16,3872]{1,0:T(8,128)(2,1)}, bf16[16,3872]{1,0:T(8,128)(2,1)}, u32[]{:S(2)}, u32[]{:S(2)}) %collective-permute-start.44) | collective-permute-done | bytes 123936 | tf_op jit(solution)/shard_map/ppermute | solution.py:22
  201.9 3.2 %pair_finish.1 = bf16[3872,128]{1,0:T(8,128)(2,1)} custom-call(s32[32]{0:T(128)S(1)} %add.121.refs_0_, bf16[16,3872]{1,0:T(8,128)(2,1)S(1)} %copy-done.10, bf16[16,3872]{1,0:T(8,128)(2,1)S(1)} %copy-done.12, bf16[16,3872]{1,0:T(8,128)(2,1)S(1)} %copy-done.14, bf16[16,3872]{1,0:T(8,128)(2,1)} %collective-permute-done.42.refs_4_, ...), custom_call_target="tpu_custom_call" | custom-call | tf_op jit(solution)/shard_map/pair_finish/pallas_call | solution.py:603
  (194 shorter events, 34.0 us)
Async XLA Ops:
  3.3 8.8 %collective-permute-start.1 = (bf16[23,16,128]{2,1,0:T(8,128)(2,1)S(1)}, bf16[23,16,128]{2,1,0:T(8,128)(2,1)S(1)}, u32[]{:S(2)}, u32[]{:S(2)}) collective-permute-start(bf16[23,16,128]{2,1,0:T(8,128)(2,1)S(1)} %get-tuple-element.67), channel_id=1, source_target_pairs={{0,2},{1,3},{2,0},{3,1},{4,6},{5,7},{6,4},{7,5},{8,10},{9,11},{10,... | collective-permute-start | bytes 282632 | tf_op jit(solution)/shard_map/ppermute | solution.py:22
  5.7 8.6 %collective-permute-start.2 = (bf16[23,16,128]{2,1,0:T(8,128)(2,1)S(1)}, bf16[23,16,128]{2,1,0:T(8,128)(2,1)S(1)}, u32[]{:S(2)}, u32[]{:S(2)}) collective-permute-start(bf16[23,16,128]{2,1,0:T(8,128)(2,1)S(1)} %get-tuple-element.67), channel_id=1, source_target_pairs={{0,3},{1,2},{2,1},{3,0},{4,7},{5,6},{6,5},{7,4},{8,11},{9,10},{10,... | collective-permute-start | bytes 282632 | tf_op jit(solution)/shard_map/ppermute | solution.py:22
  5.7 8.6 %collective-permute-start = (bf16[23,16,128]{2,1,0:T(8,128)(2,1)S(1)}, bf16[23,16,128]{2,1,0:T(8,128)(2,1)S(1)}, u32[]{:S(2)}, u32[]{:S(2)}) collective-permute-start(bf16[23,16,128]{2,1,0:T(8,128)(2,1)S(1)} %get-tuple-element.67), channel_id=1, source_target_pairs={{0,1},{1,0},{2,3},{3,2},{4,5},{5,4},{6,7},{7,6},{8,9},{9,8},{10,11... | collective-permute-start | bytes 282632 | tf_op jit(solution)/shard_map/ppermute | solution.py:22
  6.9 9.8 %collective-permute-start.7 = (bf16[33,16,128]{2,1,0:T(8,128)(2,1)S(1)}, bf16[33,16,128]{2,1,0:T(8,128)(2,1)S(1)}, u32[]{:S(2)}, u32[]{:S(2)}) collective-permute-start(bf16[33,16,128]{2,1,0:T(8,128)(2,1)S(1)} %get-tuple-element.68), channel_id=1, source_target_pairs={{0,8},{4,12},{8,0},{12,4},{16,24},{20,28},{24,16},{28,20},{1,9},{5... | collective-permute-start | bytes 405512 | tf_op jit(solution)/shard_map/ppermute | solution.py:681
  8.1 9.0 %collective-permute-start.8 = (bf16[33,16,128]{2,1,0:T(8,128)(2,1)S(1)}, bf16[33,16,128]{2,1,0:T(8,128)(2,1)S(1)}, u32[]{:S(2)}, u32[]{:S(2)}) collective-permute-start(bf16[33,16,128]{2,1,0:T(8,128)(2,1)S(1)} %get-tuple-element.68), channel_id=1, source_target_pairs={{0,16},{4,20},{8,24},{12,28},{16,0},{20,4},{24,8},{28,12},{1,17},{... | collective-permute-start | bytes 405512 | tf_op jit(solution)/shard_map/ppermute | solution.py:681
  12.1 5.5 %collective-permute-start.9 = (bf16[33,16,128]{2,1,0:T(8,128)(2,1)S(1)}, bf16[33,16,128]{2,1,0:T(8,128)(2,1)S(1)}, u32[]{:S(2)}, u32[]{:S(2)}) collective-permute-start(bf16[33,16,128]{2,1,0:T(8,128)(2,1)S(1)} %get-tuple-element.68), channel_id=1, source_target_pairs={{0,24},{4,28},{8,16},{12,20},{16,8},{20,12},{24,0},{28,4},{1,25},{... | collective-permute-start | bytes 405512 | tf_op jit(solution)/shard_map/ppermute | solution.py:681
  14.3 5.3 %collective-permute-start.3 = (bf16[23,16,128]{2,1,0:T(8,128)(2,1)S(1)}, bf16[23,16,128]{2,1,0:T(8,128)(2,1)S(1)}, u32[]{:S(2)}, u32[]{:S(2)}) collective-permute-start(bf16[23,16,128]{2,1,0:T(8,128)(2,1)S(1)} %get-tuple-element.143), channel_id=1, source_target_pairs={{0,8},{4,12},{8,0},{12,4},{16,24},{20,28},{24,16},{28,20},{1,9},{5... | collective-permute-start | bytes 282632 | tf_op jit(solution)/shard_map/ppermute | solution.py:681
  15.5 4.5 %collective-permute-start.4 = (bf16[23,16,128]{2,1,0:T(8,128)(2,1)S(1)}, bf16[23,16,128]{2,1,0:T(8,128)(2,1)S(1)}, u32[]{:S(2)}, u32[]{:S(2)}) collective-permute-start(bf16[23,16,128]{2,1,0:T(8,128)(2,1)S(1)} %get-tuple-element.142), channel_id=1, source_target_pairs={{0,16},{4,20},{8,24},{12,28},{16,0},{20,4},{24,8},{28,12},{1,17},{... | collective-permute-start | bytes 282632 | tf_op jit(solution)/shard_map/ppermute | solution.py:681
  16.7 4.7 %collective-permute-start.5 = (bf16[23,16,128]{2,1,0:T(8,128)(2,1)S(1)}, bf16[23,16,128]{2,1,0:T(8,128)(2,1)S(1)}, u32[]{:S(2)}, u32[]{:S(2)}) collective-permute-start(bf16[23,16,128]{2,1,0:T(8,128)(2,1)S(1)} %get-tuple-element.141), channel_id=1, source_target_pairs={{0,24},{4,28},{8,16},{12,20},{16,8},{20,12},{24,0},{28,4},{1,25},{... | collective-permute-start | bytes 282632 | tf_op jit(solution)/shard_map/ppermute | solution.py:681
  17.5 10.4 %collective-permute-start.10 = (bf16[132,16,128]{2,1,0:T(8,128)(2,1)S(1)}, bf16[132,16,128]{2,1,0:T(8,128)(2,1)}, u32[]{:S(2)}, u32[]{:S(2)}) collective-permute-start(bf16[132,16,128]{2,1,0:T(8,128)(2,1)S(1)} %constant_dynamic-update-slice_fusion.refs_3_), channel_id=1, source_target_pairs={{0,4},{4,0},{8,12},{12,8},{16,20},{20,16},{24,28},{28,24},{1,5},{5... | collective-permute-start | bytes 1622024 | tf_op jit(solution)/shard_map/ppermute | solution.py:686
  21.5 6.4 %collective-permute-start.6 = (bf16[92,16,128]{2,1,0:T(8,128)(2,1)S(1)}, bf16[92,16,128]{2,1,0:T(8,128)(2,1)S(1)}, u32[]{:S(2)}, u32[]{:S(2)}) collective-permute-start(bf16[92,16,128]{2,1,0:T(8,128)(2,1)S(1)} %pad_maximum_fusion.2.refs_1_), channel_id=1, source_target_pairs={{0,4},{4,0},{8,12},{12,8},{16,20},{20,16},{24,28},{28,24},{1,5},{5... | collective-permute-start | bytes 1130504 | tf_op jit(solution)/shard_map/ppermute | solution.py:686
  29.4 21.2 %collective-permute-start.11 = (bf16[4,88,256]{2,1,0:T(8,128)(2,1)S(1)}, bf16[4,88,256]{2,1,0:T(8,128)(2,1)S(1)}, u32[]{:S(2)}, u32[]{:S(2)}) collective-permute-start(bf16[4,88,256]{2,1,0:T(8,128)(2,1)S(1)} %get-tuple-element.138), channel_id=1, source_target_pairs={{0,1},{1,0},{2,3},{3,2},{4,5},{5,4},{6,7},{7,6},{8,9},{9,8},{10,11... | collective-permute-start | bytes 540680 | tf_op jit(solution)/shard_map/ppermute | solution.py:22
  29.8 20.9 %collective-permute-start.12 = (bf16[4,88,256]{2,1,0:T(8,128)(2,1)S(1)}, bf16[4,88,256]{2,1,0:T(8,128)(2,1)S(1)}, u32[]{:S(2)}, u32[]{:S(2)}) collective-permute-start(bf16[4,88,256]{2,1,0:T(8,128)(2,1)S(1)} %get-tuple-element.137), channel_id=1, source_target_pairs={{0,2},{1,3},{2,0},{3,1},{4,6},{5,7},{6,4},{7,5},{8,10},{9,11},{10,... | collective-permute-start | bytes 540680 | tf_op jit(solution)/shard_map/ppermute | solution.py:22
  32.8 17.9 %collective-permute-start.13 = (bf16[4,88,256]{2,1,0:T(8,128)(2,1)S(1)}, bf16[4,88,256]{2,1,0:T(8,128)(2,1)S(1)}, u32[]{:S(2)}, u32[]{:S(2)}) collective-permute-start(bf16[4,88,256]{2,1,0:T(8,128)(2,1)S(1)} %get-tuple-element.136), channel_id=1, source_target_pairs={{0,3},{1,2},{2,1},{3,0},{4,7},{5,6},{6,5},{7,4},{8,11},{9,10},{10,... | collective-permute-start | bytes 540680 | tf_op jit(solution)/shard_map/ppermute | solution.py:22
  49.8 40.7 %collective-permute-start.27 = (bf16[4,4,8,3872]{3,2,1,0:T(8,128)(2,1)}, bf16[4,4,8,3872]{3,2,1,0:T(8,128)(2,1)}, u32[]{:S(2)}, u32[]{:S(2)}) collective-permute-start(bf16[4,4,8,3872]{3,2,1,0:T(8,128)(2,1)} %get-tuple-element.96), channel_id=1, source_target_pairs={{0,4},{4,0},{8,12},{12,8},{16,20},{20,16},{24,28},{28,24},{1,5},{5... | collective-permute-start | bytes 2973704 | tf_op jit(solution)/shard_map/ppermute | solution.py:686
  50.6 3.9 %collective-permute-start.14 = (bf16[8,3872]{1,0:T(8,128)(2,1)}, bf16[8,3872]{1,0:T(8,128)(2,1)S(1)}, u32[]{:S(2)}, u32[]{:S(2)}) collective-permute-start(bf16[8,3872]{1,0:T(8,128)(2,1)} %get-tuple-element.80.refs_0_), channel_id=1, source_target_pairs={{0,1},{1,0},{2,3},{3,2},{4,5},{5,4},{6,7},{7,6},{8,9},{9,8},{10,11... | collective-permute-start | bytes 185864 | tf_op jit(solution)/shard_map/ppermute | solution.py:22
  51.8 6.1 %collective-permute-start.15 = (bf16[8,3872]{1,0:T(8,128)(2,1)}, bf16[8,3872]{1,0:T(8,128)(2,1)S(1)}, u32[]{:S(2)}, u32[]{:S(2)}) collective-permute-start(bf16[8,3872]{1,0:T(8,128)(2,1)} %get-tuple-element.80.refs_0_), channel_id=1, source_target_pairs={{0,2},{1,3},{2,0},{3,1},{4,6},{5,7},{6,4},{7,5},{8,10},{9,11},{10,... | collective-permute-start | bytes 185864 | tf_op jit(solution)/shard_map/ppermute | solution.py:22
  54.1 6.8 %collective-permute-start.16 = (bf16[8,3872]{1,0:T(8,128)(2,1)}, bf16[8,3872]{1,0:T(8,128)(2,1)S(1)}, u32[]{:S(2)}, u32[]{:S(2)}) collective-permute-start(bf16[8,3872]{1,0:T(8,128)(2,1)} %get-tuple-element.80.refs_0_), channel_id=1, source_target_pairs={{0,3},{1,2},{2,1},{3,0},{4,7},{5,6},{6,5},{7,4},{8,11},{9,10},{10,... | collective-permute-start | bytes 185864 | tf_op jit(solution)/shard_map/ppermute | solution.py:22
  61.7 7.0 %collective-permute-start.17 = (bf16[32,3872]{1,0:T(8,128)(2,1)S(1)}, bf16[32,3872]{1,0:T(8,128)(2,1)S(1)}, u32[]{:S(2)}, u32[]{:S(2)}) collective-permute-start(bf16[32,3872]{1,0:T(8,128)(2,1)S(1)} %stack_blocks.2.refs_0_), channel_id=1, source_target_pairs={{0,8},{4,12},{8,0},{12,4},{16,24},{20,28},{24,16},{28,20},{1,9},{5... | collective-permute-start | bytes 743432 | tf_op jit(solution)/shard_map/ppermute | solution.py:681
  63.0 6.6 %collective-permute-start.18 = (bf16[32,3872]{1,0:T(8,128)(2,1)S(1)}, bf16[32,3872]{1,0:T(8,128)(2,1)S(1)}, u32[]{:S(2)}, u32[]{:S(2)}) collective-permute-start(bf16[32,3872]{1,0:T(8,128)(2,1)S(1)} %stack_blocks.2.refs_0_), channel_id=1, source_target_pairs={{0,16},{4,20},{8,24},{12,28},{16,0},{20,4},{24,8},{28,12},{1,17},{... | collective-permute-start | bytes 743432 | tf_op jit(solution)/shard_map/ppermute | solution.py:681
  65.6 9.5 %collective-permute-start.19 = (bf16[32,3872]{1,0:T(8,128)(2,1)S(1)}, bf16[32,3872]{1,0:T(8,128)(2,1)S(1)}, u32[]{:S(2)}, u32[]{:S(2)}) collective-permute-start(bf16[32,3872]{1,0:T(8,128)(2,1)S(1)} %stack_blocks.2.refs_0_), channel_id=1, source_target_pairs={{0,24},{4,28},{8,16},{12,20},{16,8},{20,12},{24,0},{28,4},{1,25},{... | collective-permute-start | bytes 743432 | tf_op jit(solution)/shard_map/ppermute | solution.py:681
  65.8 14.8 %collective-permute-start.24 = (bf16[4,8,3872]{2,1,0:T(8,128)(2,1)}, bf16[4,8,3872]{2,1,0:T(8,128)(2,1)S(1)}, u32[]{:S(2)}, u32[]{:S(2)}) collective-permute-start(bf16[4,8,3872]{2,1,0:T(8,128)(2,1)} %get-tuple-element.93), channel_id=1, source_target_pairs={{0,1},{1,0},{2,3},{3,2},{4,5},{5,4},{6,7},{7,6},{8,9},{9,8},{10,11... | collective-permute-start | bytes 743432 | tf_op jit(solution)/shard_map/ppermute | solution.py:22
  68.6 12.0 %collective-permute-start.25 = (bf16[4,8,3872]{2,1,0:T(8,128)(2,1)}, bf16[4,8,3872]{2,1,0:T(8,128)(2,1)S(1)}, u32[]{:S(2)}, u32[]{:S(2)}) collective-permute-start(bf16[4,8,3872]{2,1,0:T(8,128)(2,1)} %get-tuple-element.94), channel_id=1, source_target_pairs={{0,2},{1,3},{2,0},{3,1},{4,6},{5,7},{6,4},{7,5},{8,10},{9,11},{10,... | collective-permute-start | bytes 743432 | tf_op jit(solution)/shard_map/ppermute | solution.py:22
  69.5 21.0 %collective-permute-start.26 = (bf16[4,8,3872]{2,1,0:T(8,128)(2,1)}, bf16[4,8,3872]{2,1,0:T(8,128)(2,1)S(1)}, u32[]{:S(2)}, u32[]{:S(2)}) collective-permute-start(bf16[4,8,3872]{2,1,0:T(8,128)(2,1)} %get-tuple-element.95), channel_id=1, source_target_pairs={{0,3},{1,2},{2,1},{3,0},{4,7},{5,6},{6,5},{7,4},{8,11},{9,10},{10,... | collective-permute-start | bytes 743432 | tf_op jit(solution)/shard_map/ppermute | solution.py:22
  76.6 20.1 %collective-permute-start.20 = (bf16[128,3872]{0,1:T(8,128)(2,1)}, bf16[128,3872]{0,1:T(8,128)(2,1)}, u32[]{:S(2)}, u32[]{:S(2)}) collective-permute-start(bf16[128,3872]{0,1:T(8,128)(2,1)} %copy.48), channel_id=1, source_target_pairs={{0,4},{4,0},{8,12},{12,8},{16,20},{20,16},{24,28},{28,24},{1,5},{5... | collective-permute-start | bytes 2973704 | tf_op jit(solution)/shard_map/ppermute | solution.py:686
  92.7 35.5 %collective-permute-start.28 = (bf16[4,8,3872]{2,1,0:T(8,128)(2,1)}, bf16[4,8,3872]{2,1,0:T(8,128)(2,1)S(1)}, u32[]{:S(2)}, u32[]{:S(2)}) collective-permute-start(bf16[4,8,3872]{2,1,0:T(8,128)(2,1)} %get-tuple-element.134), channel_id=1, source_target_pairs={{0,1},{1,0},{2,3},{3,2},{4,5},{5,4},{6,7},{7,6},{8,9},{9,8},{10,11... | collective-permute-start | bytes 743432 | tf_op jit(solution)/shard_map/ppermute | solution.py:22
  92.7 36.4 %collective-permute-start.29 = (bf16[4,8,3872]{2,1,0:T(8,128)(2,1)}, bf16[4,8,3872]{2,1,0:T(8,128)(2,1)S(1)}, u32[]{:S(2)}, u32[]{:S(2)}) collective-permute-start(bf16[4,8,3872]{2,1,0:T(8,128)(2,1)} %get-tuple-element.133), channel_id=1, source_target_pairs={{0,2},{1,3},{2,0},{3,1},{4,6},{5,7},{6,4},{7,5},{8,10},{9,11},{10,... | collective-permute-start | bytes 743432 | tf_op jit(solution)/shard_map/ppermute | solution.py:22
  93.6 35.5 %collective-permute-start.30 = (bf16[4,8,3872]{2,1,0:T(8,128)(2,1)S(1)}, bf16[4,8,3872]{2,1,0:T(8,128)(2,1)S(1)}, u32[]{:S(2)}, u32[]{:S(2)}) collective-permute-start(bf16[4,8,3872]{2,1,0:T(8,128)(2,1)S(1)} %get-tuple-element.132), channel_id=1, source_target_pairs={{0,3},{1,2},{2,1},{3,0},{4,7},{5,6},{6,5},{7,4},{8,11},{9,10},{10,... | collective-permute-start | bytes 743432 | tf_op jit(solution)/shard_map/ppermute | solution.py:22
  96.0 36.3 %collective-permute-start.31 = (bf16[32,3872]{1,0:T(8,128)(2,1)S(1)}, bf16[32,3872]{1,0:T(8,128)(2,1)S(1)}, u32[]{:S(2)}, u32[]{:S(2)}) collective-permute-start(bf16[32,3872]{1,0:T(8,128)(2,1)S(1)} %get-tuple-element.108), channel_id=1, source_target_pairs={{0,8},{4,12},{8,0},{12,4},{16,24},{20,28},{24,16},{28,20},{1,9},{5... | collective-permute-start | bytes 743432 | tf_op jit(solution)/shard_map/ppermute | solution.py:681
  96.7 36.5 %collective-permute-start.33 = (bf16[32,3872]{1,0:T(8,128)(2,1)S(1)}, bf16[32,3872]{1,0:T(8,128)(2,1)}, u32[]{:S(2)}, u32[]{:S(2)}) collective-permute-start(bf16[32,3872]{1,0:T(8,128)(2,1)S(1)} %get-tuple-element.110), channel_id=1, source_target_pairs={{0,16},{4,20},{8,24},{12,28},{16,0},{20,4},{24,8},{28,12},{1,17},{... | collective-permute-start | bytes 743432 | tf_op jit(solution)/shard_map/ppermute | solution.py:681
  128.2 6.2 %collective-permute-start.35 = (bf16[32,3872]{1,0:T(8,128)(2,1)S(1)}, bf16[32,3872]{1,0:T(8,128)(2,1)S(1)}, u32[]{:S(2)}, u32[]{:S(2)}) collective-permute-start(bf16[32,3872]{1,0:T(8,128)(2,1)S(1)} %get-tuple-element.112), channel_id=1, source_target_pairs={{0,24},{4,28},{8,16},{12,20},{16,8},{20,12},{24,0},{28,4},{1,25},{... | collective-permute-start | bytes 743432 | tf_op jit(solution)/shard_map/ppermute | solution.py:681
  130.5 5.7 %collective-permute-start.32 = (bf16[32,3872]{1,0:T(8,128)(2,1)S(1)}, bf16[32,3872]{1,0:T(8,128)(2,1)S(1)}, u32[]{:S(2)}, u32[]{:S(2)}) collective-permute-start(bf16[32,3872]{1,0:T(8,128)(2,1)S(1)} %get-tuple-element.109), channel_id=1, source_target_pairs={{0,8},{4,12},{8,0},{12,4},{16,24},{20,28},{24,16},{28,20},{1,9},{5... | collective-permute-start | bytes 743432 | tf_op jit(solution)/shard_map/ppermute | solution.py:681
  131.1 6.0 %collective-permute-start.34 = (bf16[32,3872]{1,0:T(8,128)(2,1)S(1)}, bf16[32,3872]{1,0:T(8,128)(2,1)S(1)}, u32[]{:S(2)}, u32[]{:S(2)}) collective-permute-start(bf16[32,3872]{1,0:T(8,128)(2,1)S(1)} %get-tuple-element.111), channel_id=1, source_target_pairs={{0,16},{4,20},{8,24},{12,28},{16,0},{20,4},{24,8},{28,12},{1,17},{... | collective-permute-start | bytes 743432 | tf_op jit(solution)/shard_map/ppermute | solution.py:681
  132.3 10.5 %collective-permute-start.36 = (bf16[32,3872]{1,0:T(8,128)(2,1)S(1)}, bf16[32,3872]{1,0:T(8,128)(2,1)S(1)}, u32[]{:S(2)}, u32[]{:S(2)}) collective-permute-start(bf16[32,3872]{1,0:T(8,128)(2,1)S(1)} %get-tuple-element.113), channel_id=1, source_target_pairs={{0,24},{4,28},{8,16},{12,20},{16,8},{20,12},{24,0},{28,4},{1,25},{... | collective-permute-start | bytes 743432 | tf_op jit(solution)/shard_map/ppermute | solution.py:681
  133.1 20.6 %collective-permute-start.21 = (bf16[4,88,256]{2,1,0:T(8,128)(2,1)}, bf16[4,88,256]{2,1,0:T(8,128)(2,1)S(1)}, u32[]{:S(2)}, u32[]{:S(2)}) collective-permute-start(bf16[4,88,256]{2,1,0:T(8,128)(2,1)} %get-tuple-element.89), channel_id=1, source_target_pairs={{0,1},{1,0},{2,3},{3,2},{4,5},{5,4},{6,7},{7,6},{8,9},{9,8},{10,11... | collective-permute-start | bytes 540680 | tf_op jit(solution)/shard_map/ppermute | solution.py:22
  134.4 19.3 %collective-permute-start.22 = (bf16[4,88,256]{2,1,0:T(8,128)(2,1)}, bf16[4,88,256]{2,1,0:T(8,128)(2,1)S(1)}, u32[]{:S(2)}, u32[]{:S(2)}) collective-permute-start(bf16[4,88,256]{2,1,0:T(8,128)(2,1)} %get-tuple-element.90), channel_id=1, source_target_pairs={{0,2},{1,3},{2,0},{3,1},{4,6},{5,7},{6,4},{7,5},{8,10},{9,11},{10,... | collective-permute-start | bytes 540680 | tf_op jit(solution)/shard_map/ppermute | solution.py:22
  136.1 17.6 %collective-permute-start.23 = (bf16[4,88,256]{2,1,0:T(8,128)(2,1)}, bf16[4,88,256]{2,1,0:T(8,128)(2,1)S(1)}, u32[]{:S(2)}, u32[]{:S(2)}) collective-permute-start(bf16[4,88,256]{2,1,0:T(8,128)(2,1)} %get-tuple-element.91), channel_id=1, source_target_pairs={{0,3},{1,2},{2,1},{3,0},{4,7},{5,6},{6,5},{7,4},{8,11},{9,10},{10,... | collective-permute-start | bytes 540680 | tf_op jit(solution)/shard_map/ppermute | solution.py:22
  143.4 55.0 %copy-start.16 = (bf16[128,128]{1,0:T(8,128)(2,1)S(1)}, bf16[128,128]{1,0:T(8,128)(2,1)}, u32[]{:S(2)}) copy-start(bf16[128,128]{1,0:T(8,128)(2,1)} %refs_11_.1) | copy-start | bytes 98308
  153.7 5.6 %collective-permute-start.37 = (bf16[8,4,3872]{2,1,0:T(4,128)(2,1)}, bf16[8,4,3872]{2,1,0:T(4,128)(2,1)S(1)}, u32[]{:S(2)}, u32[]{:S(2)}) collective-permute-start(bf16[8,4,3872]{2,1,0:T(4,128)(2,1)} %get-tuple-element.119), channel_id=1, source_target_pairs={{0,1},{1,0},{2,3},{3,2},{4,5},{5,4},{6,7},{7,6},{8,9},{9,8},{10,11... | collective-permute-start | bytes 743432 | tf_op jit(solution)/shard_map/ppermute | solution.py:22
  154.7 6.7 %collective-permute-start.38 = (bf16[8,4,3872]{2,1,0:T(4,128)(2,1)}, bf16[8,4,3872]{2,1,0:T(4,128)(2,1)S(1)}, u32[]{:S(2)}, u32[]{:S(2)}) collective-permute-start(bf16[8,4,3872]{2,1,0:T(4,128)(2,1)} %get-tuple-element.120), channel_id=1, source_target_pairs={{0,2},{1,3},{2,0},{3,1},{4,6},{5,7},{6,4},{7,5},{8,10},{9,11},{10,... | collective-permute-start | bytes 743432 | tf_op jit(solution)/shard_map/ppermute | solution.py:22
  154.8 23.0 %collective-permute-start.39 = (bf16[8,4,3872]{2,1,0:T(4,128)(2,1)}, bf16[8,4,3872]{2,1,0:T(4,128)(2,1)S(1)}, u32[]{:S(2)}, u32[]{:S(2)}) collective-permute-start(bf16[8,4,3872]{2,1,0:T(4,128)(2,1)} %get-tuple-element.121), channel_id=1, source_target_pairs={{0,3},{1,2},{2,1},{3,0},{4,7},{5,6},{6,5},{7,4},{8,11},{9,10},{10,... | collective-permute-start | bytes 743432 | tf_op jit(solution)/shard_map/ppermute | solution.py:22
  180.8 5.8 %collective-permute-start.40 = (bf16[16,3872]{1,0:T(8,128)(2,1)S(1)}, bf16[16,3872]{1,0:T(8,128)(2,1)S(1)}, u32[]{:S(2)}, u32[]{:S(2)}) collective-permute-start(bf16[16,3872]{1,0:T(8,128)(2,1)S(1)} %get-tuple-element.123), channel_id=1, source_target_pairs={{0,4},{4,0},{8,12},{12,8},{16,20},{20,16},{24,28},{28,24},{1,5},{5... | collective-permute-start | bytes 371720 | tf_op jit(solution)/shard_map/ppermute | solution.py:22
  183.1 5.3 %collective-permute-start.41 = (bf16[16,3872]{1,0:T(8,128)(2,1)S(1)}, bf16[16,3872]{1,0:T(8,128)(2,1)S(1)}, u32[]{:S(2)}, u32[]{:S(2)}) collective-permute-start(bf16[16,3872]{1,0:T(8,128)(2,1)S(1)} %get-tuple-element.124), channel_id=1, source_target_pairs={{0,8},{4,12},{8,0},{12,4},{16,24},{20,28},{24,16},{28,20},{1,9},{5... | collective-permute-start | bytes 371720 | tf_op jit(solution)/shard_map/ppermute | solution.py:22
  184.4 9.2 %collective-permute-start.42 = (bf16[16,3872]{1,0:T(8,128)(2,1)}, bf16[16,3872]{1,0:T(8,128)(2,1)}, u32[]{:S(2)}, u32[]{:S(2)}) collective-permute-start(bf16[16,3872]{1,0:T(8,128)(2,1)} %get-tuple-element.125), channel_id=1, source_target_pairs={{0,12},{4,8},{8,4},{12,0},{16,28},{20,24},{24,20},{28,16},{1,13},{... | collective-permute-start | bytes 371720 | tf_op jit(solution)/shard_map/ppermute | solution.py:22
  184.8 8.8 %collective-permute-start.43 = (bf16[16,3872]{1,0:T(8,128)(2,1)}, bf16[16,3872]{1,0:T(8,128)(2,1)}, u32[]{:S(2)}, u32[]{:S(2)}) collective-permute-start(bf16[16,3872]{1,0:T(8,128)(2,1)} %get-tuple-element.126), channel_id=1, source_target_pairs={{0,16},{4,20},{8,24},{12,28},{16,0},{20,4},{24,8},{28,12},{1,17},{... | collective-permute-start | bytes 371720 | tf_op jit(solution)/shard_map/ppermute | solution.py:22
  185.0 13.4 %collective-permute-start.44 = (bf16[16,3872]{1,0:T(8,128)(2,1)}, bf16[16,3872]{1,0:T(8,128)(2,1)}, u32[]{:S(2)}, u32[]{:S(2)}) collective-permute-start(bf16[16,3872]{1,0:T(8,128)(2,1)} %get-tuple-element.127), channel_id=1, source_target_pairs={{0,20},{4,16},{8,28},{12,24},{16,4},{20,0},{24,12},{28,8},{1,21},{... | collective-permute-start | bytes 371720 | tf_op jit(solution)/shard_map/ppermute | solution.py:22
  187.3 11.1 %collective-permute-start.45 = (bf16[16,3872]{1,0:T(8,128)(2,1)}, bf16[16,3872]{1,0:T(8,128)(2,1)}, u32[]{:S(2)}, u32[]{:S(2)}) collective-permute-start(bf16[16,3872]{1,0:T(8,128)(2,1)} %get-tuple-element.128), channel_id=1, source_target_pairs={{0,24},{4,28},{8,16},{12,20},{16,8},{20,12},{24,0},{28,4},{1,25},{... | collective-permute-start | bytes 371720 | tf_op jit(solution)/shard_map/ppermute | solution.py:22
  189.1 9.3 %collective-permute-start.46 = (bf16[16,3872]{1,0:T(8,128)(2,1)}, bf16[16,3872]{1,0:T(8,128)(2,1)}, u32[]{:S(2)}, u32[]{:S(2)}) collective-permute-start(bf16[16,3872]{1,0:T(8,128)(2,1)} %get-tuple-element.129), channel_id=1, source_target_pairs={{0,28},{4,24},{8,20},{12,16},{16,12},{20,8},{24,4},{28,0},{1,29},{... | collective-permute-start | bytes 371720 | tf_op jit(solution)/shard_map/ppermute | solution.py:22
  (40 other events, 535.9 us)

commit v3 on v2

--- a/solution.py
+++ b/solution.py
@@ -150,10 +150,10 @@
     cols_in = refs[3:5]
     pair_ref, place_ref, exit_ref, near_ref, open_ref, score_ref, live_ref = refs[5:12]
     outs = refs[12:]
-    z_ref, high_ref, bias_ref = outs[:3]
-    side_refs = outs[3 : 3 + total_cols]
-    given_ref = outs[3 + total_cols]
-    left, right, prod, counts, low = outs[4 + total_cols :]
+    z_ref, high_ref = outs[:2]
+    side_refs = outs[2 : 2 + total_cols]
+    given_ref = outs[2 + total_cols]
+    left, right, prod, counts, low = outs[3 + total_cols :]
     step = pl.program_id(0)
     group, places, width = pair_ref.shape
     seqs = rows_in[0].shape[1]
@@ -236,7 +236,6 @@
         transposed = (((1,), (1,)), ((), ()))
         half_rows = open_ref.shape[0] // 2
         each = half_rows // total_cols // 2
-        count = each // chips
         for first in range(0, pairs, chunk):
             last = min(first + chunk, pairs)
             ours = high_ref[first:last, :]
@@ -245,7 +244,6 @@
             ) + lax.dot_general(
                 score_ref[...], low[first:last, :], transposed, preferred_element_type=jnp.float32
             )
-            bias_ref[:, first:last] = bias[: bias_ref.shape[0]].astype(bf16)
             opened = lax.dot_general(
                 open_ref[...], ours, transposed, preferred_element_type=jnp.float32
             )
@@ -253,11 +251,12 @@
                 jax.nn.sigmoid(opened[half_rows:]) * opened[:half_rows] * live_ref[:, first:last]
             )
             for m in range(total_cols):
-                for r in range(chips):
-                    at = m * each + r * count
-                    side_refs[m][r, :, first:last] = sides[at : at + count].astype(bf16)
-                    at = (total_cols + m) * each + r * count
-                    given_ref[m, r, :, first:last] = sides[at : at + count].astype(bf16)
+                at = m * each
+                side_refs[m][:, first:last] = jnp.concatenate(
+                    [sides[at : at + each], bias], axis=0
+                ).astype(bf16)
+                at = (total_cols + m) * each
+                given_ref[m, :, first:last] = sides[at : at + each].astype(bf16)
 
 
 def pair_stage(rows_in, cols_in, pair, spots, place, exit_t, near_t, open_t, score_t, live, total_rows, total_cols):
@@ -268,7 +267,7 @@
     group = tile_rows // blocks
     opm = cols_in[0].shape[0] // chips - 1
     pairs = tile_rows * places
-    count = open_t.shape[0] // 2 // total_cols // total_rows
+    each = open_t.shape[0] // 4 // total_cols
     every = total_rows * seqs
 
     def whole(a):
@@ -283,9 +282,8 @@
     outs = [
         jax.ShapeDtypeStruct((pairs, width), jnp.float32),
         jax.ShapeDtypeStruct((pairs, width), bf16),
-        jax.ShapeDtypeStruct((score_t.shape[0], pairs), bf16),
-    ] + [jax.ShapeDtypeStruct((chips, count, pairs), bf16)] * total_cols
-    outs.append(jax.ShapeDtypeStruct((total_cols, chips, count, pairs), bf16))
+    ] + [jax.ShapeDtypeStruct((each + score_t.shape[0], pairs), bf16)] * total_cols
+    outs.append(jax.ShapeDtypeStruct((total_cols, each, pairs), bf16))
     return pl.pallas_call(
         functools.partial(pair_kernel, total_rows, total_cols),
         grid=(blocks,),
@@ -305,9 +303,6 @@
         ],
         compiler_params=pltpu.CompilerParams(
             vmem_limit_bytes=56 << 20, dimension_semantics=("arbitrary",)
-        ),
-        cost_estimate=pl.CostEstimate(
-            flops=20 * 10**9, bytes_accessed=16 * 10**6, transcendentals=10**6
         ),
         name="pair_update",
     )(spots, *ins, pair, *rest)
@@ -349,26 +344,50 @@
     lax.fori_loop(0, total, one, 0)
 
 
-def attention_kernel(halves, total_cols, *refs):
+def layout_kernel(halves, total_cols, places, *refs):
     base_ref = refs[0]
-    bias_in = refs[1 : 1 + halves]
-    x_in = refs[1 + halves : 1 + halves + total_cols]
-    mark_ref, project_ref, mix_ref = refs[1 + halves + total_cols : 4 + halves + total_cols]
-    outs = refs[4 + halves + total_cols : 4 + halves + 2 * total_cols]
-    stack, tiles, mixed = refs[4 + halves + 2 * total_cols :]
+    out_ref, stack, tiles = refs[1 + halves :]
+    spread_slots(refs[1 : 1 + halves], stack, base_ref, tiles, total_cols, places)
+    out_ref[...] = tiles[...].astype(out_ref.dtype)
+
+
+def layout_bias(base, bias_slots, total_cols, places):
+    total_rows = base.shape[0]
+    rows, pairs = bias_slots[0].shape
+    rows = rows * len(bias_slots) // total_rows
+    residues = places * total_cols
+    heads = rows // total_cols
+    shape = (-(-residues // 128), heads * residues, 128)
+    wide = -(-pairs // 128) * 128 + 128
+    return pl.pallas_call(
+        functools.partial(layout_kernel, len(bias_slots), total_cols, places),
+        in_specs=[pl.BlockSpec(memory_space=pltpu.SMEM)]
+        + [pl.BlockSpec(memory_space=pltpu.VMEM)] * len(bias_slots),
+        out_specs=pl.BlockSpec(memory_space=pltpu.VMEM),
+        out_shape=jax.ShapeDtypeStruct(shape, jnp.bfloat16),
+        scratch_shapes=[
+            pltpu.VMEM((total_rows, rows, wide), jnp.bfloat16),
+            pltpu.VMEM(shape, jnp.float32),
+        ],
+        compiler_params=pltpu.CompilerParams(vmem_limit_bytes=48 << 20),
+        name="layout_bias",
+    )(base, *bias_slots)
+
+
+def attention_kernel(total_cols, heads, *refs):
+    bias_ref = refs[0]
+    x_in = refs[1 : 1 + total_cols]
+    mark_ref, project_ref, mix_ref = refs[1 + total_cols : 4 + total_cols]
+    outs = refs[4 + total_cols : 4 + 2 * total_cols]
+    scored, termed, summed, mixed = refs[4 + 2 * total_cols :]
     places, width = x_in[0].shape[1:]
     residues = places * total_cols
-    heads = stack.shape[1] // total_cols
     each = width // heads
     group = 128 // each
-    padded = tiles.shape[0] * 128
+    padded = bias_ref.shape[0] * 128
     bf16 = jnp.bfloat16
     transposed = (((1,), (1,)), ((), ()))
-    chunk = 176
-
-    @pl.when(pl.program_id(0) == 0)
-    def _():
-        spread_slots(bias_in, stack, base_ref, tiles, total_cols, places)
+    chunk = 32
 
     x = jnp.concatenate([r[0].astype(jnp.float32) for r in x_in], axis=0)
     made = jnp.dot(
@@ -378,48 +397,54 @@
     lane = lax.broadcasted_iota(jnp.int32, (1, 128), 1)
     scale = 1.0 / math.sqrt(each)
     filler = jnp.zeros((padded - residues, 128), bf16)
-    for h0 in range(0, heads, group):
-        at = h0 * each
-        queries = made[:, at : at + 128].astype(bf16)
-        keys = made[:, width + at : width + at + 128].astype(bf16)
-        values = made[:, 2 * width + at : 2 * width + at + 128].astype(bf16)
-        keys = jnp.concatenate([keys, filler], axis=0)
-        values = jnp.concatenate([values, filler], axis=0)
+
+    def head_columns(part, h):
+        at = part * width + h // group * 128
+        return made[:, at : at + 128].astype(bf16)
+
+    def only(block, h):
+        inside = (lane >= h % group * each) & (lane < (h % group + 1) * each)
+        return jnp.concatenate([jnp.where(inside, block, jnp.zeros_like(block)), filler], axis=0)
+
+    def score(h):
+        scored[h % 2] = lax.dot_general(
+            head_columns(0, h), only(head_columns(1, h), h), transposed,
+            preferred_element_type=jnp.float32,
+        )
+
+    score(0)
+    for h in range(heads):
+        if h + 1 < heads:
+            score(h + 1)
         for first in range(0, residues, chunk):
-            total = jnp.zeros((chunk, 128), jnp.float32)
-            for h in range(group):
-                ours = (lane >= h * each) & (lane < (h + 1) * each)
-                own_keys = jnp.where(ours, keys, jnp.zeros_like(keys))
-                own_values = jnp.where(ours, values, jnp.zeros_like(values))
-                scores = lax.dot_general(
-                    queries[first : first + chunk], own_keys, transposed,
-                    preferred_element_type=jnp.float32,
-                )
-                start = (h0 + h) * residues + first
-                bias = jnp.concatenate(
-                    [tiles[t, start : start + chunk, :] for t in range(tiles.shape[0])], axis=1
-                )
-                scores = jnp.where(present, scores * scale + bias, masked_score)
-                terms = jnp.exp(scores - jnp.max(scores, axis=1, keepdims=True))
-                weight = jnp.sum(terms, axis=1, keepdims=True)
-                got = jnp.dot(terms.astype(bf16), own_values, preferred_element_type=jnp.float32)
-                total = total + got / weight
-            gate = jax.nn.sigmoid(made[first : first + chunk, 3 * width + at : 3 * width + at + 128])
-            mixed[first : first + chunk, at : at + 128] = (gate * total).astype(bf16)
+            start = h * residues + first
+            bias = jnp.concatenate(
+                [bias_ref[t, start : start + chunk, :] for t in range(bias_ref.shape[0])], axis=1
+            )
+            scores = scored[h % 2, first : first + chunk, :] * scale + bias.astype(jnp.float32)
+            scores = jnp.where(present, scores, masked_score)
+            terms = jnp.exp(scores - jnp.max(scores, axis=1, keepdims=True))
+            weight = jnp.sum(terms, axis=1, keepdims=True)
+            termed[h % 2, first : first + chunk, :] = terms.astype(bf16)
+            summed[h % 2, first : first + chunk, :] = jnp.broadcast_to(1.0 / weight, (chunk, 128))
+        got = jnp.dot(
+            termed[h % 2], only(head_columns(2, h), h), preferred_element_type=jnp.float32
+        ) * summed[h % 2]
+        total = got if h % group == 0 else total + got
+        if h % group == group - 1:
+            at = h // group * 128
+            gate = jax.nn.sigmoid(made[:, 3 * width + at : 3 * width + at + 128])
+            mixed[:, at : at + 128] = (gate * total).astype(bf16)
     after = x + jnp.dot(mixed[...], mix_ref[...], preferred_element_type=jnp.float32)
     for m in range(total_cols):
         outs[m][0] = after[m * places : (m + 1) * places].astype(bf16)
 
 
-def attend(base, bias_slots, x_slots, marks, project, mix):
-    total_rows, total_cols = base.shape[0], len(x_slots)
+def attend(bias, heads, x_slots, marks, project, mix):
+    total_cols = len(x_slots)
     seqs, places, width = x_slots[0].shape
     residues = places * total_cols
-    padded = -(-residues // 128) * 128
-    rows, pairs = bias_slots[0].shape
-    rows = rows * len(bias_slots) // total_rows
-    heads = rows // total_cols
-    wide = -(-pairs // 128) * 128 + 128
+    padded = bias.shape[0] * 128
 
     def whole(a):
         return pl.BlockSpec(a.shape, lambda s, n=a.ndim: (0,) * n)
@@ -427,48 +452,48 @@
     per_seq = pl.BlockSpec((1, places, width), lambda s: (s, 0, 0))
     bf16 = jnp.bfloat16
     return pl.pallas_call(
-        functools.partial(attention_kernel, len(bias_slots), total_cols),
+        functools.partial(attention_kernel, total_cols, heads),
         grid=(seqs,),
-        in_specs=[pl.BlockSpec(memory_space=pltpu.SMEM)]
-        + [whole(a) for a in bias_slots]
+        in_specs=[whole(bias)]
         + [per_seq] * total_cols
         + [pl.BlockSpec((1, 1, padded), lambda s: (s, 0, 0)), whole(project), whole(mix)],
         out_specs=[per_seq] * total_cols,
         out_shape=[jax.ShapeDtypeStruct((seqs, places, width), bf16)] * total_cols,
         scratch_shapes=[
-            pltpu.VMEM((total_rows, rows, wide), bf16),
-            pltpu.VMEM((padded // 128, heads * residues, 128), jnp.float32),
+            pltpu.VMEM((2, residues, padded), jnp.float32),
+            pltpu.VMEM((2, residues, padded), bf16),
+            pltpu.VMEM((2, residues, 128), jnp.float32),
             pltpu.VMEM((residues, width), bf16),
         ],
         compiler_params=pltpu.CompilerParams(
-            vmem_limit_bytes=56 << 20, dimension_semantics=("arbitrary",)
-        ),
-        cost_estimate=pl.CostEstimate(
-            flops=40 * 10**9, bytes_accessed=30 * 10**6, transcendentals=4 * 10**6
+            vmem_limit_bytes=48 << 20, dimension_semantics=("arbitrary",)
         ),
         name="row_attention",
-    )(base, *bias_slots, *x_slots, marks, project, mix)
-
-
-def regroup_kernel(ahead, lead_ref, *refs):
-    total_in = len(refs) - ahead
-    for k in range(ahead):
-        lead = lead_ref[k]
-        parts = [refs[m][lead].astype(jnp.float32) for m in range(total_in)]
-        refs[total_in + k][...] = jnp.concatenate(parts, axis=0).astype(jnp.bfloat16)
-
-
-def regroup(lead, slots):
-    total_out, count, pairs = slots[0].shape
+    )(bias, *x_slots, marks, project, mix)
+
+
+def regroup_kernel(plan, total_in, *refs):
+    for out, parts in zip(refs[total_in:], plan):
+        rows = [
+            refs[n][at] if refs[n].ndim == 3 else refs[n][at : at + count]
+            for n, at, count in parts
+        ]
+        out[...] = jnp.concatenate([r.astype(jnp.float32) for r in rows], axis=0).astype(out.dtype)
+
+
+def regroup(blocks, plan):
+    pairs = blocks[0].shape[-1]
     return pl.pallas_call(
-        functools.partial(regroup_kernel, total_out),
-        in_specs=[pl.BlockSpec(memory_space=pltpu.SMEM)]
-        + [pl.BlockSpec(memory_space=pltpu.VMEM)] * len(slots),
-        out_specs=[pl.BlockSpec(memory_space=pltpu.VMEM)] * total_out,
-        out_shape=[jax.ShapeDtypeStruct((len(slots) * count, pairs), jnp.bfloat16)] * total_out,
+        functools.partial(regroup_kernel, plan, len(blocks)),
+        in_specs=[pl.BlockSpec(memory_space=pltpu.VMEM)] * len(blocks),
+        out_specs=[pl.BlockSpec(memory_space=pltpu.VMEM)] * len(plan),
+        out_shape=[
+            jax.ShapeDtypeStruct((sum(count for _, _, count in parts), pairs), jnp.bfloat16)
+            for parts in plan
+        ],
         compiler_params=pltpu.CompilerParams(vmem_limit_bytes=40 << 20),
         name="regroup",
-    )(lead, *slots)
+    )(*blocks)
 
 
 def stack_kernel(*refs):
@@ -490,10 +515,10 @@
 def triangle_kernel(total_rows, total_cols, *refs):
     base_ref = refs[0]
     slots = refs[1 : 1 + total_rows]
-    outs = refs[1 + total_rows : 1 + total_rows + total_cols]
-    stack, tiles, crossed = refs[1 + total_rows + total_cols :]
-    pairs = outs[0].shape[2]
-    share = outs[0].shape[1]
+    kept = refs[1 + total_rows : 1 + total_rows + total_cols]
+    given, stack, tiles, crossed = refs[1 + total_rows + total_cols :]
+    pairs = kept[0].shape[2]
+    share = kept[0].shape[1]
     residues = tiles.shape[1] // (2 * share)
     rows = residues // total_rows
     places = residues // total_cols
@@ -516,8 +541,13 @@
             crossed[t, c * residues : (c + 1) * residues, :last] = got[:, t * 128 : t * 128 + last]
     lane = lax.broadcasted_iota(jnp.int32, (share, 128), 1)
 
-    def one(k, carry):
-        base = base_ref[k]
+    def one(j, carry):
+        for h in range(2):
+            outs = [given.at[m] if h else kept[m] for m in range(total_cols)]
+            rows_out(j, base_ref[2 * j + h], outs)
+        return carry
+
+    def rows_out(k, base, outs):
         made = [dict() for _ in range(total_cols)]
         for i in range(rows):
             row = [
@@ -543,14 +573,13 @@
                     if i == rows - 1 and to + 1 in made[m]:
                         size = pairs - (to + 1) * 128
                         outs[m][k, :, (to + 1) * 128 : pairs] = made[m].pop(to + 1)[:, :size].astype(bf16)
-        return carry
-
-    lax.fori_loop(0, total_rows, one, 0)
+
+    lax.fori_loop(0, total_rows // 2, one, 0)
 
 
 def triangle(base, slots, share, total_cols, residues):
     total_rows = len(slots)
-    rows, pairs = slots[0].shape
+    rows, pairs = slots[1].shape
     padded = -(-residues // 128)
     wide = -(-pairs // 128) * 128 + 128
     bf16 = jnp.bfloat16
@@ -558,25 +587,25 @@
         functools.partial(triangle_kernel, total_rows, total_cols),
         in_specs=[pl.BlockSpec(memory_space=pltpu.SMEM)]
         + [pl.BlockSpec(memory_space=pltpu.VMEM)] * total_rows,
-        out_specs=[pl.BlockSpec(memory_space=pltpu.VMEM)] * total_cols,
-        out_shape=[jax.ShapeDtypeStruct((total_rows, share, pairs), bf16)] * total_cols,
+        out_specs=[pl.BlockSpec(memory_space=pltpu.VMEM)] * (total_cols + 1),
+        out_shape=[jax.ShapeDtypeStruct((total_rows // 2, share, pairs), bf16)] * total_cols
+        + [jax.ShapeDtypeStruct((total_cols, total_rows // 2, share, pairs), bf16)],
         scratch_shapes=[
             pltpu.VMEM((total_rows, rows, wide), bf16),
             pltpu.VMEM((padded, 2 * share * residues, 128), jnp.float32),
             pltpu.VMEM((padded, share * residues, 128), jnp.float32),
         ],
         compiler_params=pltpu.CompilerParams(vmem_limit_bytes=56 << 20),
-        cost_estimate=pl.CostEstimate(
-            flops=10 * 10**9, bytes_accessed=8 * 10**6, transcendentals=0
-        ),
         name="triangle",
     )(base, *slots)
 
 
 def finish_kernel(total_rows, *refs):
     lead_ref = refs[0]
-    slots = refs[1 : 1 + total_rows]
-    high_ref, z_ref, valve_ref, exit_ref, out_ref = refs[1 + total_rows :]
+    chips = total_rows // 2
+    high_ref, z_ref, valve_ref, exit_ref, out_ref = refs[1 + chips :]
+    count = refs[1].shape[0] // 2
+    slots = [refs[1 + k // 2].at[k % 2 * count : (k % 2 + 1) * count] for k in range(total_rows)]
     pairs = out_ref.shape[0]
     chunk = 512
     exits = jnp.concatenate(
@@ -601,7 +630,7 @@
 
 def finish(lead, slots, high, z_one, valve, exit_w):
     return pl.pallas_call(
-        functools.partial(finish_kernel, len(slots)),
+        functools.partial(finish_kernel, 2 * len(slots)),
         in_specs=[pl.BlockSpec(memory_space=pltpu.SMEM)]
         + [pl.BlockSpec(memory_space=pltpu.VMEM)] * (len(slots) + 4),
         out_specs=pl.BlockSpec(memory_space=pltpu.VMEM),
@@ -703,8 +732,6 @@
     left_odd = other_core(left_even)
     operands = [left_even, left_odd, right_even, right_odd]
 
-    operands, x_own = lax.optimization_barrier((operands, homolog_activations))
-    x_slots = exchange(x_own.reshape(col_total, own_seqs, block_columns, -1), "col")
     own_marks = lax.dynamic_slice_in_dim(left_stack[:, -1], col_place * own_seqs, own_seqs, 1)
     own_marks = jnp.swapaxes(own_marks[:, :, :block_columns], 0, 1).reshape(own_seqs, 1, residues)
     padded = -(-residues // 128) * 128
@@ -742,46 +769,74 @@
     )
     open_t = jnp.concatenate(
         [lax.dynamic_slice_in_dim(open_t, col_place ^ m, 1, 2) for m in range(col_total)], axis=2
+    )
+    open_t = jnp.concatenate(
+        [lax.dynamic_slice_in_dim(open_t, row_place // 2 ^ j, 1, 3) for j in range(row_total // 2)],
+        axis=3,
     ).reshape(4 * tri_width, pair_width)
     score_t = coupling_score_mapping.T
     live_rows = lax.dynamic_slice_in_dim(observed_peptide_marks, row_first, tile_rows)
     live_cols = lax.dynamic_slice_in_dim(observed_peptide_marks, col_first, block_columns)
     live = (live_rows[:, None] * live_cols[None, :]).astype(jnp.float32).reshape(1, -1)
-    z_one, ln_tri, bias_flat, *kept, given = pair_stage(
+    operands, x_own = lax.optimization_barrier((operands, homolog_activations))
+    x_slots = exchange(x_own.reshape(col_total, own_seqs, block_columns, -1), "col")
+    z_one, ln_tri, *kept, given = pair_stage(
         operands[:2], operands[2:], coupling_activations, spots, place, exit_t, near_t, open_t,
         score_t, live, row_total, col_total,
     )
-    bias_flat, x_slots = lax.optimization_barrier((bias_flat, x_slots))
+
+    given, x_slots = lax.optimization_barrier((given, x_slots))
 
     row_ids = row_place ^ jnp.arange(row_total, dtype=jnp.int32)
     col_ids = col_place ^ jnp.arange(col_total, dtype=jnp.int32)
     base = (row_ids // group_ratio ^ col_place) * block_columns + row_ids % group_ratio * tile_rows
-    chip_ids = row_ids[::2] // 2
+    cols, spans = range(col_total), range(row_total // 2)
+    count = 2 * share
     received = other_core(given)
-    bias_part, kept = lax.optimization_barrier((collect(bias_flat, "col"), kept))
-    bias_part = stack_blocks(bias_part)
+    received = [received[m] for m in cols]
     kept = swap(kept, "col")
-    bias_even = stack_blocks(over_chips([bias_part] * len(chips)))
-    bias_slots = [bias_even, other_core(bias_even)]
     kept, received = lax.optimization_barrier((kept, received))
-    received = swap([received[m] for m in range(col_total)], "col")
-    kept = over_chips(regroup(chip_ids, kept))
+    received = swap(received, "col")
+    kept = regroup(
+        kept,
+        [
+            [(m, j * count, count) for m in cols]
+            + [(m, count * len(spans), heads) for m in cols]
+            for j in spans
+        ],
+    )
+    kept = over_chips(kept)
+    kept, received = lax.optimization_barrier((kept, received))
+    received = regroup(received, [[(m, j * count, count) for m in cols] for j in spans])
+    received = over_chips(received)
+    kept, received = lax.optimization_barrier((kept, received))
+    (bias_even,) = regroup(kept, [[(j, count * col_total, heads * col_total) for j in spans]])
+    bias_odd = other_core(bias_even)
+
+    side_slots = [slot for both in zip(kept, received) for slot in both]
+    *crossed, given = triangle(base, side_slots, share, col_total, residues)
+    bias_even, bias_odd, given = lax.optimization_barrier((bias_even, bias_odd, given))
+    bias_all = layout_bias(base, [bias_even, bias_odd], col_total, block_columns)
+    received = other_core(given)
+    crossed = regroup(
+        list(crossed) + [received[m] for m in cols],
+        [[(h * col_total + m, j, share) for h in range(2) for j in spans] for m in cols],
+    )
+    crossed = swap(crossed, "col")
 
     project = jnp.concatenate(
         [question_mapping_weights, address_payload_mapping, logistic_valve_mapping], axis=1
     )
-    own_after = attend(base, bias_slots, x_slots, own_marks, project, mixture_exit_mapping)
-
+    own_after = attend(bias_all, heads, x_slots, own_marks, project, mixture_exit_mapping)
+
+    crossed, own_after = lax.optimization_barrier((crossed, own_after))
     after_slots = swap(own_after, "col")
+    half = share * len(spans)
+    crossed = regroup(
+        crossed, [[(m, h * half + j * share, share) for h in range(2) for m in cols] for j in spans]
+    )
+    crossed = over_chips(crossed)
     homologs_after = place_slots(col_ids * own_seqs, after_slots)
-
-    received, own_after = lax.optimization_barrier((received, own_after))
-    received = over_chips(regroup(chip_ids, received))
-    side_slots = [slot for both in zip(kept, received) for slot in both]
-    crossed = triangle(base, side_slots, share, col_total, residues)
-    crossed, after_slots = lax.optimization_barrier((crossed, after_slots))
-    crossed = swap(crossed, "col")
-    crossed = swap(regroup(jnp.arange(row_total, dtype=jnp.int32), crossed), "row")
     exit_w = triad_exit_mapping.reshape(devices, share, pair_width)
     lead = (row_ids[:, None] * col_total + col_ids[None, :]).reshape(-1)
     couplings_after = finish(lead, crossed, ln_tri, z_one, triad_valve_mapping, exit_w)

time: 206 us -> 192 us (0.932)
  waiting for transfers between devices: 61.8 us -> 75.1 us
  starting transfers between devices: 52.1 us -> 41.5 us
  Pallas kernels: 63.7 us -> 53.5 us
  local copies, waits for them, and re-layouts: 23.1 us -> 15.1 us
    ppermute x28 -> x18, waiting for transfers between devices: 44.4 us -> 62.2 us  [swap(): lax.ppermute(pieces[k], axis, [(i, i ^ k) for i in range(total)])]
    pallas_call x7 -> x8, Pallas kernels: 34 us -> 23.6 us  [the longest x1 11.7 us: attend(): pl.pallas_call(functools.partial(attention_kernel, total_cols, heads), gr...]
    ppermute x28 -> x18, starting transfers between devices: 28.4 us -> 18.2 us  [swap(): lax.ppermute(pieces[k], axis, [(i, i ^ k) for i in range(total)])]
    ppermute x15, waiting for transfers between devices: 17.4 us -> 10.9 us  [over_chips(): lax.ppermute(piece, 'row', [(i, i ^ k) for i in range(row_total)])]
    unnamed x88 -> x98, local copies, waits for them, and re-layouts: 10.7 us -> 5.36 us
    ppermute x1 -> x0, local copies, waits for them, and re-layouts: 2.29 us -> none  [other_core(): return lax.ppermute(block, 'row', [(i, i ^ 1) for i in range(row_total)])]
    ppermute x4 -> x5, starting transfers between devices: 8.19 us -> 9.84 us  [other_core(): return lax.ppermute(block, 'row', [(i, i ^ 1) for i in range(row_total)])]
  transfers between devices with their start and end apart: 47 -> 38, of which waited for: 19 -> 15; matrix products, arithmetic and copies ran while one was open for 7% -> 4% of each run, Pallas kernels for 28% -> 26%
where the time goes in v3:
time: 192 us; the launch traced here: 189 us
  waiting for transfers between devices  75.1 us (39%)
  Pallas kernels  53.5 us (28%)
  starting transfers between devices  41.5 us (22%)
  local copies, waits for them, and re-layouts  15.1 us (8%)
  other arithmetic  2.72 us (1%)
    ppermute x18, waiting for transfers between devices, swap(): lax.ppermute(pieces[k], axis, [(i, i ^ k) for i in range(total)])  62.2 us
    ppermute x18, starting transfers between devices, swap(): lax.ppermute(pieces[k], axis, [(i, i ^ k) for i in range(total)])  18.2 us
    pallas_call x1, Pallas kernels, pair_stage(): pl.pallas_call(functools.partial(pair_kernel, total_rows, total_cols), gr...  17 us
    ppermute x15, starting transfers between devices, over_chips(): lax.ppermute(piece, 'row', [(i, i ^ k) for i in range(row_total)])  13.4 us
    pallas_call x1, Pallas kernels, attend(): pl.pallas_call(functools.partial(attention_kernel, total_cols, heads), gr...  11.7 us
    ppermute x15, waiting for transfers between devices, over_chips(): lax.ppermute(piece, 'row', [(i, i ^ k) for i in range(row_total)])  10.9 us
    pallas_call x1, Pallas kernels, triangle(): pl.pallas_call(functools.partial(triangle_kernel, total_rows, total_cols)...  10 us
    ppermute x5, starting transfers between devices, other_core(): return lax.ppermute(block, 'row', [(i, i ^ 1) for i in range(row_total)])  9.84 us
  transfers between devices with their start and end apart: 38, of which 15 were waited for; matrix products, arithmetic and copies ran while one was open for 4% of the time, Pallas kernels for 26%

profile of v3, /device:TPU:9, one launch (start us, length us, event | category | flops | bytes accessed | tf_op | source)
XLA Modules:
  0.0 189.4 jit_solution(8739322199508725367)
XLA Ops:
  3.0 1.0 outer_operands.1
  4.0 1.4 collective-permute-start.2
  5.4 1.1 collective-permute-start.1
  6.5 1.1 collective-permute-start
  7.6 1.2 collective-permute-start.7
  8.8 1.2 collective-permute-start.8
  11.0 0.9 copy.47.refs_7_
  13.9 2.2 %collective-permute-start.5 = (bf16[23,16,128]{2,1,0:T(8,128)(2,1)S(1)}, bf16[23,16,128]{2,1,0:T(8,128)(2,1)S(1)}, u32[]{:S(2)}, u32[]{:S(2)}) collective-permute-start(bf16[23,16,128]{2,1,0:T(8,128)(2,1)S(1)} %get-tuple-element.173), channel_id=1, source_target_pairs={{0,24},{4,28},{8,16},{12,20},{16,8},{20,12},{24,0},{28,4},{1,25},{... | collective-permute-start | bytes 282632 | tf_op jit(solution)/shard_map/ppermute | solution.py:710
  16.7 1.6 collective-permute-done.9
  18.4 4.2 %collective-permute-start.10 = (bf16[132,16,128]{2,1,0:T(8,128)(2,1)S(1)}, bf16[132,16,128]{2,1,0:T(8,128)(2,1)S(1)}, u32[]{:S(2)}, u32[]{:S(2)}) collective-permute-start(bf16[132,16,128]{2,1,0:T(8,128)(2,1)S(1)} %constant_dynamic-update-slice_fusion.refs_3_), channel_id=1, source_target_pairs={{0,4},{4,0},{8,12},{12,8},{16,20},{20,16},{24,28},{28,24},{1,5},{5... | collective-permute-start | bytes 1622024 | tf_op jit(solution)/shard_map/ppermute | solution.py:715
  23.3 1.4 collective-permute-start.6
  27.3 2.0 %collective-permute-start.15 = (bf16[4,88,256]{2,1,0:T(8,128)(2,1)S(1)}, bf16[4,88,256]{2,1,0:T(8,128)(2,1)S(1)}, u32[]{:S(2)}, u32[]{:S(2)}) collective-permute-start(bf16[4,88,256]{2,1,0:T(8,128)(2,1)S(1)} %get-tuple-element.165), channel_id=1, source_target_pairs={{0,2},{1,3},{2,0},{3,1},{4,6},{5,7},{6,4},{7,5},{8,10},{9,11},{10,... | collective-permute-start | bytes 540680 | tf_op jit(solution)/shard_map/ppermute | solution.py:22
  30.3 17.0 %pair_update.1 = (f32[3872,128]{1,0:T(8,128)}, bf16[3872,128]{1,0:T(8,128)(2,1)}, bf16[40,3872]{1,0:T(8,128)(2,1)}, bf16[40,3872]{1,0:T(8,128)(2,1)}, bf16[40,38...) custom-call(s32[4,44]{1,0:T(4,128)} %add_add_fusion.refs_0_, ...), custom_call_target="tpu_custom_call" | custom-call | tf_op jit(solution)/shard_map/pair_update/pallas_call | solution.py:287
  47.4 1.1 collective-permute-start.17
  48.4 1.3 collective-permute-start.11
  49.7 2.0 %collective-permute-start.12 = (bf16[40,3872]{1,0:T(8,128)(2,1)}, bf16[40,3872]{1,0:T(8,128)(2,1)S(1)}, u32[]{:S(2)}, u32[]{:S(2)}) collective-permute-start(bf16[40,3872]{1,0:T(8,128)(2,1)} %get-tuple-element.89), channel_id=1, source_target_pairs={{0,2},{1,3},{2,0},{3,1},{4,6},{5,7},{6,4},{7,5},{8,10},{9,11},{10,... | collective-permute-start | bytes 929288 | tf_op jit(solution)/shard_map/ppermute | solution.py:22
  52.1 11.2 %collective-permute-done.11.refs_1_ = bf16[40,3872]{1,0:T(8,128)(2,1)S(1)} collective-permute-done((bf16[40,3872]{1,0:T(8,128)(2,1)}, bf16[40,3872]{1,0:T(8,128)(2,1)S(1)}, u32[]{:S(2)}, u32[]{:S(2)}) %collective-permute-start.11) | collective-permute-done | bytes 309792 | tf_op jit(solution)/shard_map/ppermute | solution.py:22
  63.3 9.1 %collective-permute-done.12.refs_2_ = bf16[40,3872]{1,0:T(8,128)(2,1)S(1)} collective-permute-done((bf16[40,3872]{1,0:T(8,128)(2,1)}, bf16[40,3872]{1,0:T(8,128)(2,1)S(1)}, u32[]{:S(2)}, u32[]{:S(2)}) %collective-permute-start.12) | collective-permute-done | bytes 309792 | tf_op jit(solution)/shard_map/ppermute | solution.py:22
  72.4 7.9 %collective-permute-done.13.refs_3_ = bf16[40,3872]{1,0:T(8,128)(2,1)S(1)} collective-permute-done((bf16[40,3872]{1,0:T(8,128)(2,1)}, bf16[40,3872]{1,0:T(8,128)(2,1)S(1)}, u32[]{:S(2)}, u32[]{:S(2)}) %collective-permute-start.13) | collective-permute-done | bytes 309792 | tf_op jit(solution)/shard_map/ppermute | solution.py:22
  81.3 1.9 collective-permute-start.20
  83.2 2.2 %collective-permute-start.22 = (bf16[32,3872]{1,0:T(8,128)(2,1)S(1)}, bf16[32,3872]{1,0:T(8,128)(2,1)S(1)}, u32[]{:S(2)}, u32[]{:S(2)}) collective-permute-start(bf16[32,3872]{1,0:T(8,128)(2,1)S(1)} %get-tuple-element.104), channel_id=1, source_target_pairs={{0,2},{1,3},{2,0},{3,1},{4,6},{5,7},{6,4},{7,5},{8,10},{9,11},{10,... | collective-permute-start | bytes 743432 | tf_op jit(solution)/shard_map/ppermute | solution.py:22
  85.4 1.7 collective-permute-done.21.refs_1_
  87.1 0.9 collective-permute-start.23
  88.0 12.8 %collective-permute-done.22.refs_2_ = bf16[32,3872]{1,0:T(8,128)(2,1)S(1)} collective-permute-done((bf16[32,3872]{1,0:T(8,128)(2,1)S(1)}, bf16[32,3872]{1,0:T(8,128)(2,1)S(1)}, u32[]{:S(2)}, u32[]{:S(2)}) %collective-permute-start.22) | collective-permute-done | bytes 247840 | tf_op jit(solution)/shard_map/ppermute | solution.py:22
  100.8 6.4 %collective-permute-done.23.refs_3_ = bf16[32,3872]{1,0:T(8,128)(2,1)S(1)} collective-permute-done((bf16[32,3872]{1,0:T(8,128)(2,1)S(1)}, bf16[32,3872]{1,0:T(8,128)(2,1)S(1)}, u32[]{:S(2)}, u32[]{:S(2)}) %collective-permute-start.23) | collective-permute-done | bytes 247840 | tf_op jit(solution)/shard_map/ppermute | solution.py:22
  109.0 1.9 collective-permute-start.26
  110.8 3.0 %collective-permute-done.24.refs_4_ = bf16[32,3872]{1,0:T(8,128)(2,1)S(1)} collective-permute-done((bf16[32,3872]{1,0:T(8,128)(2,1)S(1)}, bf16[32,3872]{1,0:T(8,128)(2,1)S(1)}, u32[]{:S(2)}, u32[]{:S(2)}) %collective-permute-start.24) | collective-permute-done | bytes 247840 | tf_op jit(solution)/shard_map/ppermute | solution.py:710
  113.9 5.6 %collective-permute-done.26.refs_8_ = bf16[32,3872]{1,0:T(8,128)(2,1)S(1)} collective-permute-done((bf16[32,3872]{1,0:T(8,128)(2,1)S(1)}, bf16[32,3872]{1,0:T(8,128)(2,1)S(1)}, u32[]{:S(2)}, u32[]{:S(2)}) %collective-permute-start.26) | collective-permute-done | bytes 247840 | tf_op jit(solution)/shard_map/ppermute | solution.py:710
  120.3 1.4 copy.48
  121.7 3.0 %collective-permute-start.27 = (bf16[128,3872]{0,1:T(8,128)(2,1)}, bf16[128,3872]{0,1:T(8,128)(2,1)}, u32[]{:S(2)}, u32[]{:S(2)}) collective-permute-start(bf16[128,3872]{0,1:T(8,128)(2,1)} %copy.48), channel_id=1, source_target_pairs={{0,4},{4,0},{8,12},{12,8},{16,20},{20,16},{24,28},{28,24},{1,5},{5... | collective-permute-start | bytes 2973704 | tf_op jit(solution)/shard_map/ppermute | solution.py:715
  125.3 10.0 %triangle.1 = (bf16[4,4,3872]{2,1,0:T(4,128)(2,1)}, bf16[4,4,3872]{2,1,0:T(4,128)(2,1)}, bf16[4,4,3872]{2,1,0:T(4,128)(2,1)}, bf16[4,4,3872]{2,1,0:T(4,128)(2,1)}, bf16[4,4,4,3872]{3,2,1,0:T(4,128)(2,1)}) custom-call(s32[8]{0:T(128)} %fusion.7.refs_0_, bf16[64,3872]{1,0:T(8,128)(2,1)} %copy-done.1, bf16[32,3872]{1,0:T(8,128)(2,1)} %copy-done.9, ...), custom_call_target="tpu_custom_call" | custom-call | tf_op jit(solution)/shard_map/triangle/pallas_call | solution.py:586
  135.6 1.9 %collective-permute-done.28 = bf16[4,4,4,3872]{3,2,1,0:T(4,128)(2,1)S(1)} collective-permute-done((bf16[4,4,4,3872]{3,2,1,0:T(4,128)(2,1)}, bf16[4,4,4,3872]{3,2,1,0:T(4,128)(2,1)S(1)}, u32[]{:S(2)}, u32[]{:S(2)}) %collective-permute-start.28) | collective-permute-done | bytes 495648 | tf_op jit(solution)/shard_map/ppermute | solution.py:715
  137.8 0.9 regroup.8
  139.4 2.4 %collective-permute-start.30 = (bf16[32,3872]{1,0:T(8,128)(2,1)}, bf16[32,3872]{1,0:T(8,128)(2,1)}, u32[]{:S(2)}, u32[]{:S(2)}) collective-permute-start(bf16[32,3872]{1,0:T(8,128)(2,1)} %get-tuple-element.134), channel_id=1, source_target_pairs={{0,2},{1,3},{2,0},{3,1},{4,6},{5,7},{6,4},{7,5},{8,10},{9,11},{10,... | collective-permute-start | bytes 743432 | tf_op jit(solution)/shard_map/ppermute | solution.py:22
  142.2 1.6 copy.49.refs_2_
  143.9 5.3 %layout_bias.1.refs_0_ = bf16[3,2816,128]{2,1,0:T(8,128)(2,1)S(1)} custom-call(s32[8]{0:T(128)S(1)} %copy-done.29, bf16[128,3872]{1,0:T(8,128)(2,1)S(1)} %regroup.7.refs_1_, bf16[128,3872]{1,0:T(8,128)(2,1)S(1)} %copy.49.refs_2_), custom_call_target="tpu_custom_call" | custom-call | tf_op jit(solution)/shard_map/layout_bias/pallas_call | solution.py:362
  149.3 11.7 %row_attention.1 = (bf16[4,88,256]{2,1,0:T(8,128)(2,1)S(1)}, bf16[4,88,256]{2,1,0:T(8,128)(2,1)S(1)}, bf16[4,88,256]{2,1,0:T(8,128)(2,1)}, bf16[4,88,256]{2,1,0:T(8,128)(2,1)}) custom-call(bf16[3,2816,128]{2,1,0:T(8,128)(2,1)S(1)} %layout_bias.1.refs_0_, bf16[4,88,256]{2,1,0:T(8,128)(2,1)S(1)} %copy-done.7, bf16[4,88,256]{2,1,0:T(8,128)(2,1)S(1)} %copy-done.17, ...), custom_call_target="tpu_custom_call" | custom-call | tf_op jit(solution)/shard_map/row_attention/pallas_call | solution.py:454
  161.1 3.5 %collective-permute-done.31.refs_3_ = bf16[32,3872]{1,0:T(8,128)(2,1)} collective-permute-done((bf16[32,3872]{1,0:T(8,128)(2,1)}, bf16[32,3872]{1,0:T(8,128)(2,1)}, u32[]{:S(2)}, u32[]{:S(2)}) %collective-permute-start.31) | collective-permute-done | bytes 247840 | tf_op jit(solution)/shard_map/ppermute | solution.py:22
  164.6 2.4 %collective-permute-start.33 = (bf16[4,88,256]{2,1,0:T(8,128)(2,1)}, bf16[4,88,256]{2,1,0:T(8,128)(2,1)}, u32[]{:S(2)}, u32[]{:S(2)}) collective-permute-start(bf16[4,88,256]{2,1,0:T(8,128)(2,1)} %get-tuple-element.148), channel_id=1, source_target_pairs={{0,2},{1,3},{2,0},{3,1},{4,6},{5,7},{6,4},{7,5},{8,10},{9,11},{10,... | collective-permute-start | bytes 540680 | tf_op jit(solution)/shard_map/ppermute | solution.py:22
  167.2 2.2 %regroup.9 = (bf16[32,3872]{1,0:T(8,128)(2,1)S(1)}, bf16[32,3872]{1,0:T(8,128)(2,1)}, bf16[32,3872]{1,0:T(8,128)(2,1)}, bf16[32,3872]{1,0:T(8,128)(2,1)}) custom-call(bf16[32,3872]{1,0:T(8,128)(2,1)S(1)} %copy-done.11, bf16[32,3872]{1,0:T(8,128)(2,1)} %collective-permute-done.29.refs_1_, bf16[32,3872]{1,0:T(8,128)(2,1)} %collective-permute-done.30.refs_2_, ...), custom_call_target="tpu_custom_call" | custom-call | tf_op jit(solution)/shard_map/regroup/pallas_call | solution.py:486
  169.4 1.3 collective-permute-start.35
  171.9 0.8 collective-permute-start.37
  172.9 1.3 collective-permute-done.33.refs_2_
  174.2 8.2 %collective-permute-done.34.refs_3_ = bf16[4,88,256]{2,1,0:T(8,128)(2,1)} collective-permute-done((bf16[4,88,256]{2,1,0:T(8,128)(2,1)}, bf16[4,88,256]{2,1,0:T(8,128)(2,1)}, u32[]{:S(2)}, u32[]{:S(2)}) %collective-permute-start.34) | collective-permute-done | bytes 180256 | tf_op jit(solution)/shard_map/ppermute | solution.py:22
  182.5 0.9 copy-done.13
  183.4 0.9 copy-done.15
  184.3 1.9 %place_sequences.1 = bf16[16,88,256]{2,1,0:T(8,128)(2,1)} custom-call(s32[4]{0:T(128)S(1)} %broadcast_multiply_fusion.start_ref, bf16[4,88,256]{2,1,0:T(8,128)(2,1)S(1)} %copy-done.13, bf16[4,88,256]{2,1,0:T(8,128)(2,1)S(1)} %copy-done.15, bf16[4,88,256]{2,1,0:T(8,128)(2,1)} %collective-permute-done.33.refs_2_, ...), custom_call_target="tpu_custom_call" | custom-call | tf_op jit(solution)/shard_map/place_sequences/pallas_call | solution.py:652
  186.3 3.1 %pair_finish.1 = bf16[3872,128]{1,0:T(8,128)(2,1)} custom-call(s32[32]{0:T(128)S(1)} %add.136.refs_0_, bf16[32,3872]{1,0:T(8,128)(2,1)S(1)} %get-tuple-element.154.refs_1_, bf16[32,3872]{1,0:T(8,128)(2,1)S(1)} %collective-permute-done.35.refs_2_, bf16[32,3872]{1,0:T(8,128)(2,1)} %collective-permute-done.36.refs_3_, ...), custom_call_target="tpu_custom_call" | custom-call | tf_op jit(solution)/shard_map/pair_finish/pallas_call | solution.py:632
  (187 shorter events, 17.7 us)
Async XLA Ops:
  4.0 9.5 %collective-permute-start.2 = (bf16[23,16,128]{2,1,0:T(8,128)(2,1)S(1)}, bf16[23,16,128]{2,1,0:T(8,128)(2,1)S(1)}, u32[]{:S(2)}, u32[]{:S(2)}) collective-permute-start(bf16[23,16,128]{2,1,0:T(8,128)(2,1)S(1)} %get-tuple-element.81), channel_id=1, source_target_pairs={{0,3},{1,2},{2,1},{3,0},{4,7},{5,6},{6,5},{7,4},{8,11},{9,10},{10,... | collective-permute-start | bytes 282632 | tf_op jit(solution)/shard_map/ppermute | solution.py:22
  5.4 8.4 %collective-permute-start.1 = (bf16[23,16,128]{2,1,0:T(8,128)(2,1)S(1)}, bf16[23,16,128]{2,1,0:T(8,128)(2,1)S(1)}, u32[]{:S(2)}, u32[]{:S(2)}) collective-permute-start(bf16[23,16,128]{2,1,0:T(8,128)(2,1)S(1)} %get-tuple-element.81), channel_id=1, source_target_pairs={{0,2},{1,3},{2,0},{3,1},{4,6},{5,7},{6,4},{7,5},{8,10},{9,11},{10,... | collective-permute-start | bytes 282632 | tf_op jit(solution)/shard_map/ppermute | solution.py:22
  6.5 7.3 %collective-permute-start = (bf16[23,16,128]{2,1,0:T(8,128)(2,1)S(1)}, bf16[23,16,128]{2,1,0:T(8,128)(2,1)S(1)}, u32[]{:S(2)}, u32[]{:S(2)}) collective-permute-start(bf16[23,16,128]{2,1,0:T(8,128)(2,1)S(1)} %get-tuple-element.81), channel_id=1, source_target_pairs={{0,1},{1,0},{2,3},{3,2},{4,5},{5,4},{6,7},{7,6},{8,9},{9,8},{10,11... | collective-permute-start | bytes 282632 | tf_op jit(solution)/shard_map/ppermute | solution.py:22
  7.6 8.8 %collective-permute-start.7 = (bf16[33,16,128]{2,1,0:T(8,128)(2,1)S(1)}, bf16[33,16,128]{2,1,0:T(8,128)(2,1)S(1)}, u32[]{:S(2)}, u32[]{:S(2)}) collective-permute-start(bf16[33,16,128]{2,1,0:T(8,128)(2,1)S(1)} %get-tuple-element.82), channel_id=1, source_target_pairs={{0,8},{4,12},{8,0},{12,4},{16,24},{20,28},{24,16},{28,20},{1,9},{5... | collective-permute-start | bytes 405512 | tf_op jit(solution)/shard_map/ppermute | solution.py:710
  8.8 7.9 %collective-permute-start.8 = (bf16[33,16,128]{2,1,0:T(8,128)(2,1)S(1)}, bf16[33,16,128]{2,1,0:T(8,128)(2,1)S(1)}, u32[]{:S(2)}, u32[]{:S(2)}) collective-permute-start(bf16[33,16,128]{2,1,0:T(8,128)(2,1)S(1)} %get-tuple-element.82), channel_id=1, source_target_pairs={{0,16},{4,20},{8,24},{12,28},{16,0},{20,4},{24,8},{28,12},{1,17},{... | collective-permute-start | bytes 405512 | tf_op jit(solution)/shard_map/ppermute | solution.py:710
  13.5 4.8 %collective-permute-start.9 = (bf16[33,16,128]{2,1,0:T(8,128)(2,1)S(1)}, bf16[33,16,128]{2,1,0:T(8,128)(2,1)S(1)}, u32[]{:S(2)}, u32[]{:S(2)}) collective-permute-start(bf16[33,16,128]{2,1,0:T(8,128)(2,1)S(1)} %get-tuple-element.82), channel_id=1, source_target_pairs={{0,24},{4,28},{8,16},{12,20},{16,8},{20,12},{24,0},{28,4},{1,25},{... | collective-permute-start | bytes 405512 | tf_op jit(solution)/shard_map/ppermute | solution.py:710
  13.9 8.7 %collective-permute-start.5 = (bf16[23,16,128]{2,1,0:T(8,128)(2,1)S(1)}, bf16[23,16,128]{2,1,0:T(8,128)(2,1)S(1)}, u32[]{:S(2)}, u32[]{:S(2)}) collective-permute-start(bf16[23,16,128]{2,1,0:T(8,128)(2,1)S(1)} %get-tuple-element.173), channel_id=1, source_target_pairs={{0,24},{4,28},{8,16},{12,20},{16,8},{20,12},{24,0},{28,4},{1,25},{... | collective-permute-start | bytes 282632 | tf_op jit(solution)/shard_map/ppermute | solution.py:710
  16.1 7.1 %collective-permute-start.4 = (bf16[23,16,128]{2,1,0:T(8,128)(2,1)S(1)}, bf16[23,16,128]{2,1,0:T(8,128)(2,1)S(1)}, u32[]{:S(2)}, u32[]{:S(2)}) collective-permute-start(bf16[23,16,128]{2,1,0:T(8,128)(2,1)S(1)} %get-tuple-element.174), channel_id=1, source_target_pairs={{0,16},{4,20},{8,24},{12,28},{16,0},{20,4},{24,8},{28,12},{1,17},{... | collective-permute-start | bytes 282632 | tf_op jit(solution)/shard_map/ppermute | solution.py:710
  16.4 6.8 %collective-permute-start.3 = (bf16[23,16,128]{2,1,0:T(8,128)(2,1)S(1)}, bf16[23,16,128]{2,1,0:T(8,128)(2,1)S(1)}, u32[]{:S(2)}, u32[]{:S(2)}) collective-permute-start(bf16[23,16,128]{2,1,0:T(8,128)(2,1)S(1)} %get-tuple-element.175), channel_id=1, source_target_pairs={{0,8},{4,12},{8,0},{12,4},{16,24},{20,28},{24,16},{28,20},{1,9},{5... | collective-permute-start | bytes 282632 | tf_op jit(solution)/shard_map/ppermute | solution.py:710
  18.4 7.8 %collective-permute-start.10 = (bf16[132,16,128]{2,1,0:T(8,128)(2,1)S(1)}, bf16[132,16,128]{2,1,0:T(8,128)(2,1)S(1)}, u32[]{:S(2)}, u32[]{:S(2)}) collective-permute-start(bf16[132,16,128]{2,1,0:T(8,128)(2,1)S(1)} %constant_dynamic-update-slice_fusion.refs_3_), channel_id=1, source_target_pairs={{0,4},{4,0},{8,12},{12,8},{16,20},{20,16},{24,28},{28,24},{1,5},{5... | collective-permute-start | bytes 1622024 | tf_op jit(solution)/shard_map/ppermute | solution.py:715
  23.3 2.8 %collective-permute-start.6 = (bf16[92,16,128]{2,1,0:T(8,128)(2,1)S(1)}, bf16[92,16,128]{2,1,0:T(8,128)(2,1)S(1)}, u32[]{:S(2)}, u32[]{:S(2)}) collective-permute-start(bf16[92,16,128]{2,1,0:T(8,128)(2,1)S(1)} %pad_maximum_fusion.2.refs_1_), channel_id=1, source_target_pairs={{0,4},{4,0},{8,12},{12,8},{16,20},{20,16},{24,28},{28,24},{1,5},{5... | collective-permute-start | bytes 1130504 | tf_op jit(solution)/shard_map/ppermute | solution.py:715
  27.0 20.3 %collective-permute-start.14 = (bf16[4,88,256]{2,1,0:T(8,128)(2,1)S(1)}, bf16[4,88,256]{2,1,0:T(8,128)(2,1)S(1)}, u32[]{:S(2)}, u32[]{:S(2)}) collective-permute-start(bf16[4,88,256]{2,1,0:T(8,128)(2,1)S(1)} %get-tuple-element.166), channel_id=1, source_target_pairs={{0,1},{1,0},{2,3},{3,2},{4,5},{5,4},{6,7},{7,6},{8,9},{9,8},{10,11... | collective-permute-start | bytes 540680 | tf_op jit(solution)/shard_map/ppermute | solution.py:22
  27.3 20.0 %collective-permute-start.15 = (bf16[4,88,256]{2,1,0:T(8,128)(2,1)S(1)}, bf16[4,88,256]{2,1,0:T(8,128)(2,1)S(1)}, u32[]{:S(2)}, u32[]{:S(2)}) collective-permute-start(bf16[4,88,256]{2,1,0:T(8,128)(2,1)S(1)} %get-tuple-element.165), channel_id=1, source_target_pairs={{0,2},{1,3},{2,0},{3,1},{4,6},{5,7},{6,4},{7,5},{8,10},{9,11},{10,... | collective-permute-start | bytes 540680 | tf_op jit(solution)/shard_map/ppermute | solution.py:22
  29.3 18.0 %collective-permute-start.16 = (bf16[4,88,256]{2,1,0:T(8,128)(2,1)S(1)}, bf16[4,88,256]{2,1,0:T(8,128)(2,1)S(1)}, u32[]{:S(2)}, u32[]{:S(2)}) collective-permute-start(bf16[4,88,256]{2,1,0:T(8,128)(2,1)S(1)} %get-tuple-element.164), channel_id=1, source_target_pairs={{0,3},{1,2},{2,1},{3,0},{4,7},{5,6},{6,5},{7,4},{8,11},{9,10},{10,... | collective-permute-start | bytes 540680 | tf_op jit(solution)/shard_map/ppermute | solution.py:22
  47.3 33.0 %copy-start.8 = (bf16[40,3872]{1,0:T(8,128)(2,1)S(1)}, bf16[40,3872]{1,0:T(8,128)(2,1)}, u32[]{:S(2)}) copy-start(bf16[40,3872]{1,0:T(8,128)(2,1)} %get-tuple-element.94.refs_0_) | copy-start | bytes 929284
  47.3 60.0 %copy-start.16 = (bf16[4,88,256]{2,1,0:T(8,128)(2,1)}, bf16[4,88,256]{2,1,0:T(8,128)(2,1)S(1)}, u32[]{:S(2)}) copy-start(bf16[4,88,256]{2,1,0:T(8,128)(2,1)S(1)} %collective-permute-done.14.refs_2_) | copy-start | bytes 540676
  47.3 60.0 %copy-start.18 = (bf16[4,88,256]{2,1,0:T(8,128)(2,1)}, bf16[4,88,256]{2,1,0:T(8,128)(2,1)S(1)}, u32[]{:S(2)}) copy-start(bf16[4,88,256]{2,1,0:T(8,128)(2,1)S(1)} %collective-permute-done.15.refs_3_) | copy-start | bytes 540676
  47.4 60.0 %copy-start.20 = (bf16[4,88,256]{2,1,0:T(8,128)(2,1)}, bf16[4,88,256]{2,1,0:T(8,128)(2,1)S(1)}, u32[]{:S(2)}) copy-start(bf16[4,88,256]{2,1,0:T(8,128)(2,1)S(1)} %collective-permute-done.16.refs_4_) | copy-start | bytes 540676
  47.4 4.7 %collective-permute-start.17 = (bf16[4,32,3872]{2,1,0:T(8,128)(2,1)}, bf16[4,32,3872]{2,1,0:T(8,128)(2,1)S(1)}, u32[]{:S(2)}, u32[]{:S(2)}) collective-permute-start(bf16[4,32,3872]{2,1,0:T(8,128)(2,1)} %get-tuple-element.93), channel_id=1, source_target_pairs={{0,4},{4,0},{8,12},{12,8},{16,20},{20,16},{24,28},{28,24},{1,5},{5... | collective-permute-start | bytes 2973704 | tf_op jit(solution)/shard_map/ppermute | solution.py:715
  48.4 14.9 %collective-permute-start.11 = (bf16[40,3872]{1,0:T(8,128)(2,1)}, bf16[40,3872]{1,0:T(8,128)(2,1)S(1)}, u32[]{:S(2)}, u32[]{:S(2)}) collective-permute-start(bf16[40,3872]{1,0:T(8,128)(2,1)} %get-tuple-element.88), channel_id=1, source_target_pairs={{0,1},{1,0},{2,3},{3,2},{4,5},{5,4},{6,7},{7,6},{8,9},{9,8},{10,11... | collective-permute-start | bytes 929288 | tf_op jit(solution)/shard_map/ppermute | solution.py:22
  49.7 22.7 %collective-permute-start.12 = (bf16[40,3872]{1,0:T(8,128)(2,1)}, bf16[40,3872]{1,0:T(8,128)(2,1)S(1)}, u32[]{:S(2)}, u32[]{:S(2)}) collective-permute-start(bf16[40,3872]{1,0:T(8,128)(2,1)} %get-tuple-element.89), channel_id=1, source_target_pairs={{0,2},{1,3},{2,0},{3,1},{4,6},{5,7},{6,4},{7,5},{8,10},{9,11},{10,... | collective-permute-start | bytes 929288 | tf_op jit(solution)/shard_map/ppermute | solution.py:22
  51.7 28.6 %collective-permute-start.13 = (bf16[40,3872]{1,0:T(8,128)(2,1)}, bf16[40,3872]{1,0:T(8,128)(2,1)S(1)}, u32[]{:S(2)}, u32[]{:S(2)}) collective-permute-start(bf16[40,3872]{1,0:T(8,128)(2,1)} %get-tuple-element.90), channel_id=1, source_target_pairs={{0,3},{1,2},{2,1},{3,0},{4,7},{5,6},{6,5},{7,4},{8,11},{9,10},{10,... | collective-permute-start | bytes 929288 | tf_op jit(solution)/shard_map/ppermute | solution.py:22
  80.3 6.8 %collective-permute-start.21 = (bf16[32,3872]{1,0:T(8,128)(2,1)S(1)}, bf16[32,3872]{1,0:T(8,128)(2,1)S(1)}, u32[]{:S(2)}, u32[]{:S(2)}) collective-permute-start(bf16[32,3872]{1,0:T(8,128)(2,1)S(1)} %get-tuple-element.103), channel_id=1, source_target_pairs={{0,1},{1,0},{2,3},{3,2},{4,5},{5,4},{6,7},{7,6},{8,9},{9,8},{10,11... | collective-permute-start | bytes 743432 | tf_op jit(solution)/shard_map/ppermute | solution.py:22
  80.4 41.2 %copy-start.1 = (bf16[64,3872]{1,0:T(8,128)(2,1)}, bf16[64,3872]{1,0:T(8,128)(2,1)S(1)}, u32[]{:S(2)}) copy-start(bf16[64,3872]{1,0:T(8,128)(2,1)S(1)} %get-tuple-element.118.refs_1_.refs_0_) | copy-start | bytes 1486852
  80.4 26.8 %collective-permute-start.18 = (bf16[64,3872]{1,0:T(8,128)(2,1)S(1)}, bf16[64,3872]{1,0:T(8,128)(2,1)S(1)}, u32[]{:S(2)}, u32[]{:S(2)}) collective-permute-start(bf16[64,3872]{1,0:T(8,128)(2,1)S(1)} %get-tuple-element.99), channel_id=1, source_target_pairs={{0,8},{4,12},{8,0},{12,4},{16,24},{20,28},{24,16},{28,20},{1,9},{5... | collective-permute-start | bytes 1486856 | tf_op jit(solution)/shard_map/ppermute | solution.py:710
  80.8 26.4 %collective-permute-start.19 = (bf16[64,3872]{1,0:T(8,128)(2,1)S(1)}, bf16[64,3872]{1,0:T(8,128)(2,1)S(1)}, u32[]{:S(2)}, u32[]{:S(2)}) collective-permute-start(bf16[64,3872]{1,0:T(8,128)(2,1)S(1)} %get-tuple-element.100), channel_id=1, source_target_pairs={{0,16},{4,20},{8,24},{12,28},{16,0},{20,4},{24,8},{28,12},{1,17},{... | collective-permute-start | bytes 1486856 | tf_op jit(solution)/shard_map/ppermute | solution.py:710
  81.3 25.9 %collective-permute-start.20 = (bf16[64,3872]{1,0:T(8,128)(2,1)S(1)}, bf16[64,3872]{1,0:T(8,128)(2,1)S(1)}, u32[]{:S(2)}, u32[]{:S(2)}) collective-permute-start(bf16[64,3872]{1,0:T(8,128)(2,1)S(1)} %get-tuple-element.101), channel_id=1, source_target_pairs={{0,24},{4,28},{8,16},{12,20},{16,8},{20,12},{24,0},{28,4},{1,25},{... | collective-permute-start | bytes 1486856 | tf_op jit(solution)/shard_map/ppermute | solution.py:710
  83.2 17.6 %collective-permute-start.22 = (bf16[32,3872]{1,0:T(8,128)(2,1)S(1)}, bf16[32,3872]{1,0:T(8,128)(2,1)S(1)}, u32[]{:S(2)}, u32[]{:S(2)}) collective-permute-start(bf16[32,3872]{1,0:T(8,128)(2,1)S(1)} %get-tuple-element.104), channel_id=1, source_target_pairs={{0,2},{1,3},{2,0},{3,1},{4,6},{5,7},{6,4},{7,5},{8,10},{9,11},{10,... | collective-permute-start | bytes 743432 | tf_op jit(solution)/shard_map/ppermute | solution.py:22
  87.1 20.1 %collective-permute-start.23 = (bf16[32,3872]{1,0:T(8,128)(2,1)S(1)}, bf16[32,3872]{1,0:T(8,128)(2,1)S(1)}, u32[]{:S(2)}, u32[]{:S(2)}) collective-permute-start(bf16[32,3872]{1,0:T(8,128)(2,1)S(1)} %get-tuple-element.105), channel_id=1, source_target_pairs={{0,3},{1,2},{2,1},{3,0},{4,7},{5,6},{6,5},{7,4},{8,11},{9,10},{10,... | collective-permute-start | bytes 743432 | tf_op jit(solution)/shard_map/ppermute | solution.py:22
  108.2 5.6 %collective-permute-start.24 = (bf16[32,3872]{1,0:T(8,128)(2,1)S(1)}, bf16[32,3872]{1,0:T(8,128)(2,1)S(1)}, u32[]{:S(2)}, u32[]{:S(2)}) collective-permute-start(bf16[32,3872]{1,0:T(8,128)(2,1)S(1)} %get-tuple-element.115), channel_id=1, source_target_pairs={{0,8},{4,12},{8,0},{12,4},{16,24},{20,28},{24,16},{28,20},{1,9},{5... | collective-permute-start | bytes 743432 | tf_op jit(solution)/shard_map/ppermute | solution.py:710
  108.4 5.4 %collective-permute-start.25 = (bf16[32,3872]{1,0:T(8,128)(2,1)S(1)}, bf16[32,3872]{1,0:T(8,128)(2,1)S(1)}, u32[]{:S(2)}, u32[]{:S(2)}) collective-permute-start(bf16[32,3872]{1,0:T(8,128)(2,1)S(1)} %get-tuple-element.116), channel_id=1, source_target_pairs={{0,16},{4,20},{8,24},{12,28},{16,0},{20,4},{24,8},{28,12},{1,17},{... | collective-permute-start | bytes 743432 | tf_op jit(solution)/shard_map/ppermute | solution.py:710
  109.0 10.5 %collective-permute-start.26 = (bf16[32,3872]{1,0:T(8,128)(2,1)S(1)}, bf16[32,3872]{1,0:T(8,128)(2,1)S(1)}, u32[]{:S(2)}, u32[]{:S(2)}) collective-permute-start(bf16[32,3872]{1,0:T(8,128)(2,1)S(1)} %get-tuple-element.117), channel_id=1, source_target_pairs={{0,24},{4,28},{8,16},{12,20},{16,8},{20,12},{24,0},{28,4},{1,25},{... | collective-permute-start | bytes 743432 | tf_op jit(solution)/shard_map/ppermute | solution.py:710
  121.7 13.7 %collective-permute-start.27 = (bf16[128,3872]{0,1:T(8,128)(2,1)}, bf16[128,3872]{0,1:T(8,128)(2,1)}, u32[]{:S(2)}, u32[]{:S(2)}) collective-permute-start(bf16[128,3872]{0,1:T(8,128)(2,1)} %copy.48), channel_id=1, source_target_pairs={{0,4},{4,0},{8,12},{12,8},{16,20},{20,16},{24,28},{28,24},{1,5},{5... | collective-permute-start | bytes 2973704 | tf_op jit(solution)/shard_map/ppermute | solution.py:715
  135.4 2.2 %collective-permute-start.28 = (bf16[4,4,4,3872]{3,2,1,0:T(4,128)(2,1)}, bf16[4,4,4,3872]{3,2,1,0:T(4,128)(2,1)S(1)}, u32[]{:S(2)}, u32[]{:S(2)}) collective-permute-start(bf16[4,4,4,3872]{3,2,1,0:T(4,128)(2,1)} %get-tuple-element.131), channel_id=1, source_target_pairs={{0,4},{4,0},{8,12},{12,8},{16,20},{20,16},{24,28},{28,24},{1,5},{5... | collective-permute-start | bytes 1486856 | tf_op jit(solution)/shard_map/ppermute | solution.py:715
  139.4 21.6 %collective-permute-start.29 = (bf16[32,3872]{1,0:T(8,128)(2,1)}, bf16[32,3872]{1,0:T(8,128)(2,1)}, u32[]{:S(2)}, u32[]{:S(2)}) collective-permute-start(bf16[32,3872]{1,0:T(8,128)(2,1)} %get-tuple-element.133), channel_id=1, source_target_pairs={{0,1},{1,0},{2,3},{3,2},{4,5},{5,4},{6,7},{7,6},{8,9},{9,8},{10,11... | collective-permute-start | bytes 743432 | tf_op jit(solution)/shard_map/ppermute | solution.py:22
  139.4 21.6 %collective-permute-start.30 = (bf16[32,3872]{1,0:T(8,128)(2,1)}, bf16[32,3872]{1,0:T(8,128)(2,1)}, u32[]{:S(2)}, u32[]{:S(2)}) collective-permute-start(bf16[32,3872]{1,0:T(8,128)(2,1)} %get-tuple-element.134), channel_id=1, source_target_pairs={{0,2},{1,3},{2,0},{3,1},{4,6},{5,7},{6,4},{7,5},{8,10},{9,11},{10,... | collective-permute-start | bytes 743432 | tf_op jit(solution)/shard_map/ppermute | solution.py:22
  141.8 22.8 %collective-permute-start.31 = (bf16[32,3872]{1,0:T(8,128)(2,1)}, bf16[32,3872]{1,0:T(8,128)(2,1)}, u32[]{:S(2)}, u32[]{:S(2)}) collective-permute-start(bf16[32,3872]{1,0:T(8,128)(2,1)} %get-tuple-element.135), channel_id=1, source_target_pairs={{0,3},{1,2},{2,1},{3,0},{4,7},{5,6},{6,5},{7,4},{8,11},{9,10},{10,... | collective-permute-start | bytes 743432 | tf_op jit(solution)/shard_map/ppermute | solution.py:22
  149.3 17.9 %copy-start.11 = (bf16[32,3872]{1,0:T(8,128)(2,1)S(1)}, bf16[32,3872]{1,0:T(8,128)(2,1)}, u32[]{:S(2)}) copy-start(bf16[32,3872]{1,0:T(8,128)(2,1)} %copy-done.10) | copy-start | bytes 743428
  149.3 37.0 %copy-start.5 = (f32[3872,128]{1,0:T(8,128)S(1)}, f32[3872,128]{1,0:T(8,128)}, u32[]{:S(2)}) copy-start(f32[3872,128]{1,0:T(8,128)} %get-tuple-element.159.refs_6_) | copy-start | bytes 5947396
  149.3 37.0 %copy-start.6 = (bf16[3872,128]{1,0:T(8,128)(2,1)S(1)}, bf16[3872,128]{1,0:T(8,128)(2,1)}, u32[]{:S(2)}) copy-start(bf16[3872,128]{1,0:T(8,128)(2,1)} %get-tuple-element.158.refs_5_) | copy-start | bytes 2973700
  161.0 25.2 %copy-start.27 = (bf16[128,128]{1,0:T(8,128)(2,1)S(1)}, bf16[128,128]{1,0:T(8,128)(2,1)}, u32[]{:S(2)}) copy-start(bf16[128,128]{1,0:T(8,128)(2,1)} %refs_7_.3) | copy-start | bytes 98308
  161.1 25.2 %copy-start.28 = (bf16[128,128]{1,0:T(8,128)(2,1)S(1)}, bf16[128,128]{1,0:T(8,128)(2,1)}, u32[]{:S(2)}) copy-start(bf16[128,128]{1,0:T(8,128)(2,1)} %param.33) | copy-start | bytes 98308
  164.6 6.6 %collective-permute-start.32 = (bf16[4,88,256]{2,1,0:T(8,128)(2,1)S(1)}, bf16[4,88,256]{2,1,0:T(8,128)(2,1)S(1)}, u32[]{:S(2)}, u32[]{:S(2)}) collective-permute-start(bf16[4,88,256]{2,1,0:T(8,128)(2,1)S(1)} %get-tuple-element.147), channel_id=1, source_target_pairs={{0,1},{1,0},{2,3},{3,2},{4,5},{5,4},{6,7},{7,6},{8,9},{9,8},{10,11... | collective-permute-start | bytes 540680 | tf_op jit(solution)/shard_map/ppermute | solution.py:22
  164.6 9.6 %collective-permute-start.33 = (bf16[4,88,256]{2,1,0:T(8,128)(2,1)}, bf16[4,88,256]{2,1,0:T(8,128)(2,1)}, u32[]{:S(2)}, u32[]{:S(2)}) collective-permute-start(bf16[4,88,256]{2,1,0:T(8,128)(2,1)} %get-tuple-element.148), channel_id=1, source_target_pairs={{0,2},{1,3},{2,0},{3,1},{4,6},{5,7},{6,4},{7,5},{8,10},{9,11},{10,... | collective-permute-start | bytes 540680 | tf_op jit(solution)/shard_map/ppermute | solution.py:22
  166.9 15.5 %collective-permute-start.34 = (bf16[4,88,256]{2,1,0:T(8,128)(2,1)}, bf16[4,88,256]{2,1,0:T(8,128)(2,1)}, u32[]{:S(2)}, u32[]{:S(2)}) collective-permute-start(bf16[4,88,256]{2,1,0:T(8,128)(2,1)} %get-tuple-element.149), channel_id=1, source_target_pairs={{0,3},{1,2},{2,1},{3,0},{4,7},{5,6},{6,5},{7,4},{8,11},{9,10},{10,... | collective-permute-start | bytes 540680 | tf_op jit(solution)/shard_map/ppermute | solution.py:22
  169.4 16.8 %collective-permute-start.35 = (bf16[32,3872]{1,0:T(8,128)(2,1)}, bf16[32,3872]{1,0:T(8,128)(2,1)S(1)}, u32[]{:S(2)}, u32[]{:S(2)}) collective-permute-start(bf16[32,3872]{1,0:T(8,128)(2,1)} %get-tuple-element.155), channel_id=1, source_target_pairs={{0,8},{4,12},{8,0},{12,4},{16,24},{20,28},{24,16},{28,20},{1,9},{5... | collective-permute-start | bytes 743432 | tf_op jit(solution)/shard_map/ppermute | solution.py:710
  170.7 15.5 %collective-permute-start.36 = (bf16[32,3872]{1,0:T(8,128)(2,1)}, bf16[32,3872]{1,0:T(8,128)(2,1)}, u32[]{:S(2)}, u32[]{:S(2)}) collective-permute-start(bf16[32,3872]{1,0:T(8,128)(2,1)} %get-tuple-element.156), channel_id=1, source_target_pairs={{0,16},{4,20},{8,24},{12,28},{16,0},{20,4},{24,8},{28,12},{1,17},{... | collective-permute-start | bytes 743432 | tf_op jit(solution)/shard_map/ppermute | solution.py:710
  171.9 14.4 %collective-permute-start.37 = (bf16[32,3872]{1,0:T(8,128)(2,1)}, bf16[32,3872]{1,0:T(8,128)(2,1)}, u32[]{:S(2)}, u32[]{:S(2)}) collective-permute-start(bf16[32,3872]{1,0:T(8,128)(2,1)} %get-tuple-element.157), channel_id=1, source_target_pairs={{0,24},{4,28},{8,16},{12,20},{16,8},{20,12},{24,0},{28,4},{1,25},{... | collective-permute-start | bytes 743432 | tf_op jit(solution)/shard_map/ppermute | solution.py:710
  (36 other events, 236.0 us)

commit v4 on v3

--- a/solution.py
+++ b/solution.py
@@ -829,8 +829,8 @@
     )
     own_after = attend(bias_all, heads, x_slots, own_marks, project, mixture_exit_mapping)
 
-    crossed, own_after = lax.optimization_barrier((crossed, own_after))
     after_slots = swap(own_after, "col")
+    crossed, _ = lax.optimization_barrier((crossed, own_after))
     half = share * len(spans)
     crossed = regroup(
         crossed, [[(m, h * half + j * share, share) for h in range(2) for m in cols] for j in spans]

time: 192 us -> 190 us (0.990)
  waiting for transfers between devices: 75.1 us -> 72.1 us
    ppermute x18, waiting for transfers between devices: 62.2 us -> 59.5 us  [swap(): lax.ppermute(pieces[k], axis, [(i, i ^ k) for i in range(total)])]
  transfers between devices with their start and end apart: 38 -> 38, of which waited for: 15 -> 16; matrix products, arithmetic and copies ran while one was open for 4% -> 5% of each run, Pallas kernels for 26% -> 26%
where the time goes in v4:
time: 190 us; the launch traced here: 188 us
  waiting for transfers between devices  72.1 us (38%)
  Pallas kernels  53.5 us (28%)
  starting transfers between devices  43.3 us (23%)
  local copies, waits for them, and re-layouts  16.1 us (8%)
  other arithmetic  1.95 us (1%)
    ppermute x18, waiting for transfers between devices, swap(): lax.ppermute(pieces[k], axis, [(i, i ^ k) for i in range(total)])  59.5 us
    ppermute x18, starting transfers between devices, swap(): lax.ppermute(pieces[k], axis, [(i, i ^ k) for i in range(total)])  18.1 us
    pallas_call x1, Pallas kernels, pair_stage(): pl.pallas_call(functools.partial(pair_kernel, total_rows, total_cols), gr...  17 us
    ppermute x15, starting transfers between devices, over_chips(): lax.ppermute(piece, 'row', [(i, i ^ k) for i in range(row_total)])  15.3 us
    pallas_call x1, Pallas kernels, attend(): pl.pallas_call(functools.partial(attention_kernel, total_cols, heads), gr...  11.7 us
    ppermute x15, waiting for transfers between devices, over_chips(): lax.ppermute(piece, 'row', [(i, i ^ k) for i in range(row_total)])  10.8 us
    pallas_call x1, Pallas kernels, triangle(): pl.pallas_call(functools.partial(triangle_kernel, total_rows, total_cols)...  10 us
    ppermute x5, starting transfers between devices, other_core(): return lax.ppermute(block, 'row', [(i, i ^ 1) for i in range(row_total)])  9.8 us
  transfers between devices with their start and end apart: 38, of which 16 were waited for; matrix products, arithmetic and copies ran while one was open for 5% of the time, Pallas kernels for 26%

profile of v4, /device:TPU:9, one launch (start us, length us, event | category | flops | bytes accessed | tf_op | source)
XLA Modules:
  0.0 188.4 jit_solution(12493270723542796142)
XLA Ops:
  2.2 1.0 outer_operands.1
  3.3 2.4 %collective-permute-start.1 = (bf16[23,16,128]{2,1,0:T(8,128)(2,1)S(1)}, bf16[23,16,128]{2,1,0:T(8,128)(2,1)S(1)}, u32[]{:S(2)}, u32[]{:S(2)}) collective-permute-start(bf16[23,16,128]{2,1,0:T(8,128)(2,1)S(1)} %get-tuple-element.77), channel_id=1, source_target_pairs={{0,2},{1,3},{2,0},{3,1},{4,6},{5,7},{6,4},{7,5},{8,10},{9,11},{10,... | collective-permute-start | bytes 282632 | tf_op jit(solution)/shard_map/ppermute | solution.py:22
  5.7 1.3 collective-permute-start
  6.9 1.2 collective-permute-start.7
  8.1 1.2 collective-permute-start.8
  12.1 2.2 %collective-permute-start.9 = (bf16[33,16,128]{2,1,0:T(8,128)(2,1)S(1)}, bf16[33,16,128]{2,1,0:T(8,128)(2,1)S(1)}, u32[]{:S(2)}, u32[]{:S(2)}) collective-permute-start(bf16[33,16,128]{2,1,0:T(8,128)(2,1)S(1)} %get-tuple-element.78), channel_id=1, source_target_pairs={{0,24},{4,28},{8,16},{12,20},{16,8},{20,12},{24,0},{28,4},{1,25},{... | collective-permute-start | bytes 405512 | tf_op jit(solution)/shard_map/ppermute | solution.py:710
  14.3 1.1 collective-permute-start.3
  15.5 1.2 collective-permute-start.4
  17.2 3.8 %collective-permute-start.10 = (bf16[132,16,128]{2,1,0:T(8,128)(2,1)S(1)}, bf16[132,16,128]{2,1,0:T(8,128)(2,1)S(1)}, u32[]{:S(2)}, u32[]{:S(2)}) collective-permute-start(bf16[132,16,128]{2,1,0:T(8,128)(2,1)S(1)} %constant_dynamic-update-slice_fusion.refs_3_), channel_id=1, source_target_pairs={{0,4},{4,0},{8,12},{12,8},{16,20},{20,16},{24,28},{28,24},{1,5},{5... | collective-permute-start | bytes 1622024 | tf_op jit(solution)/shard_map/ppermute | solution.py:715
  21.4 1.0 collective-permute-done.5
  22.4 1.6 collective-permute-start.6
  24.8 1.1 copy.43
  28.4 2.7 %collective-permute-start.15 = (bf16[4,88,256]{2,1,0:T(8,128)(2,1)S(1)}, bf16[4,88,256]{2,1,0:T(8,128)(2,1)S(1)}, u32[]{:S(2)}, u32[]{:S(2)}) collective-permute-start(bf16[4,88,256]{2,1,0:T(8,128)(2,1)S(1)} %get-tuple-element.157), channel_id=1, source_target_pairs={{0,2},{1,3},{2,0},{3,1},{4,6},{5,7},{6,4},{7,5},{8,10},{9,11},{10,... | collective-permute-start | bytes 540680 | tf_op jit(solution)/shard_map/ppermute | solution.py:22
  31.8 17.0 %pair_update.1 = (f32[3872,128]{1,0:T(8,128)}, bf16[3872,128]{1,0:T(8,128)(2,1)}, bf16[40,3872]{1,0:T(8,128)(2,1)}, bf16[40,3872]{1,0:T(8,128)(2,1)}, bf16[40,38...) custom-call(s32[4,44]{1,0:T(4,128)} %add_add_fusion.refs_0_, ...), custom_call_target="tpu_custom_call" | custom-call | tf_op jit(solution)/shard_map/pair_update/pallas_call | solution.py:287
  49.7 0.9 collective-permute-start.11
  50.7 2.1 %collective-permute-start.12 = (bf16[40,3872]{1,0:T(8,128)(2,1)}, bf16[40,3872]{1,0:T(8,128)(2,1)S(1)}, u32[]{:S(2)}, u32[]{:S(2)}) collective-permute-start(bf16[40,3872]{1,0:T(8,128)(2,1)} %get-tuple-element.85), channel_id=1, source_target_pairs={{0,2},{1,3},{2,0},{3,1},{4,6},{5,7},{6,4},{7,5},{8,10},{9,11},{10,... | collective-permute-start | bytes 929288 | tf_op jit(solution)/shard_map/ppermute | solution.py:22
  53.1 11.1 %collective-permute-done.11.refs_1_ = bf16[40,3872]{1,0:T(8,128)(2,1)S(1)} collective-permute-done((bf16[40,3872]{1,0:T(8,128)(2,1)}, bf16[40,3872]{1,0:T(8,128)(2,1)S(1)}, u32[]{:S(2)}, u32[]{:S(2)}) %collective-permute-start.11) | collective-permute-done | bytes 309792 | tf_op jit(solution)/shard_map/ppermute | solution.py:22
  64.3 9.2 %collective-permute-done.12.refs_2_ = bf16[40,3872]{1,0:T(8,128)(2,1)S(1)} collective-permute-done((bf16[40,3872]{1,0:T(8,128)(2,1)}, bf16[40,3872]{1,0:T(8,128)(2,1)S(1)}, u32[]{:S(2)}, u32[]{:S(2)}) %collective-permute-start.12) | collective-permute-done | bytes 309792 | tf_op jit(solution)/shard_map/ppermute | solution.py:22
  73.5 7.9 %collective-permute-done.13.refs_3_ = bf16[40,3872]{1,0:T(8,128)(2,1)S(1)} collective-permute-done((bf16[40,3872]{1,0:T(8,128)(2,1)}, bf16[40,3872]{1,0:T(8,128)(2,1)S(1)}, u32[]{:S(2)}, u32[]{:S(2)}) %collective-permute-start.13) | collective-permute-done | bytes 309792 | tf_op jit(solution)/shard_map/ppermute | solution.py:22
  81.5 1.3 collective-permute-start.18
  82.8 1.2 collective-permute-start.19
  84.2 2.2 %collective-permute-start.22 = (bf16[32,3872]{1,0:T(8,128)(2,1)S(1)}, bf16[32,3872]{1,0:T(8,128)(2,1)S(1)}, u32[]{:S(2)}, u32[]{:S(2)}) collective-permute-start(bf16[32,3872]{1,0:T(8,128)(2,1)S(1)} %get-tuple-element.100), channel_id=1, source_target_pairs={{0,2},{1,3},{2,0},{3,1},{4,6},{5,7},{6,4},{7,5},{8,10},{9,11},{10,... | collective-permute-start | bytes 743432 | tf_op jit(solution)/shard_map/ppermute | solution.py:22
  86.4 1.7 collective-permute-done.21.refs_1_
  89.0 12.8 %collective-permute-done.22.refs_2_ = bf16[32,3872]{1,0:T(8,128)(2,1)S(1)} collective-permute-done((bf16[32,3872]{1,0:T(8,128)(2,1)S(1)}, bf16[32,3872]{1,0:T(8,128)(2,1)S(1)}, u32[]{:S(2)}, u32[]{:S(2)}) %collective-permute-start.22) | collective-permute-done | bytes 247840 | tf_op jit(solution)/shard_map/ppermute | solution.py:22
  101.8 6.4 %collective-permute-done.23.refs_3_ = bf16[32,3872]{1,0:T(8,128)(2,1)S(1)} collective-permute-done((bf16[32,3872]{1,0:T(8,128)(2,1)S(1)}, bf16[32,3872]{1,0:T(8,128)(2,1)S(1)}, u32[]{:S(2)}, u32[]{:S(2)}) %collective-permute-start.23) | collective-permute-done | bytes 247840 | tf_op jit(solution)/shard_map/ppermute | solution.py:22
  109.2 1.2 collective-permute-start.24
  110.4 1.2 collective-permute-start.25
  111.9 3.0 %collective-permute-done.24.refs_4_ = bf16[32,3872]{1,0:T(8,128)(2,1)S(1)} collective-permute-done((bf16[32,3872]{1,0:T(8,128)(2,1)S(1)}, bf16[32,3872]{1,0:T(8,128)(2,1)S(1)}, u32[]{:S(2)}, u32[]{:S(2)}) %collective-permute-start.24) | collective-permute-done | bytes 247840 | tf_op jit(solution)/shard_map/ppermute | solution.py:710
  114.8 1.6 collective-permute-done.25.refs_6_
  116.4 4.8 %collective-permute-done.26.refs_8_ = bf16[32,3872]{1,0:T(8,128)(2,1)S(1)} collective-permute-done((bf16[32,3872]{1,0:T(8,128)(2,1)S(1)}, bf16[32,3872]{1,0:T(8,128)(2,1)S(1)}, u32[]{:S(2)}, u32[]{:S(2)}) %collective-permute-start.26) | collective-permute-done | bytes 247840 | tf_op jit(solution)/shard_map/ppermute | solution.py:710
  122.0 1.4 copy.48
  123.4 3.4 %collective-permute-start.27 = (bf16[128,3872]{0,1:T(8,128)(2,1)}, bf16[128,3872]{0,1:T(8,128)(2,1)}, u32[]{:S(2)}, u32[]{:S(2)}) collective-permute-start(bf16[128,3872]{0,1:T(8,128)(2,1)} %copy.48), channel_id=1, source_target_pairs={{0,4},{4,0},{8,12},{12,8},{16,20},{20,16},{24,28},{28,24},{1,5},{5... | collective-permute-start | bytes 2973704 | tf_op jit(solution)/shard_map/ppermute | solution.py:715
  127.4 10.0 %triangle.1 = (bf16[4,4,3872]{2,1,0:T(4,128)(2,1)}, bf16[4,4,3872]{2,1,0:T(4,128)(2,1)}, bf16[4,4,3872]{2,1,0:T(4,128)(2,1)}, bf16[4,4,3872]{2,1,0:T(4,128)(2,1)}, bf16[4,4,4,3872]{3,2,1,0:T(4,128)(2,1)}) custom-call(s32[8]{0:T(128)} %fusion.7.refs_0_, bf16[64,3872]{1,0:T(8,128)(2,1)} %copy-done.1, bf16[32,3872]{1,0:T(8,128)(2,1)} %copy-done.9, ...), custom_call_target="tpu_custom_call" | custom-call | tf_op jit(solution)/shard_map/triangle/pallas_call | solution.py:586
  137.8 1.8 collective-permute-done.31
  139.8 1.0 regroup.8
  141.5 2.4 %collective-permute-start.33 = (bf16[32,3872]{1,0:T(8,128)(2,1)}, bf16[32,3872]{1,0:T(8,128)(2,1)}, u32[]{:S(2)}, u32[]{:S(2)}) collective-permute-start(bf16[32,3872]{1,0:T(8,128)(2,1)} %get-tuple-element.140), channel_id=1, source_target_pairs={{0,2},{1,3},{2,0},{3,1},{4,6},{5,7},{6,4},{7,5},{8,10},{9,11},{10,... | collective-permute-start | bytes 743432 | tf_op jit(solution)/shard_map/ppermute | solution.py:22
  144.2 1.6 copy.49.refs_2_
  145.8 5.3 %layout_bias.1.refs_0_ = bf16[3,2816,128]{2,1,0:T(8,128)(2,1)S(1)} custom-call(s32[8]{0:T(128)S(1)} %copy-done.29, bf16[128,3872]{1,0:T(8,128)(2,1)S(1)} %regroup.7.refs_1_, bf16[128,3872]{1,0:T(8,128)(2,1)S(1)} %copy.49.refs_2_), custom_call_target="tpu_custom_call" | custom-call | tf_op jit(solution)/shard_map/layout_bias/pallas_call | solution.py:362
  151.3 11.7 %row_attention.1 = (bf16[4,88,256]{2,1,0:T(8,128)(2,1)S(1)}, bf16[4,88,256]{2,1,0:T(8,128)(2,1)S(1)}, bf16[4,88,256]{2,1,0:T(8,128)(2,1)}, bf16[4,88,256]{2,1,0:T(8,128)(2,1)}) custom-call(bf16[3,2816,128]{2,1,0:T(8,128)(2,1)S(1)} %layout_bias.1.refs_0_, bf16[4,88,256]{2,1,0:T(8,128)(2,1)S(1)} %copy-done.7, bf16[4,88,256]{2,1,0:T(8,128)(2,1)S(1)} %copy-done.17, ...), custom_call_target="tpu_custom_call" | custom-call | tf_op jit(solution)/shard_map/row_attention/pallas_call | solution.py:454
  163.0 1.0 collective-permute-start.28
  164.0 1.5 collective-permute-start.29
  166.6 2.2 %regroup.9 = (bf16[32,3872]{1,0:T(8,128)(2,1)S(1)}, bf16[32,3872]{1,0:T(8,128)(2,1)}, bf16[32,3872]{1,0:T(8,128)(2,1)}, bf16[32,3872]{1,0:T(8,128)(2,1)}) custom-call(bf16[32,3872]{1,0:T(8,128)(2,1)S(1)} %copy-done.11, bf16[32,3872]{1,0:T(8,128)(2,1)} %collective-permute-done.32.refs_1_, bf16[32,3872]{1,0:T(8,128)(2,1)} %collective-permute-done.33.refs_2_, ...), custom_call_target="tpu_custom_call" | custom-call | tf_op jit(solution)/shard_map/regroup/pallas_call | solution.py:486
  171.0 1.2 collective-permute-start.37
  172.3 4.5 %collective-permute-done.29.refs_2_ = bf16[4,88,256]{2,1,0:T(8,128)(2,1)} collective-permute-done((bf16[4,88,256]{2,1,0:T(8,128)(2,1)}, bf16[4,88,256]{2,1,0:T(8,128)(2,1)}, u32[]{:S(2)}, u32[]{:S(2)}) %collective-permute-start.29) | collective-permute-done | bytes 180256 | tf_op jit(solution)/shard_map/ppermute | solution.py:22
  176.8 4.7 %collective-permute-done.30.refs_3_ = bf16[4,88,256]{2,1,0:T(8,128)(2,1)} collective-permute-done((bf16[4,88,256]{2,1,0:T(8,128)(2,1)}, bf16[4,88,256]{2,1,0:T(8,128)(2,1)}, u32[]{:S(2)}, u32[]{:S(2)}) %collective-permute-start.30) | collective-permute-done | bytes 180256 | tf_op jit(solution)/shard_map/ppermute | solution.py:22
  181.5 0.9 copy-done.13
  183.3 1.9 %place_sequences.1 = bf16[16,88,256]{2,1,0:T(8,128)(2,1)} custom-call(s32[4]{0:T(128)S(1)} %broadcast_multiply_fusion.start_ref, bf16[4,88,256]{2,1,0:T(8,128)(2,1)S(1)} %copy-done.13, bf16[4,88,256]{2,1,0:T(8,128)(2,1)S(1)} %copy-done.15, bf16[4,88,256]{2,1,0:T(8,128)(2,1)} %collective-permute-done.29.refs_2_, ...), custom_call_target="tpu_custom_call" | custom-call | tf_op jit(solution)/shard_map/place_sequences/pallas_call | solution.py:652
  185.3 3.1 %pair_finish.1 = bf16[3872,128]{1,0:T(8,128)(2,1)} custom-call(s32[32]{0:T(128)S(1)} %add.136.refs_0_, bf16[32,3872]{1,0:T(8,128)(2,1)S(1)} %get-tuple-element.146.refs_1_, bf16[32,3872]{1,0:T(8,128)(2,1)S(1)} %collective-permute-done.35.refs_2_, bf16[32,3872]{1,0:T(8,128)(2,1)} %collective-permute-done.36.refs_3_, ...), custom_call_target="tpu_custom_call" | custom-call | tf_op jit(solution)/shard_map/pair_finish/pallas_call | solution.py:632
  (187 shorter events, 19.9 us)
Async XLA Ops:
  3.3 8.8 %collective-permute-start.1 = (bf16[23,16,128]{2,1,0:T(8,128)(2,1)S(1)}, bf16[23,16,128]{2,1,0:T(8,128)(2,1)S(1)}, u32[]{:S(2)}, u32[]{:S(2)}) collective-permute-start(bf16[23,16,128]{2,1,0:T(8,128)(2,1)S(1)} %get-tuple-element.77), channel_id=1, source_target_pairs={{0,2},{1,3},{2,0},{3,1},{4,6},{5,7},{6,4},{7,5},{8,10},{9,11},{10,... | collective-permute-start | bytes 282632 | tf_op jit(solution)/shard_map/ppermute | solution.py:22
  5.7 8.6 %collective-permute-start.2 = (bf16[23,16,128]{2,1,0:T(8,128)(2,1)S(1)}, bf16[23,16,128]{2,1,0:T(8,128)(2,1)S(1)}, u32[]{:S(2)}, u32[]{:S(2)}) collective-permute-start(bf16[23,16,128]{2,1,0:T(8,128)(2,1)S(1)} %get-tuple-element.77), channel_id=1, source_target_pairs={{0,3},{1,2},{2,1},{3,0},{4,7},{5,6},{6,5},{7,4},{8,11},{9,10},{10,... | collective-permute-start | bytes 282632 | tf_op jit(solution)/shard_map/ppermute | solution.py:22
  5.7 8.6 %collective-permute-start = (bf16[23,16,128]{2,1,0:T(8,128)(2,1)S(1)}, bf16[23,16,128]{2,1,0:T(8,128)(2,1)S(1)}, u32[]{:S(2)}, u32[]{:S(2)}) collective-permute-start(bf16[23,16,128]{2,1,0:T(8,128)(2,1)S(1)} %get-tuple-element.77), channel_id=1, source_target_pairs={{0,1},{1,0},{2,3},{3,2},{4,5},{5,4},{6,7},{7,6},{8,9},{9,8},{10,11... | collective-permute-start | bytes 282632 | tf_op jit(solution)/shard_map/ppermute | solution.py:22
  6.9 9.8 %collective-permute-start.7 = (bf16[33,16,128]{2,1,0:T(8,128)(2,1)S(1)}, bf16[33,16,128]{2,1,0:T(8,128)(2,1)S(1)}, u32[]{:S(2)}, u32[]{:S(2)}) collective-permute-start(bf16[33,16,128]{2,1,0:T(8,128)(2,1)S(1)} %get-tuple-element.78), channel_id=1, source_target_pairs={{0,8},{4,12},{8,0},{12,4},{16,24},{20,28},{24,16},{28,20},{1,9},{5... | collective-permute-start | bytes 405512 | tf_op jit(solution)/shard_map/ppermute | solution.py:710
  8.1 8.9 %collective-permute-start.8 = (bf16[33,16,128]{2,1,0:T(8,128)(2,1)S(1)}, bf16[33,16,128]{2,1,0:T(8,128)(2,1)S(1)}, u32[]{:S(2)}, u32[]{:S(2)}) collective-permute-start(bf16[33,16,128]{2,1,0:T(8,128)(2,1)S(1)} %get-tuple-element.78), channel_id=1, source_target_pairs={{0,16},{4,20},{8,24},{12,28},{16,0},{20,4},{24,8},{28,12},{1,17},{... | collective-permute-start | bytes 405512 | tf_op jit(solution)/shard_map/ppermute | solution.py:710
  12.1 5.1 %collective-permute-start.9 = (bf16[33,16,128]{2,1,0:T(8,128)(2,1)S(1)}, bf16[33,16,128]{2,1,0:T(8,128)(2,1)S(1)}, u32[]{:S(2)}, u32[]{:S(2)}) collective-permute-start(bf16[33,16,128]{2,1,0:T(8,128)(2,1)S(1)} %get-tuple-element.78), channel_id=1, source_target_pairs={{0,24},{4,28},{8,16},{12,20},{16,8},{20,12},{24,0},{28,4},{1,25},{... | collective-permute-start | bytes 405512 | tf_op jit(solution)/shard_map/ppermute | solution.py:710
  14.3 6.6 %collective-permute-start.3 = (bf16[23,16,128]{2,1,0:T(8,128)(2,1)S(1)}, bf16[23,16,128]{2,1,0:T(8,128)(2,1)S(1)}, u32[]{:S(2)}, u32[]{:S(2)}) collective-permute-start(bf16[23,16,128]{2,1,0:T(8,128)(2,1)S(1)} %get-tuple-element.167), channel_id=1, source_target_pairs={{0,8},{4,12},{8,0},{12,4},{16,24},{20,28},{24,16},{28,20},{1,9},{5... | collective-permute-start | bytes 282632 | tf_op jit(solution)/shard_map/ppermute | solution.py:710
  15.5 5.9 %collective-permute-start.4 = (bf16[23,16,128]{2,1,0:T(8,128)(2,1)S(1)}, bf16[23,16,128]{2,1,0:T(8,128)(2,1)S(1)}, u32[]{:S(2)}, u32[]{:S(2)}) collective-permute-start(bf16[23,16,128]{2,1,0:T(8,128)(2,1)S(1)} %get-tuple-element.166), channel_id=1, source_target_pairs={{0,16},{4,20},{8,24},{12,28},{16,0},{20,4},{24,8},{28,12},{1,17},{... | collective-permute-start | bytes 282632 | tf_op jit(solution)/shard_map/ppermute | solution.py:710
  16.7 5.7 %collective-permute-start.5 = (bf16[23,16,128]{2,1,0:T(8,128)(2,1)S(1)}, bf16[23,16,128]{2,1,0:T(8,128)(2,1)S(1)}, u32[]{:S(2)}, u32[]{:S(2)}) collective-permute-start(bf16[23,16,128]{2,1,0:T(8,128)(2,1)S(1)} %get-tuple-element.165), channel_id=1, source_target_pairs={{0,24},{4,28},{8,16},{12,20},{16,8},{20,12},{24,0},{28,4},{1,25},{... | collective-permute-start | bytes 282632 | tf_op jit(solution)/shard_map/ppermute | solution.py:710
  17.2 10.4 %collective-permute-start.10 = (bf16[132,16,128]{2,1,0:T(8,128)(2,1)S(1)}, bf16[132,16,128]{2,1,0:T(8,128)(2,1)S(1)}, u32[]{:S(2)}, u32[]{:S(2)}) collective-permute-start(bf16[132,16,128]{2,1,0:T(8,128)(2,1)S(1)} %constant_dynamic-update-slice_fusion.refs_3_), channel_id=1, source_target_pairs={{0,4},{4,0},{8,12},{12,8},{16,20},{20,16},{24,28},{28,24},{1,5},{5... | collective-permute-start | bytes 1622024 | tf_op jit(solution)/shard_map/ppermute | solution.py:715
  22.4 5.1 %collective-permute-start.6 = (bf16[92,16,128]{2,1,0:T(8,128)(2,1)S(1)}, bf16[92,16,128]{2,1,0:T(8,128)(2,1)S(1)}, u32[]{:S(2)}, u32[]{:S(2)}) collective-permute-start(bf16[92,16,128]{2,1,0:T(8,128)(2,1)S(1)} %pad_maximum_fusion.2.refs_1_), channel_id=1, source_target_pairs={{0,4},{4,0},{8,12},{12,8},{16,20},{20,16},{24,28},{28,24},{1,5},{5... | collective-permute-start | bytes 1130504 | tf_op jit(solution)/shard_map/ppermute | solution.py:715
  28.4 20.3 %collective-permute-start.14 = (bf16[4,88,256]{2,1,0:T(8,128)(2,1)S(1)}, bf16[4,88,256]{2,1,0:T(8,128)(2,1)S(1)}, u32[]{:S(2)}, u32[]{:S(2)}) collective-permute-start(bf16[4,88,256]{2,1,0:T(8,128)(2,1)S(1)} %get-tuple-element.158), channel_id=1, source_target_pairs={{0,1},{1,0},{2,3},{3,2},{4,5},{5,4},{6,7},{7,6},{8,9},{9,8},{10,11... | collective-permute-start | bytes 540680 | tf_op jit(solution)/shard_map/ppermute | solution.py:22
  28.4 20.3 %collective-permute-start.15 = (bf16[4,88,256]{2,1,0:T(8,128)(2,1)S(1)}, bf16[4,88,256]{2,1,0:T(8,128)(2,1)S(1)}, u32[]{:S(2)}, u32[]{:S(2)}) collective-permute-start(bf16[4,88,256]{2,1,0:T(8,128)(2,1)S(1)} %get-tuple-element.157), channel_id=1, source_target_pairs={{0,2},{1,3},{2,0},{3,1},{4,6},{5,7},{6,4},{7,5},{8,10},{9,11},{10,... | collective-permute-start | bytes 540680 | tf_op jit(solution)/shard_map/ppermute | solution.py:22
  31.1 17.7 %collective-permute-start.16 = (bf16[4,88,256]{2,1,0:T(8,128)(2,1)S(1)}, bf16[4,88,256]{2,1,0:T(8,128)(2,1)S(1)}, u32[]{:S(2)}, u32[]{:S(2)}) collective-permute-start(bf16[4,88,256]{2,1,0:T(8,128)(2,1)S(1)} %get-tuple-element.156), channel_id=1, source_target_pairs={{0,3},{1,2},{2,1},{3,0},{4,7},{5,6},{6,5},{7,4},{8,11},{9,10},{10,... | collective-permute-start | bytes 540680 | tf_op jit(solution)/shard_map/ppermute | solution.py:22
  48.7 32.6 %copy-start.8 = (bf16[40,3872]{1,0:T(8,128)(2,1)S(1)}, bf16[40,3872]{1,0:T(8,128)(2,1)}, u32[]{:S(2)}) copy-start(bf16[40,3872]{1,0:T(8,128)(2,1)} %get-tuple-element.90.refs_0_) | copy-start | bytes 929284
  48.8 59.6 %copy-start.16 = (bf16[4,88,256]{2,1,0:T(8,128)(2,1)}, bf16[4,88,256]{2,1,0:T(8,128)(2,1)S(1)}, u32[]{:S(2)}) copy-start(bf16[4,88,256]{2,1,0:T(8,128)(2,1)S(1)} %collective-permute-done.14.refs_2_) | copy-start | bytes 540676
  48.8 59.6 %copy-start.18 = (bf16[4,88,256]{2,1,0:T(8,128)(2,1)}, bf16[4,88,256]{2,1,0:T(8,128)(2,1)S(1)}, u32[]{:S(2)}) copy-start(bf16[4,88,256]{2,1,0:T(8,128)(2,1)S(1)} %collective-permute-done.15.refs_3_) | copy-start | bytes 540676
  48.8 59.6 %copy-start.20 = (bf16[4,88,256]{2,1,0:T(8,128)(2,1)}, bf16[4,88,256]{2,1,0:T(8,128)(2,1)S(1)}, u32[]{:S(2)}) copy-start(bf16[4,88,256]{2,1,0:T(8,128)(2,1)S(1)} %collective-permute-done.16.refs_4_) | copy-start | bytes 540676
  48.8 4.2 %collective-permute-start.17 = (bf16[4,32,3872]{2,1,0:T(8,128)(2,1)}, bf16[4,32,3872]{2,1,0:T(8,128)(2,1)S(1)}, u32[]{:S(2)}, u32[]{:S(2)}) collective-permute-start(bf16[4,32,3872]{2,1,0:T(8,128)(2,1)} %get-tuple-element.89), channel_id=1, source_target_pairs={{0,4},{4,0},{8,12},{12,8},{16,20},{20,16},{24,28},{28,24},{1,5},{5... | collective-permute-start | bytes 2973704 | tf_op jit(solution)/shard_map/ppermute | solution.py:715
  49.7 14.6 %collective-permute-start.11 = (bf16[40,3872]{1,0:T(8,128)(2,1)}, bf16[40,3872]{1,0:T(8,128)(2,1)S(1)}, u32[]{:S(2)}, u32[]{:S(2)}) collective-permute-start(bf16[40,3872]{1,0:T(8,128)(2,1)} %get-tuple-element.84), channel_id=1, source_target_pairs={{0,1},{1,0},{2,3},{3,2},{4,5},{5,4},{6,7},{7,6},{8,9},{9,8},{10,11... | collective-permute-start | bytes 929288 | tf_op jit(solution)/shard_map/ppermute | solution.py:22
  50.7 22.8 %collective-permute-start.12 = (bf16[40,3872]{1,0:T(8,128)(2,1)}, bf16[40,3872]{1,0:T(8,128)(2,1)S(1)}, u32[]{:S(2)}, u32[]{:S(2)}) collective-permute-start(bf16[40,3872]{1,0:T(8,128)(2,1)} %get-tuple-element.85), channel_id=1, source_target_pairs={{0,2},{1,3},{2,0},{3,1},{4,6},{5,7},{6,4},{7,5},{8,10},{9,11},{10,... | collective-permute-start | bytes 929288 | tf_op jit(solution)/shard_map/ppermute | solution.py:22
  52.8 28.6 %collective-permute-start.13 = (bf16[40,3872]{1,0:T(8,128)(2,1)}, bf16[40,3872]{1,0:T(8,128)(2,1)S(1)}, u32[]{:S(2)}, u32[]{:S(2)}) collective-permute-start(bf16[40,3872]{1,0:T(8,128)(2,1)} %get-tuple-element.86), channel_id=1, source_target_pairs={{0,3},{1,2},{2,1},{3,0},{4,7},{5,6},{6,5},{7,4},{8,11},{9,10},{10,... | collective-permute-start | bytes 929288 | tf_op jit(solution)/shard_map/ppermute | solution.py:22
  81.3 6.8 %collective-permute-start.21 = (bf16[32,3872]{1,0:T(8,128)(2,1)S(1)}, bf16[32,3872]{1,0:T(8,128)(2,1)S(1)}, u32[]{:S(2)}, u32[]{:S(2)}) collective-permute-start(bf16[32,3872]{1,0:T(8,128)(2,1)S(1)} %get-tuple-element.99), channel_id=1, source_target_pairs={{0,1},{1,0},{2,3},{3,2},{4,5},{5,4},{6,7},{7,6},{8,9},{9,8},{10,11... | collective-permute-start | bytes 743432 | tf_op jit(solution)/shard_map/ppermute | solution.py:22
  81.5 41.9 %copy-start.1 = (bf16[64,3872]{1,0:T(8,128)(2,1)}, bf16[64,3872]{1,0:T(8,128)(2,1)S(1)}, u32[]{:S(2)}) copy-start(bf16[64,3872]{1,0:T(8,128)(2,1)S(1)} %get-tuple-element.114.refs_0_.refs_1_) | copy-start | bytes 1486852
  81.5 26.8 %collective-permute-start.18 = (bf16[64,3872]{1,0:T(8,128)(2,1)S(1)}, bf16[64,3872]{1,0:T(8,128)(2,1)S(1)}, u32[]{:S(2)}, u32[]{:S(2)}) collective-permute-start(bf16[64,3872]{1,0:T(8,128)(2,1)S(1)} %get-tuple-element.95), channel_id=1, source_target_pairs={{0,8},{4,12},{8,0},{12,4},{16,24},{20,28},{24,16},{28,20},{1,9},{5... | collective-permute-start | bytes 1486856 | tf_op jit(solution)/shard_map/ppermute | solution.py:710
  82.8 25.5 %collective-permute-start.19 = (bf16[64,3872]{1,0:T(8,128)(2,1)S(1)}, bf16[64,3872]{1,0:T(8,128)(2,1)S(1)}, u32[]{:S(2)}, u32[]{:S(2)}) collective-permute-start(bf16[64,3872]{1,0:T(8,128)(2,1)S(1)} %get-tuple-element.96), channel_id=1, source_target_pairs={{0,16},{4,20},{8,24},{12,28},{16,0},{20,4},{24,8},{28,12},{1,17},{... | collective-permute-start | bytes 1486856 | tf_op jit(solution)/shard_map/ppermute | solution.py:710
  84.0 24.3 %collective-permute-start.20 = (bf16[64,3872]{1,0:T(8,128)(2,1)S(1)}, bf16[64,3872]{1,0:T(8,128)(2,1)S(1)}, u32[]{:S(2)}, u32[]{:S(2)}) collective-permute-start(bf16[64,3872]{1,0:T(8,128)(2,1)S(1)} %get-tuple-element.97), channel_id=1, source_target_pairs={{0,24},{4,28},{8,16},{12,20},{16,8},{20,12},{24,0},{28,4},{1,25},{... | collective-permute-start | bytes 1486856 | tf_op jit(solution)/shard_map/ppermute | solution.py:710
  84.2 17.6 %collective-permute-start.22 = (bf16[32,3872]{1,0:T(8,128)(2,1)S(1)}, bf16[32,3872]{1,0:T(8,128)(2,1)S(1)}, u32[]{:S(2)}, u32[]{:S(2)}) collective-permute-start(bf16[32,3872]{1,0:T(8,128)(2,1)S(1)} %get-tuple-element.100), channel_id=1, source_target_pairs={{0,2},{1,3},{2,0},{3,1},{4,6},{5,7},{6,4},{7,5},{8,10},{9,11},{10,... | collective-permute-start | bytes 743432 | tf_op jit(solution)/shard_map/ppermute | solution.py:22
  88.1 20.1 %collective-permute-start.23 = (bf16[32,3872]{1,0:T(8,128)(2,1)S(1)}, bf16[32,3872]{1,0:T(8,128)(2,1)S(1)}, u32[]{:S(2)}, u32[]{:S(2)}) collective-permute-start(bf16[32,3872]{1,0:T(8,128)(2,1)S(1)} %get-tuple-element.101), channel_id=1, source_target_pairs={{0,3},{1,2},{2,1},{3,0},{4,7},{5,6},{6,5},{7,4},{8,11},{9,10},{10,... | collective-permute-start | bytes 743432 | tf_op jit(solution)/shard_map/ppermute | solution.py:22
  109.2 5.6 %collective-permute-start.24 = (bf16[32,3872]{1,0:T(8,128)(2,1)S(1)}, bf16[32,3872]{1,0:T(8,128)(2,1)S(1)}, u32[]{:S(2)}, u32[]{:S(2)}) collective-permute-start(bf16[32,3872]{1,0:T(8,128)(2,1)S(1)} %get-tuple-element.111), channel_id=1, source_target_pairs={{0,8},{4,12},{8,0},{12,4},{16,24},{20,28},{24,16},{28,20},{1,9},{5... | collective-permute-start | bytes 743432 | tf_op jit(solution)/shard_map/ppermute | solution.py:710
  110.4 6.0 %collective-permute-start.25 = (bf16[32,3872]{1,0:T(8,128)(2,1)S(1)}, bf16[32,3872]{1,0:T(8,128)(2,1)S(1)}, u32[]{:S(2)}, u32[]{:S(2)}) collective-permute-start(bf16[32,3872]{1,0:T(8,128)(2,1)S(1)} %get-tuple-element.112), channel_id=1, source_target_pairs={{0,16},{4,20},{8,24},{12,28},{16,0},{20,4},{24,8},{28,12},{1,17},{... | collective-permute-start | bytes 743432 | tf_op jit(solution)/shard_map/ppermute | solution.py:710
  111.7 9.5 %collective-permute-start.26 = (bf16[32,3872]{1,0:T(8,128)(2,1)S(1)}, bf16[32,3872]{1,0:T(8,128)(2,1)S(1)}, u32[]{:S(2)}, u32[]{:S(2)}) collective-permute-start(bf16[32,3872]{1,0:T(8,128)(2,1)S(1)} %get-tuple-element.113), channel_id=1, source_target_pairs={{0,24},{4,28},{8,16},{12,20},{16,8},{20,12},{24,0},{28,4},{1,25},{... | collective-permute-start | bytes 743432 | tf_op jit(solution)/shard_map/ppermute | solution.py:710
  122.0 15.5 %copy-start.39 = (bf16[256,256]{1,0:T(8,128)(2,1)S(1)}, bf16[256,256]{1,0:T(8,128)(2,1)}, u32[]{:S(2)}) copy-start(bf16[256,256]{1,0:T(8,128)(2,1)} %param.27) | copy-start | bytes 393220
  123.4 14.0 %collective-permute-start.27 = (bf16[128,3872]{0,1:T(8,128)(2,1)}, bf16[128,3872]{0,1:T(8,128)(2,1)}, u32[]{:S(2)}, u32[]{:S(2)}) collective-permute-start(bf16[128,3872]{0,1:T(8,128)(2,1)} %copy.48), channel_id=1, source_target_pairs={{0,4},{4,0},{8,12},{12,8},{16,20},{20,16},{24,28},{28,24},{1,5},{5... | collective-permute-start | bytes 2973704 | tf_op jit(solution)/shard_map/ppermute | solution.py:715
  137.4 2.2 %collective-permute-start.31 = (bf16[4,4,4,3872]{3,2,1,0:T(4,128)(2,1)}, bf16[4,4,4,3872]{3,2,1,0:T(4,128)(2,1)S(1)}, u32[]{:S(2)}, u32[]{:S(2)}) collective-permute-start(bf16[4,4,4,3872]{3,2,1,0:T(4,128)(2,1)} %get-tuple-element.137), channel_id=1, source_target_pairs={{0,4},{4,0},{8,12},{12,8},{16,20},{20,16},{24,28},{28,24},{1,5},{5... | collective-permute-start | bytes 1486856 | tf_op jit(solution)/shard_map/ppermute | solution.py:715
  141.5 24.0 %collective-permute-start.32 = (bf16[32,3872]{1,0:T(8,128)(2,1)}, bf16[32,3872]{1,0:T(8,128)(2,1)}, u32[]{:S(2)}, u32[]{:S(2)}) collective-permute-start(bf16[32,3872]{1,0:T(8,128)(2,1)} %get-tuple-element.139), channel_id=1, source_target_pairs={{0,1},{1,0},{2,3},{3,2},{4,5},{5,4},{6,7},{7,6},{8,9},{9,8},{10,11... | collective-permute-start | bytes 743432 | tf_op jit(solution)/shard_map/ppermute | solution.py:22
  141.5 24.3 %collective-permute-start.33 = (bf16[32,3872]{1,0:T(8,128)(2,1)}, bf16[32,3872]{1,0:T(8,128)(2,1)}, u32[]{:S(2)}, u32[]{:S(2)}) collective-permute-start(bf16[32,3872]{1,0:T(8,128)(2,1)} %get-tuple-element.140), channel_id=1, source_target_pairs={{0,2},{1,3},{2,0},{3,1},{4,6},{5,7},{6,4},{7,5},{8,10},{9,11},{10,... | collective-permute-start | bytes 743432 | tf_op jit(solution)/shard_map/ppermute | solution.py:22
  143.9 22.7 %collective-permute-start.34 = (bf16[32,3872]{1,0:T(8,128)(2,1)}, bf16[32,3872]{1,0:T(8,128)(2,1)}, u32[]{:S(2)}, u32[]{:S(2)}) collective-permute-start(bf16[32,3872]{1,0:T(8,128)(2,1)} %get-tuple-element.141), channel_id=1, source_target_pairs={{0,3},{1,2},{2,1},{3,0},{4,7},{5,6},{6,5},{7,4},{8,11},{9,10},{10,... | collective-permute-start | bytes 743432 | tf_op jit(solution)/shard_map/ppermute | solution.py:22
  151.3 34.0 %copy-start.5 = (f32[3872,128]{1,0:T(8,128)S(1)}, f32[3872,128]{1,0:T(8,128)}, u32[]{:S(2)}) copy-start(f32[3872,128]{1,0:T(8,128)} %get-tuple-element.151.refs_6_) | copy-start | bytes 5947396
  151.3 34.0 %copy-start.6 = (bf16[3872,128]{1,0:T(8,128)(2,1)S(1)}, bf16[3872,128]{1,0:T(8,128)(2,1)}, u32[]{:S(2)}) copy-start(bf16[3872,128]{1,0:T(8,128)(2,1)} %get-tuple-element.150.refs_5_) | copy-start | bytes 2973700
  163.0 22.2 %copy-start.27 = (bf16[128,128]{1,0:T(8,128)(2,1)S(1)}, bf16[128,128]{1,0:T(8,128)(2,1)}, u32[]{:S(2)}) copy-start(bf16[128,128]{1,0:T(8,128)(2,1)} %refs_7_.3) | copy-start | bytes 98308
  163.0 22.3 %copy-start.28 = (bf16[128,128]{1,0:T(8,128)(2,1)S(1)}, bf16[128,128]{1,0:T(8,128)(2,1)}, u32[]{:S(2)}) copy-start(bf16[128,128]{1,0:T(8,128)(2,1)} %param.33) | copy-start | bytes 98308
  163.0 7.3 %collective-permute-start.28 = (bf16[4,88,256]{2,1,0:T(8,128)(2,1)S(1)}, bf16[4,88,256]{2,1,0:T(8,128)(2,1)S(1)}, u32[]{:S(2)}, u32[]{:S(2)}) collective-permute-start(bf16[4,88,256]{2,1,0:T(8,128)(2,1)S(1)} %get-tuple-element.130), channel_id=1, source_target_pairs={{0,1},{1,0},{2,3},{3,2},{4,5},{5,4},{6,7},{7,6},{8,9},{9,8},{10,11... | collective-permute-start | bytes 540680 | tf_op jit(solution)/shard_map/ppermute | solution.py:22
  164.0 12.8 %collective-permute-start.29 = (bf16[4,88,256]{2,1,0:T(8,128)(2,1)}, bf16[4,88,256]{2,1,0:T(8,128)(2,1)}, u32[]{:S(2)}, u32[]{:S(2)}) collective-permute-start(bf16[4,88,256]{2,1,0:T(8,128)(2,1)} %get-tuple-element.131), channel_id=1, source_target_pairs={{0,2},{1,3},{2,0},{3,1},{4,6},{5,7},{6,4},{7,5},{8,10},{9,11},{10,... | collective-permute-start | bytes 540680 | tf_op jit(solution)/shard_map/ppermute | solution.py:22
  165.5 16.0 %collective-permute-start.30 = (bf16[4,88,256]{2,1,0:T(8,128)(2,1)}, bf16[4,88,256]{2,1,0:T(8,128)(2,1)}, u32[]{:S(2)}, u32[]{:S(2)}) collective-permute-start(bf16[4,88,256]{2,1,0:T(8,128)(2,1)} %get-tuple-element.132), channel_id=1, source_target_pairs={{0,3},{1,2},{2,1},{3,0},{4,7},{5,6},{6,5},{7,4},{8,11},{9,10},{10,... | collective-permute-start | bytes 540680 | tf_op jit(solution)/shard_map/ppermute | solution.py:22
  168.8 16.4 %collective-permute-start.35 = (bf16[32,3872]{1,0:T(8,128)(2,1)}, bf16[32,3872]{1,0:T(8,128)(2,1)S(1)}, u32[]{:S(2)}, u32[]{:S(2)}) collective-permute-start(bf16[32,3872]{1,0:T(8,128)(2,1)} %get-tuple-element.147), channel_id=1, source_target_pairs={{0,8},{4,12},{8,0},{12,4},{16,24},{20,28},{24,16},{28,20},{1,9},{5... | collective-permute-start | bytes 743432 | tf_op jit(solution)/shard_map/ppermute | solution.py:710
  169.7 15.6 %collective-permute-start.36 = (bf16[32,3872]{1,0:T(8,128)(2,1)}, bf16[32,3872]{1,0:T(8,128)(2,1)}, u32[]{:S(2)}, u32[]{:S(2)}) collective-permute-start(bf16[32,3872]{1,0:T(8,128)(2,1)} %get-tuple-element.148), channel_id=1, source_target_pairs={{0,16},{4,20},{8,24},{12,28},{16,0},{20,4},{24,8},{28,12},{1,17},{... | collective-permute-start | bytes 743432 | tf_op jit(solution)/shard_map/ppermute | solution.py:710
  171.0 14.3 %collective-permute-start.37 = (bf16[32,3872]{1,0:T(8,128)(2,1)}, bf16[32,3872]{1,0:T(8,128)(2,1)}, u32[]{:S(2)}, u32[]{:S(2)}) collective-permute-start(bf16[32,3872]{1,0:T(8,128)(2,1)} %get-tuple-element.149), channel_id=1, source_target_pairs={{0,24},{4,28},{8,16},{12,20},{16,8},{20,12},{24,0},{28,4},{1,25},{... | collective-permute-start | bytes 743432 | tf_op jit(solution)/shard_map/ppermute | solution.py:710
  (36 other events, 233.8 us)

commit v5 on v4

--- a/solution.py
+++ b/solution.py
@@ -314,6 +314,7 @@
     count = high // total_cols
     rows = pairs // places
     residues = rows * total
+    pitch = tiles.shape[1] // count
     lane = lax.broadcasted_iota(jnp.int32, (count, 128), 1)
     for k in range(total):
         slot, at = k % len(slots), k // len(slots) * high
@@ -338,7 +339,7 @@
             kept = residues - 128 * (len(made) - 1)
             made[-1] = jnp.where(lane < kept, made[-1], 0.0)
             for t, tile in enumerate(made):
-                tiles[t, pl.ds(base + i, count, stride=residues), :] = tile
+                tiles[t, pl.ds(base + i, count, stride=pitch), :] = tile
         return carry
 
     lax.fori_loop(0, total, one, 0)
@@ -348,7 +349,13 @@
     base_ref = refs[0]
     out_ref, stack, tiles = refs[1 + halves :]
     spread_slots(refs[1 : 1 + halves], stack, base_ref, tiles, total_cols, places)
-    out_ref[...] = tiles[...].astype(out_ref.dtype)
+    residues = places * total_cols
+    heads = out_ref.shape[1] // residues
+    pitch = tiles.shape[1] // heads
+    for h in range(heads):
+        out_ref[:, h * residues : (h + 1) * residues, :] = tiles[
+            :, h * pitch : h * pitch + residues, :
+        ].astype(out_ref.dtype)
 
 
 def layout_bias(base, bias_slots, total_cols, places):
@@ -367,7 +374,7 @@
         out_shape=jax.ShapeDtypeStruct(shape, jnp.bfloat16),
         scratch_shapes=[
             pltpu.VMEM((total_rows, rows, wide), jnp.bfloat16),
-            pltpu.VMEM(shape, jnp.float32),
+            pltpu.VMEM((shape[0], heads * (residues + 8), 128), jnp.float32),
         ],
         compiler_params=pltpu.CompilerParams(vmem_limit_bytes=48 << 20),
         name="layout_bias",
@@ -512,14 +519,14 @@
     )(*blocks)
 
 
-def triangle_kernel(total_rows, total_cols, *refs):
+def triangle_kernel(total_rows, total_cols, residues, *refs):
     base_ref = refs[0]
     slots = refs[1 : 1 + total_rows]
     kept = refs[1 + total_rows : 1 + total_rows + total_cols]
     given, stack, tiles, crossed = refs[1 + total_rows + total_cols :]
     pairs = kept[0].shape[2]
     share = kept[0].shape[1]
-    residues = tiles.shape[1] // (2 * share)
+    pitch = tiles.shape[1] // (2 * share)
     rows = residues // total_rows
     places = residues // total_cols
     bf16 = jnp.bfloat16
@@ -527,7 +534,7 @@
     for c in range(share):
         sides = []
         for side in range(2):
-            start = (side * share + c) * residues
+            start = (side * share + c) * pitch
             sides.append(
                 jnp.concatenate(
                     [tiles[t, start : start + residues, :] for t in range(tiles.shape[0])], axis=1
@@ -538,7 +545,7 @@
         )
         for t in range(tiles.shape[0]):
             last = min(128, residues - t * 128)
-            crossed[t, c * residues : (c + 1) * residues, :last] = got[:, t * 128 : t * 128 + last]
+            crossed[t, c * pitch : c * pitch + residues, :last] = got[:, t * 128 : t * 128 + last]
     lane = lax.broadcasted_iota(jnp.int32, (share, 128), 1)
 
     def one(j, carry):
@@ -551,7 +558,7 @@
         made = [dict() for _ in range(total_cols)]
         for i in range(rows):
             row = [
-                crossed[t, pl.ds(base + i, share, stride=residues), :]
+                crossed[t, pl.ds(base + i, share, stride=pitch), :]
                 for t in range(tiles.shape[0])
             ]
             for m in range(total_cols):
@@ -584,7 +591,7 @@
     wide = -(-pairs // 128) * 128 + 128
     bf16 = jnp.bfloat16
     return pl.pallas_call(
-        functools.partial(triangle_kernel, total_rows, total_cols),
+        functools.partial(triangle_kernel, total_rows, total_cols, residues),
         in_specs=[pl.BlockSpec(memory_space=pltpu.SMEM)]
         + [pl.BlockSpec(memory_space=pltpu.VMEM)] * total_rows,
         out_specs=[pl.BlockSpec(memory_space=pltpu.VMEM)] * (total_cols + 1),
@@ -592,8 +599,8 @@
         + [jax.ShapeDtypeStruct((total_cols, total_rows // 2, share, pairs), bf16)],
         scratch_shapes=[
             pltpu.VMEM((total_rows, rows, wide), bf16),
-            pltpu.VMEM((padded, 2 * share * residues, 128), jnp.float32),
-            pltpu.VMEM((padded, share * residues, 128), jnp.float32),
+            pltpu.VMEM((padded, 2 * share * (residues + 8), 128), jnp.float32),
+            pltpu.VMEM((padded, max(share, 8) * (residues + 8), 128), jnp.float32),
         ],
         compiler_params=pltpu.CompilerParams(vmem_limit_bytes=56 << 20),
         name="triangle",

time: 190 us -> 189 us (level)
  Pallas kernels: 53.5 us -> 48.3 us
  waiting for transfers between devices: 72.1 us -> 75.2 us
    ppermute x18, waiting for transfers between devices: 59.5 us -> 62.6 us  [swap(): lax.ppermute(pieces[k], axis, [(i, i ^ k) for i in range(total)])]
    pallas_call x1, Pallas kernels: 10 us -> 7.29 us  [triangle(): pl.pallas_call(functools.partial(triangle_kernel, total_rows, total_cols,...]
    pallas_call x1, Pallas kernels: 5.34 us -> 2.85 us  [layout_bias(): pl.pallas_call(functools.partial(layout_kernel, len(bias_slots), total_co...]
  transfers between devices with their start and end apart: 38 -> 38, of which waited for: 16 -> 16; matrix products, arithmetic and copies ran while one was open for 5% -> 5% of each run, Pallas kernels for 26% -> 23%
where the time goes in v5:
time: 189 us; the launch traced here: 186 us
  waiting for transfers between devices  75.2 us (40%)
  Pallas kernels  48.3 us (26%)
  starting transfers between devices  43.3 us (23%)
  local copies, waits for them, and re-layouts  16.1 us (9%)
  other arithmetic  1.95 us (1%)
    ppermute x18, waiting for transfers between devices, swap(): lax.ppermute(pieces[k], axis, [(i, i ^ k) for i in range(total)])  62.6 us
    ppermute x18, starting transfers between devices, swap(): lax.ppermute(pieces[k], axis, [(i, i ^ k) for i in range(total)])  18.1 us
    pallas_call x1, Pallas kernels, pair_stage(): pl.pallas_call(functools.partial(pair_kernel, total_rows, total_cols), gr...  17 us
    ppermute x15, starting transfers between devices, over_chips(): lax.ppermute(piece, 'row', [(i, i ^ k) for i in range(row_total)])  15.3 us
    pallas_call x1, Pallas kernels, attend(): pl.pallas_call(functools.partial(attention_kernel, total_cols, heads), gr...  11.7 us
    ppermute x15, waiting for transfers between devices, over_chips(): lax.ppermute(piece, 'row', [(i, i ^ k) for i in range(row_total)])  10.8 us
    ppermute x5, starting transfers between devices, other_core(): return lax.ppermute(block, 'row', [(i, i ^ 1) for i in range(row_total)])  9.8 us
    pallas_call x1, Pallas kernels, triangle(): pl.pallas_call(functools.partial(triangle_kernel, total_rows, total_cols,...  7.29 us
  transfers between devices with their start and end apart: 38, of which 16 were waited for; matrix products, arithmetic and copies ran while one was open for 5% of the time, Pallas kernels for 23%

profile of v5, /device:TPU:9, one launch (start us, length us, event | category | flops | bytes accessed | tf_op | source)
XLA Modules:
  0.0 186.3 jit_solution(3294199553917324098)
XLA Ops:
  2.2 1.0 outer_operands.1
  3.3 2.4 %collective-permute-start.1 = (bf16[23,16,128]{2,1,0:T(8,128)(2,1)S(1)}, bf16[23,16,128]{2,1,0:T(8,128)(2,1)S(1)}, u32[]{:S(2)}, u32[]{:S(2)}) collective-permute-start(bf16[23,16,128]{2,1,0:T(8,128)(2,1)S(1)} %get-tuple-element.77), channel_id=1, source_target_pairs={{0,2},{1,3},{2,0},{3,1},{4,6},{5,7},{6,4},{7,5},{8,10},{9,11},{10,... | collective-permute-start | bytes 282632 | tf_op jit(solution)/shard_map/ppermute | solution.py:22
  5.7 1.3 collective-permute-start
  6.9 1.2 collective-permute-start.7
  8.1 1.2 collective-permute-start.8
  12.1 2.2 %collective-permute-start.9 = (bf16[33,16,128]{2,1,0:T(8,128)(2,1)S(1)}, bf16[33,16,128]{2,1,0:T(8,128)(2,1)S(1)}, u32[]{:S(2)}, u32[]{:S(2)}) collective-permute-start(bf16[33,16,128]{2,1,0:T(8,128)(2,1)S(1)} %get-tuple-element.78), channel_id=1, source_target_pairs={{0,24},{4,28},{8,16},{12,20},{16,8},{20,12},{24,0},{28,4},{1,25},{... | collective-permute-start | bytes 405512 | tf_op jit(solution)/shard_map/ppermute | solution.py:717
  14.3 1.1 collective-permute-start.3
  15.5 1.2 collective-permute-start.4
  17.2 3.8 %collective-permute-start.10 = (bf16[132,16,128]{2,1,0:T(8,128)(2,1)S(1)}, bf16[132,16,128]{2,1,0:T(8,128)(2,1)S(1)}, u32[]{:S(2)}, u32[]{:S(2)}) collective-permute-start(bf16[132,16,128]{2,1,0:T(8,128)(2,1)S(1)} %constant_dynamic-update-slice_fusion.refs_3_), channel_id=1, source_target_pairs={{0,4},{4,0},{8,12},{12,8},{16,20},{20,16},{24,28},{28,24},{1,5},{5... | collective-permute-start | bytes 1622024 | tf_op jit(solution)/shard_map/ppermute | solution.py:722
  21.4 1.0 collective-permute-done.5
  22.4 1.6 collective-permute-start.6
  24.8 1.1 copy.43
  28.4 2.7 %collective-permute-start.15 = (bf16[4,88,256]{2,1,0:T(8,128)(2,1)S(1)}, bf16[4,88,256]{2,1,0:T(8,128)(2,1)S(1)}, u32[]{:S(2)}, u32[]{:S(2)}) collective-permute-start(bf16[4,88,256]{2,1,0:T(8,128)(2,1)S(1)} %get-tuple-element.157), channel_id=1, source_target_pairs={{0,2},{1,3},{2,0},{3,1},{4,6},{5,7},{6,4},{7,5},{8,10},{9,11},{10,... | collective-permute-start | bytes 540680 | tf_op jit(solution)/shard_map/ppermute | solution.py:22
  31.8 17.0 %pair_update.1 = (f32[3872,128]{1,0:T(8,128)}, bf16[3872,128]{1,0:T(8,128)(2,1)}, bf16[40,3872]{1,0:T(8,128)(2,1)}, bf16[40,3872]{1,0:T(8,128)(2,1)}, bf16[40,38...) custom-call(s32[4,44]{1,0:T(4,128)} %add_add_fusion.refs_0_, ...), custom_call_target="tpu_custom_call" | custom-call | tf_op jit(solution)/shard_map/pair_update/pallas_call | solution.py:287
  49.7 0.9 collective-permute-start.11
  50.7 2.1 %collective-permute-start.12 = (bf16[40,3872]{1,0:T(8,128)(2,1)}, bf16[40,3872]{1,0:T(8,128)(2,1)S(1)}, u32[]{:S(2)}, u32[]{:S(2)}) collective-permute-start(bf16[40,3872]{1,0:T(8,128)(2,1)} %get-tuple-element.85), channel_id=1, source_target_pairs={{0,2},{1,3},{2,0},{3,1},{4,6},{5,7},{6,4},{7,5},{8,10},{9,11},{10,... | collective-permute-start | bytes 929288 | tf_op jit(solution)/shard_map/ppermute | solution.py:22
  53.1 11.1 %collective-permute-done.11.refs_1_ = bf16[40,3872]{1,0:T(8,128)(2,1)S(1)} collective-permute-done((bf16[40,3872]{1,0:T(8,128)(2,1)}, bf16[40,3872]{1,0:T(8,128)(2,1)S(1)}, u32[]{:S(2)}, u32[]{:S(2)}) %collective-permute-start.11) | collective-permute-done | bytes 309792 | tf_op jit(solution)/shard_map/ppermute | solution.py:22
  64.3 9.2 %collective-permute-done.12.refs_2_ = bf16[40,3872]{1,0:T(8,128)(2,1)S(1)} collective-permute-done((bf16[40,3872]{1,0:T(8,128)(2,1)}, bf16[40,3872]{1,0:T(8,128)(2,1)S(1)}, u32[]{:S(2)}, u32[]{:S(2)}) %collective-permute-start.12) | collective-permute-done | bytes 309792 | tf_op jit(solution)/shard_map/ppermute | solution.py:22
  73.5 7.9 %collective-permute-done.13.refs_3_ = bf16[40,3872]{1,0:T(8,128)(2,1)S(1)} collective-permute-done((bf16[40,3872]{1,0:T(8,128)(2,1)}, bf16[40,3872]{1,0:T(8,128)(2,1)S(1)}, u32[]{:S(2)}, u32[]{:S(2)}) %collective-permute-start.13) | collective-permute-done | bytes 309792 | tf_op jit(solution)/shard_map/ppermute | solution.py:22
  81.5 1.3 collective-permute-start.18
  82.8 1.2 collective-permute-start.19
  84.2 2.2 %collective-permute-start.22 = (bf16[32,3872]{1,0:T(8,128)(2,1)S(1)}, bf16[32,3872]{1,0:T(8,128)(2,1)S(1)}, u32[]{:S(2)}, u32[]{:S(2)}) collective-permute-start(bf16[32,3872]{1,0:T(8,128)(2,1)S(1)} %get-tuple-element.100), channel_id=1, source_target_pairs={{0,2},{1,3},{2,0},{3,1},{4,6},{5,7},{6,4},{7,5},{8,10},{9,11},{10,... | collective-permute-start | bytes 743432 | tf_op jit(solution)/shard_map/ppermute | solution.py:22
  86.4 1.7 collective-permute-done.21.refs_1_
  89.0 12.8 %collective-permute-done.22.refs_2_ = bf16[32,3872]{1,0:T(8,128)(2,1)S(1)} collective-permute-done((bf16[32,3872]{1,0:T(8,128)(2,1)S(1)}, bf16[32,3872]{1,0:T(8,128)(2,1)S(1)}, u32[]{:S(2)}, u32[]{:S(2)}) %collective-permute-start.22) | collective-permute-done | bytes 247840 | tf_op jit(solution)/shard_map/ppermute | solution.py:22
  101.8 6.4 %collective-permute-done.23.refs_3_ = bf16[32,3872]{1,0:T(8,128)(2,1)S(1)} collective-permute-done((bf16[32,3872]{1,0:T(8,128)(2,1)S(1)}, bf16[32,3872]{1,0:T(8,128)(2,1)S(1)}, u32[]{:S(2)}, u32[]{:S(2)}) %collective-permute-start.23) | collective-permute-done | bytes 247840 | tf_op jit(solution)/shard_map/ppermute | solution.py:22
  109.2 1.2 collective-permute-start.24
  110.4 1.2 collective-permute-start.25
  111.9 3.0 %collective-permute-done.24.refs_4_ = bf16[32,3872]{1,0:T(8,128)(2,1)S(1)} collective-permute-done((bf16[32,3872]{1,0:T(8,128)(2,1)S(1)}, bf16[32,3872]{1,0:T(8,128)(2,1)S(1)}, u32[]{:S(2)}, u32[]{:S(2)}) %collective-permute-start.24) | collective-permute-done | bytes 247840 | tf_op jit(solution)/shard_map/ppermute | solution.py:717
  114.8 1.6 collective-permute-done.25.refs_6_
  116.4 4.8 %collective-permute-done.26.refs_8_ = bf16[32,3872]{1,0:T(8,128)(2,1)S(1)} collective-permute-done((bf16[32,3872]{1,0:T(8,128)(2,1)S(1)}, bf16[32,3872]{1,0:T(8,128)(2,1)S(1)}, u32[]{:S(2)}, u32[]{:S(2)}) %collective-permute-start.26) | collective-permute-done | bytes 247840 | tf_op jit(solution)/shard_map/ppermute | solution.py:717
  122.0 1.4 copy.48
  123.4 3.4 %collective-permute-start.27 = (bf16[128,3872]{0,1:T(8,128)(2,1)}, bf16[128,3872]{0,1:T(8,128)(2,1)}, u32[]{:S(2)}, u32[]{:S(2)}) collective-permute-start(bf16[128,3872]{0,1:T(8,128)(2,1)} %copy.48), channel_id=1, source_target_pairs={{0,4},{4,0},{8,12},{12,8},{16,20},{20,16},{24,28},{28,24},{1,5},{5... | collective-permute-start | bytes 2973704 | tf_op jit(solution)/shard_map/ppermute | solution.py:722
  127.4 7.3 %triangle.1 = (bf16[4,4,3872]{2,1,0:T(4,128)(2,1)}, bf16[4,4,3872]{2,1,0:T(4,128)(2,1)}, bf16[4,4,3872]{2,1,0:T(4,128)(2,1)}, bf16[4,4,3872]{2,1,0:T(4,128)(2,1)}, bf16[4,4,4,3872]{3,2,1,0:T(4,128)(2,1)}) custom-call(s32[8]{0:T(128)} %fusion.7.refs_0_, bf16[64,3872]{1,0:T(8,128)(2,1)} %copy-done.1, bf16[32,3872]{1,0:T(8,128)(2,1)} %copy-done.9, ...), custom_call_target="tpu_custom_call" | custom-call | tf_op jit(solution)/shard_map/triangle/pallas_call | solution.py:593
  135.1 1.8 collective-permute-done.31
  137.1 1.0 regroup.8
  138.8 2.4 %collective-permute-start.33 = (bf16[32,3872]{1,0:T(8,128)(2,1)}, bf16[32,3872]{1,0:T(8,128)(2,1)}, u32[]{:S(2)}, u32[]{:S(2)}) collective-permute-start(bf16[32,3872]{1,0:T(8,128)(2,1)} %get-tuple-element.140), channel_id=1, source_target_pairs={{0,2},{1,3},{2,0},{3,1},{4,6},{5,7},{6,4},{7,5},{8,10},{9,11},{10,... | collective-permute-start | bytes 743432 | tf_op jit(solution)/shard_map/ppermute | solution.py:22
  141.4 1.6 copy.49.refs_2_
  143.1 2.9 %layout_bias.1.refs_0_ = bf16[3,2816,128]{2,1,0:T(8,128)(2,1)S(1)} custom-call(s32[8]{0:T(128)S(1)} %copy-done.29, bf16[128,3872]{1,0:T(8,128)(2,1)S(1)} %regroup.7.refs_1_, bf16[128,3872]{1,0:T(8,128)(2,1)S(1)} %copy.49.refs_2_), custom_call_target="tpu_custom_call" | custom-call | tf_op jit(solution)/shard_map/layout_bias/pallas_call | solution.py:369
  146.1 11.7 %row_attention.1 = (bf16[4,88,256]{2,1,0:T(8,128)(2,1)S(1)}, bf16[4,88,256]{2,1,0:T(8,128)(2,1)S(1)}, bf16[4,88,256]{2,1,0:T(8,128)(2,1)}, bf16[4,88,256]{2,1,0:T(8,128)(2,1)}) custom-call(bf16[3,2816,128]{2,1,0:T(8,128)(2,1)S(1)} %layout_bias.1.refs_0_, bf16[4,88,256]{2,1,0:T(8,128)(2,1)S(1)} %copy-done.7, bf16[4,88,256]{2,1,0:T(8,128)(2,1)S(1)} %copy-done.17, ...), custom_call_target="tpu_custom_call" | custom-call | tf_op jit(solution)/shard_map/row_attention/pallas_call | solution.py:461
  157.8 1.0 collective-permute-start.28
  158.8 1.5 collective-permute-start.29
  160.5 3.4 %collective-permute-done.34.refs_3_ = bf16[32,3872]{1,0:T(8,128)(2,1)} collective-permute-done((bf16[32,3872]{1,0:T(8,128)(2,1)}, bf16[32,3872]{1,0:T(8,128)(2,1)}, u32[]{:S(2)}, u32[]{:S(2)}) %collective-permute-start.34) | collective-permute-done | bytes 247840 | tf_op jit(solution)/shard_map/ppermute | solution.py:22
  163.9 2.2 %regroup.9 = (bf16[32,3872]{1,0:T(8,128)(2,1)S(1)}, bf16[32,3872]{1,0:T(8,128)(2,1)}, bf16[32,3872]{1,0:T(8,128)(2,1)}, bf16[32,3872]{1,0:T(8,128)(2,1)}) custom-call(bf16[32,3872]{1,0:T(8,128)(2,1)S(1)} %copy-done.11, bf16[32,3872]{1,0:T(8,128)(2,1)} %collective-permute-done.32.refs_1_, bf16[32,3872]{1,0:T(8,128)(2,1)} %collective-permute-done.33.refs_2_, ...), custom_call_target="tpu_custom_call" | custom-call | tf_op jit(solution)/shard_map/regroup/pallas_call | solution.py:493
  168.3 1.2 collective-permute-start.37
  169.6 5.0 %collective-permute-done.29.refs_2_ = bf16[4,88,256]{2,1,0:T(8,128)(2,1)} collective-permute-done((bf16[4,88,256]{2,1,0:T(8,128)(2,1)}, bf16[4,88,256]{2,1,0:T(8,128)(2,1)}, u32[]{:S(2)}, u32[]{:S(2)}) %collective-permute-start.29) | collective-permute-done | bytes 180256 | tf_op jit(solution)/shard_map/ppermute | solution.py:22
  174.5 4.8 %collective-permute-done.30.refs_3_ = bf16[4,88,256]{2,1,0:T(8,128)(2,1)} collective-permute-done((bf16[4,88,256]{2,1,0:T(8,128)(2,1)}, bf16[4,88,256]{2,1,0:T(8,128)(2,1)}, u32[]{:S(2)}, u32[]{:S(2)}) %collective-permute-start.30) | collective-permute-done | bytes 180256 | tf_op jit(solution)/shard_map/ppermute | solution.py:22
  181.2 1.9 %place_sequences.1 = bf16[16,88,256]{2,1,0:T(8,128)(2,1)} custom-call(s32[4]{0:T(128)S(1)} %broadcast_multiply_fusion.start_ref, bf16[4,88,256]{2,1,0:T(8,128)(2,1)S(1)} %copy-done.13, bf16[4,88,256]{2,1,0:T(8,128)(2,1)S(1)} %copy-done.15, bf16[4,88,256]{2,1,0:T(8,128)(2,1)} %collective-permute-done.29.refs_2_, ...), custom_call_target="tpu_custom_call" | custom-call | tf_op jit(solution)/shard_map/place_sequences/pallas_call | solution.py:659
  183.2 3.1 %pair_finish.1 = bf16[3872,128]{1,0:T(8,128)(2,1)} custom-call(s32[32]{0:T(128)S(1)} %add.136.refs_0_, bf16[32,3872]{1,0:T(8,128)(2,1)S(1)} %get-tuple-element.146.refs_1_, bf16[32,3872]{1,0:T(8,128)(2,1)S(1)} %collective-permute-done.35.refs_2_, bf16[32,3872]{1,0:T(8,128)(2,1)} %collective-permute-done.36.refs_3_, ...), custom_call_target="tpu_custom_call" | custom-call | tf_op jit(solution)/shard_map/pair_finish/pallas_call | solution.py:639
  (187 shorter events, 19.9 us)
Async XLA Ops:
  3.3 8.8 %collective-permute-start.1 = (bf16[23,16,128]{2,1,0:T(8,128)(2,1)S(1)}, bf16[23,16,128]{2,1,0:T(8,128)(2,1)S(1)}, u32[]{:S(2)}, u32[]{:S(2)}) collective-permute-start(bf16[23,16,128]{2,1,0:T(8,128)(2,1)S(1)} %get-tuple-element.77), channel_id=1, source_target_pairs={{0,2},{1,3},{2,0},{3,1},{4,6},{5,7},{6,4},{7,5},{8,10},{9,11},{10,... | collective-permute-start | bytes 282632 | tf_op jit(solution)/shard_map/ppermute | solution.py:22
  5.7 8.6 %collective-permute-start.2 = (bf16[23,16,128]{2,1,0:T(8,128)(2,1)S(1)}, bf16[23,16,128]{2,1,0:T(8,128)(2,1)S(1)}, u32[]{:S(2)}, u32[]{:S(2)}) collective-permute-start(bf16[23,16,128]{2,1,0:T(8,128)(2,1)S(1)} %get-tuple-element.77), channel_id=1, source_target_pairs={{0,3},{1,2},{2,1},{3,0},{4,7},{5,6},{6,5},{7,4},{8,11},{9,10},{10,... | collective-permute-start | bytes 282632 | tf_op jit(solution)/shard_map/ppermute | solution.py:22
  5.7 8.6 %collective-permute-start = (bf16[23,16,128]{2,1,0:T(8,128)(2,1)S(1)}, bf16[23,16,128]{2,1,0:T(8,128)(2,1)S(1)}, u32[]{:S(2)}, u32[]{:S(2)}) collective-permute-start(bf16[23,16,128]{2,1,0:T(8,128)(2,1)S(1)} %get-tuple-element.77), channel_id=1, source_target_pairs={{0,1},{1,0},{2,3},{3,2},{4,5},{5,4},{6,7},{7,6},{8,9},{9,8},{10,11... | collective-permute-start | bytes 282632 | tf_op jit(solution)/shard_map/ppermute | solution.py:22
  6.9 9.8 %collective-permute-start.7 = (bf16[33,16,128]{2,1,0:T(8,128)(2,1)S(1)}, bf16[33,16,128]{2,1,0:T(8,128)(2,1)S(1)}, u32[]{:S(2)}, u32[]{:S(2)}) collective-permute-start(bf16[33,16,128]{2,1,0:T(8,128)(2,1)S(1)} %get-tuple-element.78), channel_id=1, source_target_pairs={{0,8},{4,12},{8,0},{12,4},{16,24},{20,28},{24,16},{28,20},{1,9},{5... | collective-permute-start | bytes 405512 | tf_op jit(solution)/shard_map/ppermute | solution.py:717
  8.1 8.9 %collective-permute-start.8 = (bf16[33,16,128]{2,1,0:T(8,128)(2,1)S(1)}, bf16[33,16,128]{2,1,0:T(8,128)(2,1)S(1)}, u32[]{:S(2)}, u32[]{:S(2)}) collective-permute-start(bf16[33,16,128]{2,1,0:T(8,128)(2,1)S(1)} %get-tuple-element.78), channel_id=1, source_target_pairs={{0,16},{4,20},{8,24},{12,28},{16,0},{20,4},{24,8},{28,12},{1,17},{... | collective-permute-start | bytes 405512 | tf_op jit(solution)/shard_map/ppermute | solution.py:717
  12.1 5.1 %collective-permute-start.9 = (bf16[33,16,128]{2,1,0:T(8,128)(2,1)S(1)}, bf16[33,16,128]{2,1,0:T(8,128)(2,1)S(1)}, u32[]{:S(2)}, u32[]{:S(2)}) collective-permute-start(bf16[33,16,128]{2,1,0:T(8,128)(2,1)S(1)} %get-tuple-element.78), channel_id=1, source_target_pairs={{0,24},{4,28},{8,16},{12,20},{16,8},{20,12},{24,0},{28,4},{1,25},{... | collective-permute-start | bytes 405512 | tf_op jit(solution)/shard_map/ppermute | solution.py:717
  14.3 6.6 %collective-permute-start.3 = (bf16[23,16,128]{2,1,0:T(8,128)(2,1)S(1)}, bf16[23,16,128]{2,1,0:T(8,128)(2,1)S(1)}, u32[]{:S(2)}, u32[]{:S(2)}) collective-permute-start(bf16[23,16,128]{2,1,0:T(8,128)(2,1)S(1)} %get-tuple-element.167), channel_id=1, source_target_pairs={{0,8},{4,12},{8,0},{12,4},{16,24},{20,28},{24,16},{28,20},{1,9},{5... | collective-permute-start | bytes 282632 | tf_op jit(solution)/shard_map/ppermute | solution.py:717
  15.5 5.9 %collective-permute-start.4 = (bf16[23,16,128]{2,1,0:T(8,128)(2,1)S(1)}, bf16[23,16,128]{2,1,0:T(8,128)(2,1)S(1)}, u32[]{:S(2)}, u32[]{:S(2)}) collective-permute-start(bf16[23,16,128]{2,1,0:T(8,128)(2,1)S(1)} %get-tuple-element.166), channel_id=1, source_target_pairs={{0,16},{4,20},{8,24},{12,28},{16,0},{20,4},{24,8},{28,12},{1,17},{... | collective-permute-start | bytes 282632 | tf_op jit(solution)/shard_map/ppermute | solution.py:717
  16.7 5.7 %collective-permute-start.5 = (bf16[23,16,128]{2,1,0:T(8,128)(2,1)S(1)}, bf16[23,16,128]{2,1,0:T(8,128)(2,1)S(1)}, u32[]{:S(2)}, u32[]{:S(2)}) collective-permute-start(bf16[23,16,128]{2,1,0:T(8,128)(2,1)S(1)} %get-tuple-element.165), channel_id=1, source_target_pairs={{0,24},{4,28},{8,16},{12,20},{16,8},{20,12},{24,0},{28,4},{1,25},{... | collective-permute-start | bytes 282632 | tf_op jit(solution)/shard_map/ppermute | solution.py:717
  17.2 10.4 %collective-permute-start.10 = (bf16[132,16,128]{2,1,0:T(8,128)(2,1)S(1)}, bf16[132,16,128]{2,1,0:T(8,128)(2,1)S(1)}, u32[]{:S(2)}, u32[]{:S(2)}) collective-permute-start(bf16[132,16,128]{2,1,0:T(8,128)(2,1)S(1)} %constant_dynamic-update-slice_fusion.refs_3_), channel_id=1, source_target_pairs={{0,4},{4,0},{8,12},{12,8},{16,20},{20,16},{24,28},{28,24},{1,5},{5... | collective-permute-start | bytes 1622024 | tf_op jit(solution)/shard_map/ppermute | solution.py:722
  22.4 5.1 %collective-permute-start.6 = (bf16[92,16,128]{2,1,0:T(8,128)(2,1)S(1)}, bf16[92,16,128]{2,1,0:T(8,128)(2,1)S(1)}, u32[]{:S(2)}, u32[]{:S(2)}) collective-permute-start(bf16[92,16,128]{2,1,0:T(8,128)(2,1)S(1)} %pad_maximum_fusion.2.refs_1_), channel_id=1, source_target_pairs={{0,4},{4,0},{8,12},{12,8},{16,20},{20,16},{24,28},{28,24},{1,5},{5... | collective-permute-start | bytes 1130504 | tf_op jit(solution)/shard_map/ppermute | solution.py:722
  28.4 20.3 %collective-permute-start.14 = (bf16[4,88,256]{2,1,0:T(8,128)(2,1)S(1)}, bf16[4,88,256]{2,1,0:T(8,128)(2,1)S(1)}, u32[]{:S(2)}, u32[]{:S(2)}) collective-permute-start(bf16[4,88,256]{2,1,0:T(8,128)(2,1)S(1)} %get-tuple-element.158), channel_id=1, source_target_pairs={{0,1},{1,0},{2,3},{3,2},{4,5},{5,4},{6,7},{7,6},{8,9},{9,8},{10,11... | collective-permute-start | bytes 540680 | tf_op jit(solution)/shard_map/ppermute | solution.py:22
  28.4 20.3 %collective-permute-start.15 = (bf16[4,88,256]{2,1,0:T(8,128)(2,1)S(1)}, bf16[4,88,256]{2,1,0:T(8,128)(2,1)S(1)}, u32[]{:S(2)}, u32[]{:S(2)}) collective-permute-start(bf16[4,88,256]{2,1,0:T(8,128)(2,1)S(1)} %get-tuple-element.157), channel_id=1, source_target_pairs={{0,2},{1,3},{2,0},{3,1},{4,6},{5,7},{6,4},{7,5},{8,10},{9,11},{10,... | collective-permute-start | bytes 540680 | tf_op jit(solution)/shard_map/ppermute | solution.py:22
  31.1 17.7 %collective-permute-start.16 = (bf16[4,88,256]{2,1,0:T(8,128)(2,1)S(1)}, bf16[4,88,256]{2,1,0:T(8,128)(2,1)S(1)}, u32[]{:S(2)}, u32[]{:S(2)}) collective-permute-start(bf16[4,88,256]{2,1,0:T(8,128)(2,1)S(1)} %get-tuple-element.156), channel_id=1, source_target_pairs={{0,3},{1,2},{2,1},{3,0},{4,7},{5,6},{6,5},{7,4},{8,11},{9,10},{10,... | collective-permute-start | bytes 540680 | tf_op jit(solution)/shard_map/ppermute | solution.py:22
  48.7 32.6 %copy-start.8 = (bf16[40,3872]{1,0:T(8,128)(2,1)S(1)}, bf16[40,3872]{1,0:T(8,128)(2,1)}, u32[]{:S(2)}) copy-start(bf16[40,3872]{1,0:T(8,128)(2,1)} %get-tuple-element.90.refs_0_) | copy-start | bytes 929284
  48.8 59.6 %copy-start.16 = (bf16[4,88,256]{2,1,0:T(8,128)(2,1)}, bf16[4,88,256]{2,1,0:T(8,128)(2,1)S(1)}, u32[]{:S(2)}) copy-start(bf16[4,88,256]{2,1,0:T(8,128)(2,1)S(1)} %collective-permute-done.14.refs_2_) | copy-start | bytes 540676
  48.8 59.6 %copy-start.18 = (bf16[4,88,256]{2,1,0:T(8,128)(2,1)}, bf16[4,88,256]{2,1,0:T(8,128)(2,1)S(1)}, u32[]{:S(2)}) copy-start(bf16[4,88,256]{2,1,0:T(8,128)(2,1)S(1)} %collective-permute-done.15.refs_3_) | copy-start | bytes 540676
  48.8 59.6 %copy-start.20 = (bf16[4,88,256]{2,1,0:T(8,128)(2,1)}, bf16[4,88,256]{2,1,0:T(8,128)(2,1)S(1)}, u32[]{:S(2)}) copy-start(bf16[4,88,256]{2,1,0:T(8,128)(2,1)S(1)} %collective-permute-done.16.refs_4_) | copy-start | bytes 540676
  48.8 4.2 %collective-permute-start.17 = (bf16[4,32,3872]{2,1,0:T(8,128)(2,1)}, bf16[4,32,3872]{2,1,0:T(8,128)(2,1)S(1)}, u32[]{:S(2)}, u32[]{:S(2)}) collective-permute-start(bf16[4,32,3872]{2,1,0:T(8,128)(2,1)} %get-tuple-element.89), channel_id=1, source_target_pairs={{0,4},{4,0},{8,12},{12,8},{16,20},{20,16},{24,28},{28,24},{1,5},{5... | collective-permute-start | bytes 2973704 | tf_op jit(solution)/shard_map/ppermute | solution.py:722
  49.7 14.6 %collective-permute-start.11 = (bf16[40,3872]{1,0:T(8,128)(2,1)}, bf16[40,3872]{1,0:T(8,128)(2,1)S(1)}, u32[]{:S(2)}, u32[]{:S(2)}) collective-permute-start(bf16[40,3872]{1,0:T(8,128)(2,1)} %get-tuple-element.84), channel_id=1, source_target_pairs={{0,1},{1,0},{2,3},{3,2},{4,5},{5,4},{6,7},{7,6},{8,9},{9,8},{10,11... | collective-permute-start | bytes 929288 | tf_op jit(solution)/shard_map/ppermute | solution.py:22
  50.7 22.8 %collective-permute-start.12 = (bf16[40,3872]{1,0:T(8,128)(2,1)}, bf16[40,3872]{1,0:T(8,128)(2,1)S(1)}, u32[]{:S(2)}, u32[]{:S(2)}) collective-permute-start(bf16[40,3872]{1,0:T(8,128)(2,1)} %get-tuple-element.85), channel_id=1, source_target_pairs={{0,2},{1,3},{2,0},{3,1},{4,6},{5,7},{6,4},{7,5},{8,10},{9,11},{10,... | collective-permute-start | bytes 929288 | tf_op jit(solution)/shard_map/ppermute | solution.py:22
  52.8 28.6 %collective-permute-start.13 = (bf16[40,3872]{1,0:T(8,128)(2,1)}, bf16[40,3872]{1,0:T(8,128)(2,1)S(1)}, u32[]{:S(2)}, u32[]{:S(2)}) collective-permute-start(bf16[40,3872]{1,0:T(8,128)(2,1)} %get-tuple-element.86), channel_id=1, source_target_pairs={{0,3},{1,2},{2,1},{3,0},{4,7},{5,6},{6,5},{7,4},{8,11},{9,10},{10,... | collective-permute-start | bytes 929288 | tf_op jit(solution)/shard_map/ppermute | solution.py:22
  81.3 6.8 %collective-permute-start.21 = (bf16[32,3872]{1,0:T(8,128)(2,1)S(1)}, bf16[32,3872]{1,0:T(8,128)(2,1)S(1)}, u32[]{:S(2)}, u32[]{:S(2)}) collective-permute-start(bf16[32,3872]{1,0:T(8,128)(2,1)S(1)} %get-tuple-element.99), channel_id=1, source_target_pairs={{0,1},{1,0},{2,3},{3,2},{4,5},{5,4},{6,7},{7,6},{8,9},{9,8},{10,11... | collective-permute-start | bytes 743432 | tf_op jit(solution)/shard_map/ppermute | solution.py:22
  81.5 41.9 %copy-start.1 = (bf16[64,3872]{1,0:T(8,128)(2,1)}, bf16[64,3872]{1,0:T(8,128)(2,1)S(1)}, u32[]{:S(2)}) copy-start(bf16[64,3872]{1,0:T(8,128)(2,1)S(1)} %get-tuple-element.114.refs_0_.refs_1_) | copy-start | bytes 1486852
  81.5 26.8 %collective-permute-start.18 = (bf16[64,3872]{1,0:T(8,128)(2,1)S(1)}, bf16[64,3872]{1,0:T(8,128)(2,1)S(1)}, u32[]{:S(2)}, u32[]{:S(2)}) collective-permute-start(bf16[64,3872]{1,0:T(8,128)(2,1)S(1)} %get-tuple-element.95), channel_id=1, source_target_pairs={{0,8},{4,12},{8,0},{12,4},{16,24},{20,28},{24,16},{28,20},{1,9},{5... | collective-permute-start | bytes 1486856 | tf_op jit(solution)/shard_map/ppermute | solution.py:717
  82.8 25.5 %collective-permute-start.19 = (bf16[64,3872]{1,0:T(8,128)(2,1)S(1)}, bf16[64,3872]{1,0:T(8,128)(2,1)S(1)}, u32[]{:S(2)}, u32[]{:S(2)}) collective-permute-start(bf16[64,3872]{1,0:T(8,128)(2,1)S(1)} %get-tuple-element.96), channel_id=1, source_target_pairs={{0,16},{4,20},{8,24},{12,28},{16,0},{20,4},{24,8},{28,12},{1,17},{... | collective-permute-start | bytes 1486856 | tf_op jit(solution)/shard_map/ppermute | solution.py:717
  84.0 24.3 %collective-permute-start.20 = (bf16[64,3872]{1,0:T(8,128)(2,1)S(1)}, bf16[64,3872]{1,0:T(8,128)(2,1)S(1)}, u32[]{:S(2)}, u32[]{:S(2)}) collective-permute-start(bf16[64,3872]{1,0:T(8,128)(2,1)S(1)} %get-tuple-element.97), channel_id=1, source_target_pairs={{0,24},{4,28},{8,16},{12,20},{16,8},{20,12},{24,0},{28,4},{1,25},{... | collective-permute-start | bytes 1486856 | tf_op jit(solution)/shard_map/ppermute | solution.py:717
  84.2 17.6 %collective-permute-start.22 = (bf16[32,3872]{1,0:T(8,128)(2,1)S(1)}, bf16[32,3872]{1,0:T(8,128)(2,1)S(1)}, u32[]{:S(2)}, u32[]{:S(2)}) collective-permute-start(bf16[32,3872]{1,0:T(8,128)(2,1)S(1)} %get-tuple-element.100), channel_id=1, source_target_pairs={{0,2},{1,3},{2,0},{3,1},{4,6},{5,7},{6,4},{7,5},{8,10},{9,11},{10,... | collective-permute-start | bytes 743432 | tf_op jit(solution)/shard_map/ppermute | solution.py:22
  88.1 20.1 %collective-permute-start.23 = (bf16[32,3872]{1,0:T(8,128)(2,1)S(1)}, bf16[32,3872]{1,0:T(8,128)(2,1)S(1)}, u32[]{:S(2)}, u32[]{:S(2)}) collective-permute-start(bf16[32,3872]{1,0:T(8,128)(2,1)S(1)} %get-tuple-element.101), channel_id=1, source_target_pairs={{0,3},{1,2},{2,1},{3,0},{4,7},{5,6},{6,5},{7,4},{8,11},{9,10},{10,... | collective-permute-start | bytes 743432 | tf_op jit(solution)/shard_map/ppermute | solution.py:22
  109.2 5.6 %collective-permute-start.24 = (bf16[32,3872]{1,0:T(8,128)(2,1)S(1)}, bf16[32,3872]{1,0:T(8,128)(2,1)S(1)}, u32[]{:S(2)}, u32[]{:S(2)}) collective-permute-start(bf16[32,3872]{1,0:T(8,128)(2,1)S(1)} %get-tuple-element.111), channel_id=1, source_target_pairs={{0,8},{4,12},{8,0},{12,4},{16,24},{20,28},{24,16},{28,20},{1,9},{5... | collective-permute-start | bytes 743432 | tf_op jit(solution)/shard_map/ppermute | solution.py:717
  110.4 6.0 %collective-permute-start.25 = (bf16[32,3872]{1,0:T(8,128)(2,1)S(1)}, bf16[32,3872]{1,0:T(8,128)(2,1)S(1)}, u32[]{:S(2)}, u32[]{:S(2)}) collective-permute-start(bf16[32,3872]{1,0:T(8,128)(2,1)S(1)} %get-tuple-element.112), channel_id=1, source_target_pairs={{0,16},{4,20},{8,24},{12,28},{16,0},{20,4},{24,8},{28,12},{1,17},{... | collective-permute-start | bytes 743432 | tf_op jit(solution)/shard_map/ppermute | solution.py:717
  111.7 9.5 %collective-permute-start.26 = (bf16[32,3872]{1,0:T(8,128)(2,1)S(1)}, bf16[32,3872]{1,0:T(8,128)(2,1)S(1)}, u32[]{:S(2)}, u32[]{:S(2)}) collective-permute-start(bf16[32,3872]{1,0:T(8,128)(2,1)S(1)} %get-tuple-element.113), channel_id=1, source_target_pairs={{0,24},{4,28},{8,16},{12,20},{16,8},{20,12},{24,0},{28,4},{1,25},{... | collective-permute-start | bytes 743432 | tf_op jit(solution)/shard_map/ppermute | solution.py:717
  123.4 11.3 %collective-permute-start.27 = (bf16[128,3872]{0,1:T(8,128)(2,1)}, bf16[128,3872]{0,1:T(8,128)(2,1)}, u32[]{:S(2)}, u32[]{:S(2)}) collective-permute-start(bf16[128,3872]{0,1:T(8,128)(2,1)} %copy.48), channel_id=1, source_target_pairs={{0,4},{4,0},{8,12},{12,8},{16,20},{20,16},{24,28},{28,24},{1,5},{5... | collective-permute-start | bytes 2973704 | tf_op jit(solution)/shard_map/ppermute | solution.py:722
  134.7 2.2 %collective-permute-start.31 = (bf16[4,4,4,3872]{3,2,1,0:T(4,128)(2,1)}, bf16[4,4,4,3872]{3,2,1,0:T(4,128)(2,1)S(1)}, u32[]{:S(2)}, u32[]{:S(2)}) collective-permute-start(bf16[4,4,4,3872]{3,2,1,0:T(4,128)(2,1)} %get-tuple-element.137), channel_id=1, source_target_pairs={{0,4},{4,0},{8,12},{12,8},{16,20},{20,16},{24,28},{28,24},{1,5},{5... | collective-permute-start | bytes 1486856 | tf_op jit(solution)/shard_map/ppermute | solution.py:722
  138.8 21.5 %collective-permute-start.32 = (bf16[32,3872]{1,0:T(8,128)(2,1)}, bf16[32,3872]{1,0:T(8,128)(2,1)}, u32[]{:S(2)}, u32[]{:S(2)}) collective-permute-start(bf16[32,3872]{1,0:T(8,128)(2,1)} %get-tuple-element.139), channel_id=1, source_target_pairs={{0,1},{1,0},{2,3},{3,2},{4,5},{5,4},{6,7},{7,6},{8,9},{9,8},{10,11... | collective-permute-start | bytes 743432 | tf_op jit(solution)/shard_map/ppermute | solution.py:22
  138.8 21.8 %collective-permute-start.33 = (bf16[32,3872]{1,0:T(8,128)(2,1)}, bf16[32,3872]{1,0:T(8,128)(2,1)}, u32[]{:S(2)}, u32[]{:S(2)}) collective-permute-start(bf16[32,3872]{1,0:T(8,128)(2,1)} %get-tuple-element.140), channel_id=1, source_target_pairs={{0,2},{1,3},{2,0},{3,1},{4,6},{5,7},{6,4},{7,5},{8,10},{9,11},{10,... | collective-permute-start | bytes 743432 | tf_op jit(solution)/shard_map/ppermute | solution.py:22
  141.2 22.7 %collective-permute-start.34 = (bf16[32,3872]{1,0:T(8,128)(2,1)}, bf16[32,3872]{1,0:T(8,128)(2,1)}, u32[]{:S(2)}, u32[]{:S(2)}) collective-permute-start(bf16[32,3872]{1,0:T(8,128)(2,1)} %get-tuple-element.141), channel_id=1, source_target_pairs={{0,3},{1,2},{2,1},{3,0},{4,7},{5,6},{6,5},{7,4},{8,11},{9,10},{10,... | collective-permute-start | bytes 743432 | tf_op jit(solution)/shard_map/ppermute | solution.py:22
  146.0 17.9 %copy-start.11 = (bf16[32,3872]{1,0:T(8,128)(2,1)S(1)}, bf16[32,3872]{1,0:T(8,128)(2,1)}, u32[]{:S(2)}) copy-start(bf16[32,3872]{1,0:T(8,128)(2,1)} %copy-done.10) | copy-start | bytes 743428
  146.0 37.1 %copy-start.5 = (f32[3872,128]{1,0:T(8,128)S(1)}, f32[3872,128]{1,0:T(8,128)}, u32[]{:S(2)}) copy-start(f32[3872,128]{1,0:T(8,128)} %get-tuple-element.151.refs_6_) | copy-start | bytes 5947396
  146.1 37.1 %copy-start.6 = (bf16[3872,128]{1,0:T(8,128)(2,1)S(1)}, bf16[3872,128]{1,0:T(8,128)(2,1)}, u32[]{:S(2)}) copy-start(bf16[3872,128]{1,0:T(8,128)(2,1)} %get-tuple-element.150.refs_5_) | copy-start | bytes 2973700
  157.8 25.4 %copy-start.27 = (bf16[128,128]{1,0:T(8,128)(2,1)S(1)}, bf16[128,128]{1,0:T(8,128)(2,1)}, u32[]{:S(2)}) copy-start(bf16[128,128]{1,0:T(8,128)(2,1)} %refs_7_.3) | copy-start | bytes 98308
  157.8 25.4 %copy-start.28 = (bf16[128,128]{1,0:T(8,128)(2,1)S(1)}, bf16[128,128]{1,0:T(8,128)(2,1)}, u32[]{:S(2)}) copy-start(bf16[128,128]{1,0:T(8,128)(2,1)} %param.33) | copy-start | bytes 98308
  157.8 9.8 %collective-permute-start.28 = (bf16[4,88,256]{2,1,0:T(8,128)(2,1)S(1)}, bf16[4,88,256]{2,1,0:T(8,128)(2,1)S(1)}, u32[]{:S(2)}, u32[]{:S(2)}) collective-permute-start(bf16[4,88,256]{2,1,0:T(8,128)(2,1)S(1)} %get-tuple-element.130), channel_id=1, source_target_pairs={{0,1},{1,0},{2,3},{3,2},{4,5},{5,4},{6,7},{7,6},{8,9},{9,8},{10,11... | collective-permute-start | bytes 540680 | tf_op jit(solution)/shard_map/ppermute | solution.py:22
  158.8 15.7 %collective-permute-start.29 = (bf16[4,88,256]{2,1,0:T(8,128)(2,1)}, bf16[4,88,256]{2,1,0:T(8,128)(2,1)}, u32[]{:S(2)}, u32[]{:S(2)}) collective-permute-start(bf16[4,88,256]{2,1,0:T(8,128)(2,1)} %get-tuple-element.131), channel_id=1, source_target_pairs={{0,2},{1,3},{2,0},{3,1},{4,6},{5,7},{6,4},{7,5},{8,10},{9,11},{10,... | collective-permute-start | bytes 540680 | tf_op jit(solution)/shard_map/ppermute | solution.py:22
  160.3 19.1 %collective-permute-start.30 = (bf16[4,88,256]{2,1,0:T(8,128)(2,1)}, bf16[4,88,256]{2,1,0:T(8,128)(2,1)}, u32[]{:S(2)}, u32[]{:S(2)}) collective-permute-start(bf16[4,88,256]{2,1,0:T(8,128)(2,1)} %get-tuple-element.132), channel_id=1, source_target_pairs={{0,3},{1,2},{2,1},{3,0},{4,7},{5,6},{6,5},{7,4},{8,11},{9,10},{10,... | collective-permute-start | bytes 540680 | tf_op jit(solution)/shard_map/ppermute | solution.py:22
  166.1 17.0 %collective-permute-start.35 = (bf16[32,3872]{1,0:T(8,128)(2,1)}, bf16[32,3872]{1,0:T(8,128)(2,1)S(1)}, u32[]{:S(2)}, u32[]{:S(2)}) collective-permute-start(bf16[32,3872]{1,0:T(8,128)(2,1)} %get-tuple-element.147), channel_id=1, source_target_pairs={{0,8},{4,12},{8,0},{12,4},{16,24},{20,28},{24,16},{28,20},{1,9},{5... | collective-permute-start | bytes 743432 | tf_op jit(solution)/shard_map/ppermute | solution.py:717
  167.0 16.2 %collective-permute-start.36 = (bf16[32,3872]{1,0:T(8,128)(2,1)}, bf16[32,3872]{1,0:T(8,128)(2,1)}, u32[]{:S(2)}, u32[]{:S(2)}) collective-permute-start(bf16[32,3872]{1,0:T(8,128)(2,1)} %get-tuple-element.148), channel_id=1, source_target_pairs={{0,16},{4,20},{8,24},{12,28},{16,0},{20,4},{24,8},{28,12},{1,17},{... | collective-permute-start | bytes 743432 | tf_op jit(solution)/shard_map/ppermute | solution.py:717
  168.3 14.9 %collective-permute-start.37 = (bf16[32,3872]{1,0:T(8,128)(2,1)}, bf16[32,3872]{1,0:T(8,128)(2,1)}, u32[]{:S(2)}, u32[]{:S(2)}) collective-permute-start(bf16[32,3872]{1,0:T(8,128)(2,1)} %get-tuple-element.149), channel_id=1, source_target_pairs={{0,24},{4,28},{8,16},{12,20},{16,8},{20,12},{24,0},{28,4},{1,25},{... | collective-permute-start | bytes 743432 | tf_op jit(solution)/shard_map/ppermute | solution.py:717
  (36 other events, 215.8 us)
